TPU v7x, 32 devices: a whole 2x2x4 slice. The times are simulated.
32 devices in a mesh: dp: 16 (over z, y, core), seq: 2 (over x).
Axes of the slice: x: 2, y: 2, z: 4, core: 2. Of those that a mesh axis runs over, the one named last changes fastest.
Arguments:
- tokens: bfloat16 [32768, 1024], P(('dp', 'seq')), may hold values from -6 to 6
- ln1_gain: float32 [1024], replicated, may hold values from 0.5 to 1.5
- ln1_bias: float32 [1024], replicated, may hold values from -1.5 to 1.5
- qkv_weight: bfloat16 [1024, 3072], P(('dp', 'seq')), may hold values from -0.1875 to 0.1875
- qkv_bias: float32 [2048], replicated, may hold values from -1.5 to 1.5
- dense_weight: bfloat16 [1024, 1024], P(('dp', 'seq')), may hold values from -0.5 to 0.5
- dense_bias: float32 [1024], replicated, may hold values from -1.5 to 1.5
- ln2_gain: float32 [1024], replicated, may hold values from 0.5 to 1.5
- ln2_bias: float32 [1024], replicated, may hold values from -1.5 to 1.5
- up_weight: bfloat16 [1024, 4096], P(('dp', 'seq')), may hold values from -0.1875 to 0.1875
- up_bias: float32 [4096], replicated, may hold values from -1.5 to 1.5
- down_weight: bfloat16 [4096, 1024], P(('dp', 'seq')), may hold values from -0.09375 to 0.09375
- down_bias: float32 [1024], replicated, may hold values from -1.5 to 1.5
- cotangent: bfloat16 [32768, 1024], P(('dp', 'seq')), may hold values from -6 to 6
- seq_lengths: int32 [32], replicated, may hold values from 256 to 1024, as said below
- slot_order: int32 [32], replicated, may hold values from 0 to 31, as said below
Outputs:
- block_output: bfloat16 [32768, 1024], P(('dp', 'seq'))
- token_grad: bfloat16 [32768, 1024], P(('dp', 'seq'))
- ln1_gain_grad: float32 [1024], replicated
- ln1_bias_grad: float32 [1024], replicated
- qkv_weight_grad: float32 [1024, 3072], P(('dp', 'seq'))
- qkv_bias_grad: float32 [2048], replicated
- dense_weight_grad: float32 [1024, 1024], P(('dp', 'seq'))
- dense_bias_grad: float32 [1024], replicated
- ln2_gain_grad: float32 [1024], replicated
- ln2_bias_grad: float32 [1024], replicated
- up_weight_grad: float32 [1024, 4096], P(('dp', 'seq'))
- up_bias_grad: float32 [4096], replicated
- down_weight_grad: float32 [4096, 1024], P(('dp', 'seq'))
- down_bias_grad: float32 [1024], replicated
Inputs may be any that keep to these rules, and one draw needn't show every extreme that they name: `seq_lengths`: in every block of 2 consecutive slots, the sequence of at least one slot has more than 512 valid tokens; some sequence has 1024. `slot_order`: every sequence number appears once.
All inputs are finite; a program needn't handle non-finite values.
Results may differ from a plain program's by a relative error of at most 0.012.
Values may be sent and summed in bfloat16 or wider, within the bound.
No kernel may reach another device: no remote copies, remote signals or barrier semaphores. Data moves between devices by JAX's collectives and lax.ppermute only.
A program may use at most 256 MiB of HBM per device.

v0:
```python
import jax
import jax.numpy as jnp
from jax import lax
from jax.sharding import PartitionSpec as P

H = 16
SEQLEN = 1024
SG = 2


def layer_norm(values, gain, shift):
    center = values - jnp.mean(values, axis=-1, keepdims=True)
    spread = jnp.mean(center * center, axis=-1, keepdims=True)
    return center * lax.rsqrt(spread + 1e-05) * gain + shift


def gelu_tanh(values):
    return jax.nn.gelu(values, approximate=True)


def shards(
    tokens,
    ln1_gain,
    ln1_bias,
    qkv_weight,
    qkv_bias,
    dense_weight,
    dense_bias,
    ln2_gain,
    ln2_bias,
    up_weight,
    up_bias,
    down_weight,
    down_bias,
    cotangent,
    seq_lengths,
    slot_order,
):
    rows = tokens.shape[0]
    width = tokens.shape[1]
    group = rows * lax.axis_size("seq")
    f32 = jnp.float32
    bf16 = jnp.bfloat16
    window = SEQLEN
    w_qkv, w_dense, w_up, w_down = (
        lax.all_gather(qkv_weight, ("dp", "seq"), axis=0, tiled=True),
        lax.all_gather(dense_weight, ("dp", "seq"), axis=0, tiled=True),
        lax.all_gather(up_weight, ("dp", "seq"), axis=0, tiled=True),
        lax.all_gather(down_weight, ("dp", "seq"), axis=0, tiled=True),
    )
    order_group = lax.dynamic_slice_in_dim(slot_order, lax.axis_index("dp") * SG, SG)
    every_seq = jnp.arange(seq_lengths.shape[0], dtype=jnp.int32)
    lengths_group = jnp.sum(
        jnp.where(every_seq[None, :] == order_group[:, None], seq_lengths[None, :], 0), axis=1
    )
    slot_numbers = jnp.arange(SG, dtype=jnp.int32)

    def length_of(slots):
        return jnp.sum(
            jnp.where(slots[:, None] == slot_numbers[None, :], lengths_group[None, :], 0), axis=1
        )

    first_row = lax.axis_index("seq") * rows
    window_start = jnp.minimum(first_row // SEQLEN * SEQLEN, group - window)
    key_index = window_start + jnp.arange(window, dtype=jnp.int32)
    key_slot = key_index // SEQLEN
    key_place = key_index % SEQLEN
    key_live = key_place < length_of(key_slot)
    query_index = first_row + jnp.arange(rows, dtype=jnp.int32)
    query_slot = query_index // SEQLEN
    query_place = query_index % SEQLEN
    valid = (query_place < length_of(query_slot)).astype(f32)
    allowed = (
        (query_slot[:, None] == key_slot[None, :])
        & (key_place[None, :] <= query_place[:, None])
        & key_live[None, :]
    )
    offset = (key_place[None, :] - query_place[:, None]).astype(f32)
    slopes = jnp.exp2(-8.0 * (jnp.arange(H, dtype=f32) + 1.0) / H)
    inputs = tokens.astype(f32)
    normed_one, norm_one_back = jax.vjp(layer_norm, inputs, ln1_gain, ln1_bias)
    normed_low = normed_one.astype(bf16)
    bias_full = jnp.concatenate([qkv_bias[:width], jnp.zeros((width,), f32), qkv_bias[width:]])
    joined = (jnp.dot(normed_low, w_qkv, preferred_element_type=f32) + bias_full).astype(bf16)
    query = joined[:, :width]
    keys_group, values_group = (
        lax.all_gather(joined[:, width : 2 * width], "seq", axis=0, tiled=True),
        lax.all_gather(joined[:, 2 * width :], "seq", axis=0, tiled=True),
    )
    keys_all = lax.dynamic_slice_in_dim(keys_group, window_start, window, 0)
    values_all = lax.dynamic_slice_in_dim(values_group, window_start, window, 0)

    def split_heads(matrix):
        return matrix.reshape(matrix.shape[0], H, width // H).transpose(1, 0, 2)

    def merge_heads(stack):
        return stack.transpose(1, 0, 2).reshape(stack.shape[1], width)

    head_queries = split_heads(query)
    head_keys = split_heads(keys_all)
    head_values = split_heads(values_all)

    def scores_of(head_query, head_key, head_slope):
        scores = jnp.einsum("qd,kd->qk", head_query, head_key, preferred_element_type=f32) * 0.125
        return jnp.where(allowed, scores + head_slope * offset, -1e30)

    def head_forward(packed):
        head_query, head_key, head_value, head_slope = packed
        scores = scores_of(head_query, head_key, head_slope)
        top = jnp.max(scores, axis=-1, keepdims=True)
        expo = jnp.exp(scores - top)
        totals = jnp.sum(expo, axis=-1, keepdims=True)
        probs = (expo / totals).astype(bf16)
        result = jnp.einsum("qk,kd->qd", probs, head_value, preferred_element_type=f32)
        return (result, top[:, 0] + jnp.log(totals[:, 0]))

    head_context, head_lse = lax.map(head_forward, (head_queries, head_keys, head_values, slopes))
    context = merge_heads(head_context).astype(bf16)
    hidden = inputs + jnp.dot(context, w_dense, preferred_element_type=f32) + dense_bias
    normed_two, norm_two_back = jax.vjp(layer_norm, hidden, ln2_gain, ln2_bias)
    normed_two_low = normed_two.astype(bf16)
    before = jnp.dot(normed_two_low, w_up, preferred_element_type=f32) + up_bias
    active, gelu_back = jax.vjp(gelu_tanh, before)
    active_low = active.astype(bf16)
    outputs = hidden + jnp.dot(active_low, w_down, preferred_element_type=f32) + down_bias
    block_output = outputs.astype(bf16)
    back_qkv, back_dense, back_up, back_down = (
        lax.all_gather(qkv_weight, ("dp", "seq"), axis=0, tiled=True),
        lax.all_gather(dense_weight, ("dp", "seq"), axis=0, tiled=True),
        lax.all_gather(up_weight, ("dp", "seq"), axis=0, tiled=True),
        lax.all_gather(down_weight, ("dp", "seq"), axis=0, tiled=True),
    )
    grad_out = cotangent.astype(f32) * valid[:, None]
    grad_out_low = grad_out.astype(bf16)
    grad_down_w = jnp.einsum("rf,rd->fd", active_low, grad_out_low, preferred_element_type=f32)
    grad_down_b = jnp.sum(grad_out_low.astype(f32), axis=0)
    grad_active = jnp.einsum("rd,fd->rf", grad_out_low, back_down, preferred_element_type=f32)
    (grad_before,) = gelu_back(grad_active)
    grad_before_low = grad_before.astype(bf16)
    grad_up_w = jnp.einsum("rd,rf->df", normed_two_low, grad_before_low, preferred_element_type=f32)
    grad_up_b = jnp.sum(grad_before_low.astype(f32), axis=0)
    grad_normed_two = jnp.einsum("rf,df->rd", grad_before_low, back_up, preferred_element_type=f32)
    grad_hidden_norm, grad_gain_two, grad_shift_two = norm_two_back(grad_normed_two)
    grad_hidden = grad_out + grad_hidden_norm
    grad_hidden_low = grad_hidden.astype(bf16)
    grad_dense_w = jnp.einsum("rd,re->de", context, grad_hidden_low, preferred_element_type=f32)
    grad_dense_b = jnp.sum(grad_hidden_low.astype(f32), axis=0)
    grad_context = jnp.einsum(
        "re,de->rd", grad_hidden_low, back_dense, preferred_element_type=f32
    ).astype(bf16)

    def head_backward(packed):
        head_query, head_key, head_value, head_slope, head_grad, head_norm = packed
        scores = scores_of(head_query, head_key, head_slope)
        probs = jnp.exp(scores - head_norm[:, None])
        prob_grad = jnp.einsum("qd,kd->qk", head_grad, head_value, preferred_element_type=f32)
        value_grad = jnp.einsum(
            "qk,qd->kd", probs.astype(bf16), head_grad, preferred_element_type=f32
        )
        row_dot = jnp.sum(probs * prob_grad, axis=-1, keepdims=True)
        score_grad = (probs * (prob_grad - row_dot)).astype(bf16)
        query_grad = (
            jnp.einsum("qk,kd->qd", score_grad, head_key, preferred_element_type=f32) * 0.125
        )
        key_grad = (
            jnp.einsum("qk,qd->kd", score_grad, head_query, preferred_element_type=f32) * 0.125
        )
        return (query_grad, key_grad, value_grad)

    grad_queries, grad_keys, grad_values = lax.map(
        head_backward,
        (head_queries, head_keys, head_values, slopes, split_heads(grad_context), head_lse),
    )
    empty_group = jnp.zeros((group, width), f32)
    key_terms = lax.dynamic_update_slice_in_dim(
        empty_group, merge_heads(grad_keys), window_start, 0
    )
    value_terms = lax.dynamic_update_slice_in_dim(
        empty_group, merge_heads(grad_values), window_start, 0
    )
    grad_key, grad_value = (
        lax.psum_scatter(
            key_terms.astype(jnp.bfloat16), "seq", scatter_dimension=0, tiled=True
        ).astype(jnp.float32),
        lax.psum_scatter(
            value_terms.astype(jnp.bfloat16), "seq", scatter_dimension=0, tiled=True
        ).astype(jnp.float32),
    )
    grad_query = merge_heads(grad_queries)
    grad_joined = jnp.concatenate([grad_query, grad_key, grad_value], axis=1).astype(bf16)
    grad_qkv_w = jnp.einsum("rd,rc->dc", normed_low, grad_joined, preferred_element_type=f32)
    joined_sums = jnp.sum(grad_joined.astype(f32), axis=0)
    grad_qkv_b = jnp.concatenate([joined_sums[:width], joined_sums[2 * width :]])
    grad_normed_one = jnp.einsum("rc,dc->rd", grad_joined, back_qkv, preferred_element_type=f32)
    grad_input_norm, grad_gain_one, grad_shift_one = norm_one_back(grad_normed_one)
    token_grad = (grad_hidden + grad_input_norm).astype(bf16)
    owner_qkv, owner_dense, owner_up, owner_down = (
        lax.psum_scatter(grad_qkv_w, ("dp", "seq"), scatter_dimension=0, tiled=True),
        lax.psum_scatter(grad_dense_w, ("dp", "seq"), scatter_dimension=0, tiled=True),
        lax.psum_scatter(grad_up_w, ("dp", "seq"), scatter_dimension=0, tiled=True),
        lax.psum_scatter(grad_down_w, ("dp", "seq"), scatter_dimension=0, tiled=True),
    )
    (
        total_gain_one,
        total_shift_one,
        total_qkv_b,
        total_dense_b,
        total_gain_two,
        total_shift_two,
        total_up_b,
        total_down_b,
    ) = lax.psum(
        (
            grad_gain_one,
            grad_shift_one,
            grad_qkv_b,
            grad_dense_b,
            grad_gain_two,
            grad_shift_two,
            grad_up_b,
            grad_down_b,
        ),
        ("dp", "seq"),
    )
    return (
        block_output,
        token_grad,
        total_gain_one,
        total_shift_one,
        owner_qkv,
        total_qkv_b,
        owner_dense,
        total_dense_b,
        total_gain_two,
        total_shift_two,
        owner_up,
        total_up_b,
        owner_down,
        total_down_b,
    )


def solution(mesh):
    in_specs = (
        P(("dp", "seq"), None),
        P(),
        P(),
        P(("dp", "seq"), None),
        P(),
        P(("dp", "seq"), None),
        P(),
        P(),
        P(),
        P(("dp", "seq"), None),
        P(),
        P(("dp", "seq"), None),
        P(),
        P(("dp", "seq"), None),
        P(),
        P(),
    )
    out_specs = (
        P(("dp", "seq"), None),
        P(("dp", "seq"), None),
        P(),
        P(),
        P(("dp", "seq"), None),
        P(),
        P(("dp", "seq"), None),
        P(),
        P(),
        P(),
        P(("dp", "seq"), None),
        P(),
        P(("dp", "seq"), None),
        P(),
    )
    return jax.shard_map(shards, mesh=mesh, in_specs=in_specs, out_specs=out_specs, check_vma=False)
```

profile of v0, /device:TPU:0, one launch (start us, length us, event | category | flops | bytes accessed | tf_op | source)
XLA Modules:
  0.0 1887.0 jit_solution(14205844134495295240)
XLA Ops:
  12.5 70.6 %all-gather.7.cloned.1.call-done = bf16[1024,3072]{1,0:T(8,128)(2,1)} async-done(((bf16[32,3072]{1,0:T(8,128)(2,1)}), bf16[1024,3072]{1,0:T(8,128)(2,1)}) %all-gather.7.cloned.1.call-update) | async-done | bytes 6291472 | tf_op jit(solution)/shard_map/all_gather | solution.py:46
  83.2 10.3 add_convert_fusion
  107.7 4.9 copy.64
  112.6 39.2 %all-gather.11.cloned.1.call-done = bf16[2048,1024]{1,0:T(8,128)(2,1)} async-done(((bf16[1024,1024]{1,0:T(8,128)(2,1)}), bf16[2048,1024]{1,0:T(8,128)(2,1)}) %all-gather.11.cloned.1.call-update) | async-done | bytes 4194320 | tf_op jit(solution)/shard_map/all_gather | solution.py:88
  151.8 58.9 %all-gather.9.cloned.1.call-done = bf16[2048,1024]{1,0:T(8,128)(2,1)} async-done(((bf16[1024,1024]{1,0:T(8,128)(2,1)}), bf16[2048,1024]{1,0:T(8,128)(2,1)}) %all-gather.9.cloned.1.call-update) | async-done | bytes 4194320 | tf_op jit(solution)/shard_map/all_gather | solution.py:87
  210.7 5.5 constant_dynamic-slice_fusion.1
  220.1 4.9 copy.65
  228.9 4.8 copy.66
  235.3 124.6 %while.30 = (s32[]{:T(128)}, bf16[16,1024,64]{1,2,0:T(8,128)(2,1)}, f32[16,1024]{1,0:T(8,128)S(1)}, bf16[16,1024,64]{2,1,0:T(8,128)(2,1)}, bf16[16,1024,64]{2,1,...) while((s32[]{:T(128)}, bf16[16,1024,64]{1,2,0:T(8,128)(2,1)}, ...), condition=%wide.region_7.8_spmd.clone.clone, body=%wide.region_4.7_spmd.clone.clone.sunk | while | flops 285211648 | bytes 13692573 | solution.py:117
  359.9 5.0 fusion.114
  367.7 17.1 fusion.107
  384.8 43.3 %all-gather.17.cloned.1.call-done = bf16[4096,1024]{1,0:T(8,128)(2,1)} async-done(((bf16[128,1024]{1,0:T(8,128)(2,1)}), bf16[4096,1024]{1,0:T(8,128)(2,1)}) %all-gather.17.cloned.1.call-update) | async-done | bytes 8388624 | tf_op jit(solution)/shard_map/all_gather | solution.py:49
  428.2 24.9 %convert_reduce_fusion = (f32[4096]{0:T(1024)}, bf16[1024,4096]{1,0:T(8,128)(2,1)}) fusion(f32[1024,4096]{1,0:T(8,128)} %fusion.107, f32[4096]{0:T(1024)S(1)} %copy-done.31, bf16[4096,1024]{1,0:T(8,128)(2,1)} %all-gather.17.cloned.1.call-done, bf16[1024,1024]{0,1:T(8,128)(2,1)S(1)} %copy-done.8, f32[1024]{0:T(1024)S(1)} %compare_convert_fusion), kind=kOutput, calls=%fused_computation.69 | convolution fusion | flops 8689545216 | bytes 35688448 | tf_op jit(solution)/shard_map/rd,fd->rf/dot_general | solution.py:137
  453.0 16.1 fusion.116
  469.1 5.4 copy.69
  474.5 5.4 multiply_reduce_fusion.1
  493.6 229.3 %while.31 = (s32[]{:T(128)}, bf16[16,1024,64]{1,2,0:T(8,128)(2,1)}, bf16[16,1024,64]{1,2,0:T(8,128)(2,1)S(1)}, bf16[16,1024,64]{1,2,0:T(8,128)(2,1)}, bf16[16,10...) while((s32[]{:T(128)}, bf16[16,1024,64]{1,2,0:T(8,128)(2,1)}, ...), condition=%wide.region_15.16_spmd.clone.clone, body=%wide.region_13.15_spmd.clone.clone.sunk | while | flops 689044480 | bytes 34122412 | solution.py:170
  725.4 19.4 %dynamic_update_slice.24 = bf16[2048,1024]{0,1:T(8,128)(2,1)} dynamic-update-slice(bf16[2048,1024]{0,1:T(8,128)(2,1)} %broadcast_in_dim.112.clone, bf16[1024,1024]{0,1:T(8,128)(2,1)} %bitcast.136, s32[]{:T(128)S(6)} %select_n.77, s32[]{:T(128)} %constant.124.clone.1) | dynamic-update-slice | bytes 4194308 | tf_op jit(solution)/shard_map/dynamic_update_slice | solution.py:178
  747.4 19.0 %dynamic_update_slice.23 = bf16[2048,1024]{0,1:T(8,128)(2,1)} dynamic-update-slice(bf16[2048,1024]{0,1:T(8,128)(2,1)} %broadcast_in_dim.112.clone.1, bf16[1024,1024]{0,1:T(8,128)(2,1)S(1)} %bitcast.135, s32[]{:T(128)S(6)} %select_n.77, s32[]{:T(128)} %constant.124.clone.1) | dynamic-update-slice | bytes 4194308 | tf_op jit(solution)/shard_map/dynamic_update_slice | solution.py:175
  768.0 6.0 fusion.117
  774.4 23.5 %reduce-scatter.9.cloned.1.call-done = bf16[1024,1024]{0,1:T(8,128)(2,1)} async-done(((bf16[2048,1024]{0,1:T(8,128)(2,1)}), bf16[1024,1024]{0,1:T(8,128)(2,1)}) %reduce-scatter.9.cloned.1.call-update) | async-done | bytes 2097168 | tf_op jit(solution)/shard_map/reduce_scatter | solution.py:185
  797.9 56.7 %reduce-scatter.7.cloned.1.call-done = bf16[1024,1024]{0,1:T(8,128)(2,1)} async-done(((bf16[2048,1024]{0,1:T(8,128)(2,1)}), bf16[1024,1024]{0,1:T(8,128)(2,1)}) %reduce-scatter.7.cloned.1.call-update) | async-done | bytes 2097168 | tf_op jit(solution)/shard_map/reduce_scatter | solution.py:182
  854.7 14.2 fusion.102
  869.5 16.7 fusion.106
  887.0 21.0 %fusion.79 = f32[4096,1024]{1,0:T(8,128)} fusion(bf16[1024,1024]{0,1:T(8,128)(2,1)} %copy.68, f32[1024]{0:T(1024)S(1)} %compare_convert_fusion, f32[1024,4096]{1,0:T(8,128)} %fusion.107, f32[4096]{0:T(1024)S(1)} %copy-done.32), kind=kOutput, calls=%fused_computation.104 | convolution fusion | flops 8635023360 | bytes 35672064 | tf_op jit(solution)/shard_map/rf,rd->fd/dot_general | solution.py:135
  908.7 17.2 add_convert_fusion.2
  929.8 12.3 fusion.115
  942.1 5.4 copy.74
  965.2 40.9 %all-reduce = (f32[1024]{0:T(1024)}, f32[1024]{0:T(1024)}, f32[2048]{0:T(1024)}, f32[1024]{0:T(1024)}, f32[1024]{0:T(1024)}, /*index=5*/f32[1024]{0:T(1024)}, f32[4096]{0:T(1024)}, f32[1024]{0:T(1024)}) all-reduce(f32[1024]{0:T(1024)S(1)} %get-tuple-element.379, ...), channel_id=1, replica_groups=mesh['dp'=16,'seq'=2] {'dp','seq'}, use_global_device_ids=true, to_apply=%region_21.22 | all-reduce | flops 12288 | bytes 98304 | tf_op jit(solution)/shard_map/psum | solution.py:212
  1006.0 152.9 %reduce-scatter.11.cloned.1.call-done = f32[32,3072]{1,0:T(8,128)} async-done(((f32[1024,3072]{1,0:T(8,128)}), f32[32,3072]{1,0:T(8,128)}) %reduce-scatter.11.cloned.1.call-update) | async-done | bytes 393232 | tf_op jit(solution)/shard_map/reduce_scatter | solution.py:198
  1158.9 359.5 %reduce-scatter.15.cloned.1.call-done = f32[32,4096]{1,0:T(8,128)} async-done(((f32[1024,4096]{1,0:T(8,128)}), f32[32,4096]{1,0:T(8,128)}) %reduce-scatter.15.cloned.1.call-update) | async-done | bytes 524304 | tf_op jit(solution)/shard_map/reduce_scatter | solution.py:200
  1518.4 361.5 %reduce-scatter.17.cloned.1.call-done = f32[128,1024]{1,0:T(8,128)} async-done(((f32[4096,1024]{1,0:T(8,128)}), f32[128,1024]{1,0:T(8,128)}) %reduce-scatter.17.cloned.1.call-update) | async-done | bytes 524304 | tf_op jit(solution)/shard_map/reduce_scatter | solution.py:201
  (380 shorter events, 428.2 us)
Async XLA Ops:
  7.2 76.0 %all-gather.7.cloned.1.call-start = ((), (), s32[]{:S(2)}) async-start(), calls=%async_computation.6 | async-start | bytes 6488064 | tf_op jit(solution)/shard_map/all_gather | solution.py:46
  7.9 75.2 %copy-start.21 = (f32[1024]{0:T(1024)S(1)}, f32[1024]{0:T(1024)}, u32[]{:S(2)}) copy-start(f32[1024]{0:T(1024)} %param.21) | copy-start | bytes 12292
  7.9 75.2 %copy-start.34 = (f32[1024]{0:T(1024)S(1)}, f32[1024]{0:T(1024)}, u32[]{:S(2)}) copy-start(f32[1024]{0:T(1024)} %param.22) | copy-start | bytes 12292
  7.9 143.9 %all-gather.11.cloned.1.call-start = ((), (), s32[]{:S(2)}) async-start(), calls=%async_computation.8 | async-start | bytes 6291456 | tf_op jit(solution)/shard_map/all_gather | solution.py:88
  10.9 349.1 %copy-start = (bf16[1024,1024]{0,1:T(8,128)(2,1)}, bf16[1024,1024]{0,1:T(8,128)(2,1)S(1)}, u32[]{:S(2)}) copy-start(bf16[1024,1024]{0,1:T(8,128)(2,1)S(1)} %copy.60) | copy-start | bytes 6291460
  11.3 82.2 %copy-start.13 = (f32[1024]{0:T(1024)}, f32[1024]{0:T(1024)S(1)}, u32[]{:S(2)}) copy-start(f32[1024]{0:T(1024)S(1)} %broadcast_multiply_fusion.1) | copy-start | bytes 12292
  12.5 81.0 %copy-start.15 = (f32[1024]{0:T(1024)}, f32[1024]{0:T(1024)S(1)}, u32[]{:S(2)}) copy-start(f32[1024]{0:T(1024)S(1)} %fusion.98) | copy-start | bytes 12292
  96.4 114.3 %all-gather.9.cloned.1.call-start = ((), (), s32[]{:S(2)}) async-start(), calls=%async_computation.7 | async-start | bytes 6291456 | tf_op jit(solution)/shard_map/all_gather | solution.py:87
  97.1 262.8 %all-gather.13.cloned.1.call-start = ((), (), s32[]{:S(2)}) async-start(), calls=%async_computation.9 | async-start | bytes 2162688 | tf_op jit(solution)/shard_map/all_gather | solution.py:47
  97.7 269.9 %all-gather.15.cloned.1.call-start = ((), (), s32[]{:S(2)}) async-start(), calls=%async_computation.10 | async-start | bytes 8650752 | tf_op jit(solution)/shard_map/all_gather | solution.py:48
  98.3 329.8 %all-gather.17.cloned.1.call-start = ((), (), s32[]{:S(2)}) async-start(), calls=%async_computation.11 | async-start | bytes 8650752 | tf_op jit(solution)/shard_map/all_gather | solution.py:49
  98.9 699.0 %reduce-scatter.9.cloned.1.call-start = ((), (), s32[]{:S(2)}) async-start(), calls=%async_computation.13 | async-start | bytes 6291456 | tf_op jit(solution)/shard_map/reduce_scatter | solution.py:185
  235.3 124.7 %copy-start.33 = (f32[1024]{0:T(1024)S(1)}, f32[1024]{0:T(1024)}, u32[]{:S(2)}) copy-start(f32[1024]{0:T(1024)} %param.26) | copy-start | bytes 12292
  367.6 60.5 %copy-start.8 = (bf16[1024,1024]{0,1:T(8,128)(2,1)S(1)}, bf16[1024,1024]{0,1:T(8,128)(2,1)}, u32[]{:S(2)}) copy-start(bf16[1024,1024]{0,1:T(8,128)(2,1)} %copy.68) | copy-start | bytes 6291460
  367.6 60.5 %copy-start.31 = (f32[4096]{0:T(1024)S(1)}, f32[4096]{0:T(1024)}, u32[]{:S(2)}) copy-start(f32[4096]{0:T(1024)} %param.30) | copy-start | bytes 49156
  474.5 5.4 copy-start.6
  474.5 5.9 copy-start.7
  744.9 109.8 %reduce-scatter.7.cloned.1.call-start = ((), (), s32[]{:S(2)}) async-start(), calls=%async_computation.12 | async-start | bytes 6291456 | tf_op jit(solution)/shard_map/reduce_scatter | solution.py:182
  766.5 239.6 %reduce-scatter.13.cloned.1.call-start = ((), (), s32[]{:S(2)}) async-start(), calls=%async_computation.15 | async-start | bytes 4325376 | tf_op jit(solution)/shard_map/reduce_scatter | solution.py:199
  774.1 80.6 %copy-start.1 = (bf16[1024,1024]{0,1:T(8,128)(2,1)S(1)}, bf16[1024,1024]{0,1:T(8,128)(2,1)}, u32[]{:S(2)}) copy-start(bf16[1024,1024]{0,1:T(8,128)(2,1)} %copy-done) | copy-start | bytes 6291460
  774.1 80.6 %copy-start.14 = (f32[1024]{0:T(1024)S(1)}, f32[1024]{0:T(1024)}, u32[]{:S(2)}) copy-start(f32[1024]{0:T(1024)} %copy-done.13) | copy-start | bytes 12292
  774.1 80.6 %copy-start.16 = (f32[1024]{0:T(1024)S(1)}, f32[1024]{0:T(1024)}, u32[]{:S(2)}) copy-start(f32[1024]{0:T(1024)} %copy-done.15) | copy-start | bytes 12292
  774.1 80.6 %copy-start.22 = (f32[1024]{0:T(1024)S(1)}, f32[1024]{0:T(1024)}, u32[]{:S(2)}) copy-start(f32[1024]{0:T(1024)} %param.21) | copy-start | bytes 12292
  774.1 80.6 %copy-start.35 = (f32[1024]{0:T(1024)S(1)}, f32[1024]{0:T(1024)}, u32[]{:S(2)}) copy-start(f32[1024]{0:T(1024)} %param.22) | copy-start | bytes 12292
  774.1 384.8 %reduce-scatter.11.cloned.1.call-start = ((), (), s32[]{:S(2)}) async-start(), calls=%async_computation.14 | async-start | bytes 12976128 | tf_op jit(solution)/shard_map/reduce_scatter | solution.py:198
  868.9 649.6 %reduce-scatter.15.cloned.1.call-start = ((), (), s32[]{:S(2)}) async-start(), calls=%async_computation.16 | async-start | bytes 17301504 | tf_op jit(solution)/shard_map/reduce_scatter | solution.py:200
  886.3 993.7 %reduce-scatter.17.cloned.1.call-start = ((), (), s32[]{:S(2)}) async-start(), calls=%async_computation.17 | async-start | bytes 17301504 | tf_op jit(solution)/shard_map/reduce_scatter | solution.py:201
  956.9 4.1 copy-start.10
  961.0 4.1 copy-start.25
  961.0 4.1 copy-start.26
  961.0 4.1 copy-start.27
  961.1 4.1 copy-start.29
  (21 other events, 50.9 us)
Sparse Core Ops, SparseCore 0:
  10.9 72.1 all-gather.6
  96.5 55.2 all-gather.10
  153.9 56.7 all-gather.8
  213.6 56.4 all-gather.12
  272.9 76.3 all-gather.14
  352.1 75.9 all-gather.16
  745.0 52.8 reduce-scatter.8
  800.3 54.3 reduce-scatter.6
  857.5 142.2 reduce-scatter.12
  1006.2 152.6 reduce-scatter.10
  1161.9 356.4 reduce-scatter.14
  1521.3 358.6 reduce-scatter.16
where the time goes:
time: 1900 us; the launch traced here: 1890 us
  waiting for transfers between devices  1170 us (62%)
  matrix products  468 us (25%)
  local copies, waits for them, and re-layouts  141 us (7%)
  other arithmetic  50.8 us (3%)
  blocking collectives  40.9 us (2%)
    reduce_scatter x1, waiting for transfers between devices, shards(): lax.psum_scatter(grad_down_w, ('dp', 'seq'), scatter_dimension=0, tiled=T...  362 us
    reduce_scatter x1, waiting for transfers between devices, shards(): lax.psum_scatter(grad_up_w, ('dp', 'seq'), scatter_dimension=0, tiled=True)  359 us
    reduce_scatter x1, waiting for transfers between devices, shards(): lax.psum_scatter(grad_qkv_w, ('dp', 'seq'), scatter_dimension=0, tiled=True)  153 us
    dot_general x32, matrix products, scores_of(): jnp.einsum('qd,kd->qk', head_query, head_key, preferred_element_type=f32)  137 us
    all_gather x1, waiting for transfers between devices, shards(): lax.all_gather(qkv_weight, ('dp', 'seq'), axis=0, tiled=True)  70.6 us
    all_gather x1, waiting for transfers between devices, shards(): lax.all_gather(joined[:, width:2 * width], 'seq', axis=0, tiled=True)  58.9 us
    reduce_scatter x1, waiting for transfers between devices, shards(): lax.psum_scatter(key_terms.astype(jnp.bfloat16), 'seq', scatter_dimension...  56.7 us
    all_gather x1, waiting for transfers between devices, shards(): lax.all_gather(down_weight, ('dp', 'seq'), axis=0, tiled=True)  43.3 us
  transfers between devices with their start and end apart: 12, of which 9 were waited for; matrix products, arithmetic and copies ran while one was open for 17% of the time, Pallas kernels for 0%

commit v1 on v0

--- a/solution.py
+++ b/solution.py
@@ -1,11 +1,142 @@
+import functools
+
 import jax
 import jax.numpy as jnp
+import ml_dtypes
+import numpy as np
 from jax import lax
+from jax.experimental import pallas as pl
+from jax.experimental.pallas import tpu as pltpu
 from jax.sharding import PartitionSpec as P
 
 H = 16
 SEQLEN = 1024
 SG = 2
+BQ = 256
+f32 = jnp.float32
+bf16 = jnp.bfloat16
+NT = (((1,), (1,)), ((), ()))
+
+
+def dot(a, b):
+    return jnp.dot(a, b, preferred_element_type=f32)
+
+
+def dotnt(a, b):
+    return lax.dot_general(a, b, NT, preferred_element_type=f32)
+
+
+LOG2E=1.4426950408889634
+
+def attn_fwd_kernel(len_ref, slope_ref, q_ref, k_ref, v_ref, o_ref, lse_ref):
+    pair=pl.program_id(0)
+    n=q_ref.shape[0]
+    length=len_ref[0]
+    lane=lax.broadcasted_iota(jnp.int32,(1,128),1)
+    first=lane<64
+    place=lax.broadcasted_iota(jnp.int32,(1,n),1)
+    ones=jnp.ones((n,128),bf16)
+    vaug=jnp.concatenate([v_ref[...],ones],axis=1)
+    k=k_ref[...]
+    diag=lax.broadcasted_iota(jnp.int32,(BQ,BQ),1)<=lax.broadcasted_iota(jnp.int32,(BQ,BQ),0)
+    bias=[jnp.where(place<length, place.astype(f32)*(slope_ref[2*pair+h]*LOG2E), -1e30) for h in range(2)]
+    for i in range(n//BQ):
+        nk=(i+1)*BQ
+        q=q_ref[i*BQ:(i+1)*BQ,:]*jnp.array(0.125,bf16)
+        outs=[];lses=[]
+        for h in range(2):
+            qh=jnp.where(first if h==0 else ~first, q, jnp.zeros_like(q))
+            s=dotnt(qh,k[:nk])*LOG2E+bias[h][:,:nk]
+            sd=jnp.where(diag,s[:,nk-BQ:],-1e30)
+            s=sd if i==0 else jnp.concatenate([s[:,:nk-BQ],sd],axis=1)
+            m=jnp.max(s,axis=1,keepdims=True)
+            p=jnp.exp2(s-m).astype(bf16)
+            o=dot(p,vaug[:nk])
+            tot=o[:,128:]
+            outs.append(o[:,:128]/tot)
+            lses.append((m+jnp.log2(tot))*(1.0/LOG2E))
+        o_ref[i*BQ:(i+1)*BQ,:]=jnp.where(first,outs[0],outs[1]).astype(bf16)
+        lse_ref[i*BQ:(i+1)*BQ,:]=jnp.where(first,lses[0],lses[1])
+
+def attn_fwd(length,slopes,q,k,v):
+    n,D=q.shape; np_=D//128
+    spec=lambda off: pl.BlockSpec((n,128),lambda p,*_: (0,p+off))
+    return pl.pallas_call(attn_fwd_kernel,
+        grid_spec=pltpu.PrefetchScalarGridSpec(num_scalar_prefetch=2,grid=(np_,),
+            in_specs=[spec(0)]*3,out_specs=[spec(0),spec(0)]),
+        out_shape=[jax.ShapeDtypeStruct((n,D),bf16),jax.ShapeDtypeStruct((n,D),f32)],
+        compiler_params=pltpu.CompilerParams(vmem_limit_bytes=48*2**20),
+        cost_estimate=pl.CostEstimate(flops=int(2*2*n*n*D*2.5),bytes_accessed=n*D*12,transcendentals=n*n*10),
+        name="attn_fwd")(length,slopes,q,k,v)
+
+def split3(x):
+    a=x.astype(bf16); r=x-a.astype(f32); b=r.astype(bf16); c=(r-b.astype(f32)).astype(bf16)
+    return a,b,c
+
+def attn_bwd_kernel(len_ref, slope_ref, q_ref, k_ref, v_ref, o_ref, lse_ref, do_ref, dq_ref, dk_ref, dv_ref, qa_ref, doa_ref, dqt_ref):
+    pair=pl.program_id(0)
+    n=q_ref.shape[0]
+    nb=n//BQ
+    length=len_ref[0]
+    lane=lax.broadcasted_iota(jnp.int32,(1,128),1)
+    sub=lane%64
+    first=lane<64
+    place=lax.broadcasted_iota(jnp.int32,(n,128),0)
+    hi=(place//8*8).astype(f32); lo=(place%8).astype(f32)
+    kf=jnp.where(sub<3,-1.0,jnp.where(sub<9,jnp.where(sub%2==1,hi,lo),jnp.where(sub==9,jnp.where(place<length,0.0,-1e30),0.0))).astype(bf16)
+    vf=jnp.where(sub<3,-1.0,0.0).astype(bf16)
+    k=k_ref[...]; v=v_ref[...]
+    kaug=jnp.concatenate([k,kf],axis=1)
+    vaug=jnp.concatenate([v,jnp.broadcast_to(vf,(n,128))],axis=1)
+    q=q_ref[...]*jnp.array(0.125,bf16)
+    do=do_ref[...]
+    prod=do.astype(f32)*o_ref[...].astype(f32)
+    same=(lax.broadcasted_iota(jnp.int32,(128,128),0)//64==lax.broadcasted_iota(jnp.int32,(128,128),1)//64).astype(bf16)
+    p1,p2,p3=split3(prod)
+    dd=dot(p1,same)+dot(p2,same)+dot(p3,same)
+    d1,d2,d3=split3(dd)
+    l1,l2,l3=split3(lse_ref[...])
+    zero=jnp.zeros((n,128),bf16)
+    for h in range(2):
+        mine=first if h==0 else ~first
+        m1=slope_ref[3*(2*pair+h)];m2=slope_ref[3*(2*pair+h)+1];m3=slope_ref[3*(2*pair+h)+2]
+        mf=jnp.where(sub<5,m1,jnp.where(sub<7,m2,jnp.where(sub<9,m3,jnp.where(sub==9,1.0,0.0)))).astype(bf16)
+        qf=jnp.where(sub==0,l1,jnp.where(sub==1,l2,jnp.where(sub==2,l3,jnp.broadcast_to(mf,(n,128)))))
+        df=jnp.where(sub==0,d1,jnp.where(sub==1,d2,jnp.where(sub==2,d3,zero)))
+        qa_ref[h]=jnp.concatenate([jnp.where(mine,q,zero),jnp.where(mine,qf,zero)],axis=1)
+        doa_ref[h]=jnp.concatenate([jnp.where(mine,do,zero),jnp.where(mine,df,zero)],axis=1)
+    kt=k.T
+    diag=lax.broadcasted_iota(jnp.int32,(BQ,BQ),0)<=lax.broadcasted_iota(jnp.int32,(BQ,BQ),1)
+    for j in range(nb):
+        ks=slice(j*BQ,(j+1)*BQ); qs=slice(j*BQ,n)
+        dvs=[];dks=[]
+        for h in range(2):
+            sT=dotnt(kaug[ks],qa_ref[h,qs,:])
+            dpT=dotnt(vaug[ks],doa_ref[h,qs,:])
+            p=jnp.exp(sT)
+            pd=jnp.where(diag,p[:,:BQ],0.0)
+            p=pd if j==nb-1 else jnp.concatenate([pd,p[:,BQ:]],axis=1)
+            ds=(p*dpT).astype(bf16)
+            dvs.append(dot(p.astype(bf16),do_ref[qs,:]))
+            dks.append(dot(ds,q[qs]))
+            t=dot(kt[64*h:64*h+64,ks],ds)
+            if j==0: dqt_ref[64*h:64*h+64,:]=t
+            else: dqt_ref[64*h:64*h+64,qs]+=t
+        dv_ref[ks,:]=jnp.where(first,dvs[0],dvs[1]).astype(bf16)
+        dk_ref[ks,:]=jnp.where(first,dks[0],dks[1]).astype(bf16)
+    dq_ref[...]=(dqt_ref[...]*0.125).T.astype(bf16)
+
+def attn_bwd(length,slopes3,q,k,v,o,lse,do):
+    n,D=q.shape; np_=D//128
+    spec=lambda off: pl.BlockSpec((n,128),lambda p,*_: (0,p+off))
+    return pl.pallas_call(attn_bwd_kernel,
+        grid_spec=pltpu.PrefetchScalarGridSpec(num_scalar_prefetch=2,grid=(np_,),
+            in_specs=[spec(0)]*6,out_specs=[spec(0)]*3,
+            scratch_shapes=[pltpu.VMEM((2,n,256),bf16),pltpu.VMEM((2,n,256),bf16),pltpu.VMEM((128,n),f32)]),
+        out_shape=[jax.ShapeDtypeStruct((n,D),bf16)]*3,
+        compiler_params=pltpu.CompilerParams(vmem_limit_bytes=48*2**20),
+        cost_estimate=pl.CostEstimate(flops=int(5*2*n*n*D*2.5),bytes_accessed=n*D*20,transcendentals=n*n*10),
+        name="attn_bwd")(length,slopes3,q,k,v,o,lse,do)
 
 
 def layer_norm(values, gain, shift):
@@ -18,7 +149,7 @@
     return jax.nn.gelu(values, approximate=True)
 
 
-def shards(
+def generic_shards(
     tokens,
     ln1_gain,
     ln1_bias,
@@ -240,6 +371,277 @@
     )
 
 
+ALL = ("dp", "seq")
+
+
+def flat_index(z, y, c, x):
+    return ((z * 2 + y) * 2 + c) * 2 + x
+
+
+def permutation(move):
+    pairs = []
+    for z in range(4):
+        for y in range(2):
+            for c in range(2):
+                for x in range(2):
+                    pairs.append((flat_index(z, y, c, x), flat_index(*move(z, y, c, x))))
+    return pairs
+
+
+OVER_X = permutation(lambda z, y, c, x: (z, y, c, 1 - x))
+OVER_Y = permutation(lambda z, y, c, x: (z, 1 - y, c, x))
+OVER_C = permutation(lambda z, y, c, x: (z, y, 1 - c, x))
+OVER_Z = [permutation(lambda z, y, c, x, k=k: ((z + k) % 4, y, c, x)) for k in range(4)]
+
+
+def send(array, pairs):
+    return lax.ppermute(array, ALL, pairs)
+
+
+def gather_half(parts, first, second):
+    own = jnp.stack(parts)
+    own_core = send(own, OVER_C)
+    near = send(own, first)
+    near_core = send(near, OVER_C)
+    both = jnp.stack([own, near])
+    far = send(both, second)
+    far_core = send(far, OVER_C)
+    return both, far, own_core, near_core, far_core
+
+
+def gather_stage(shard):
+    parts = [shard] + [send(shard, OVER_Z[k]) for k in (1, 2, 3)]
+    return (
+        gather_half([p[0] for p in parts], OVER_X, OVER_Y),
+        gather_half([p[1] for p in parts], OVER_Y, OVER_X),
+    )
+
+
+def assemble_kernel(put, place_ref, *refs):
+    outs, sem = refs[10:-1], refs[-1]
+    z, y, c, x = (place_ref[i] for i in range(4))
+
+    def copies(go):
+        for half in range(2):
+            both, far, own_core, near_core, far_core = refs[5 * half : 5 * half + 5]
+            for zr in range(4):
+                za = (z + 4 - zr) % 4
+                for near in range(2):
+                    for turn in range(2):
+                        for core in range(2):
+                            if core == 0:
+                                src = (far if turn else both).at[near, zr]
+                            elif turn:
+                                src = far_core.at[near, zr]
+                            else:
+                                src = (near_core if near else own_core).at[zr]
+                            xr, yr = (near, turn) if half == 0 else (turn, near)
+                            d = flat_index(
+                                za, y + yr - 2 * y * yr, c + core - 2 * c * core, x + xr - 2 * x * xr
+                            )
+                            for b, dst in put(half, d, outs):
+                                go(pltpu.make_async_copy(src.at[b], dst, sem))
+
+    copies(lambda copy: copy.start())
+    copies(lambda copy: copy.wait())
+
+
+def put_blocks(half, d, outs):
+    return [(b, outs[2 * half + b].at[pl.ds(pl.multiple_of(d * 32, 32), 32), :]) for b in range(2)]
+
+
+def put_rows(half, d, outs):
+    return [(0, outs[0].at[pl.ds(pl.multiple_of(d * 128 + half * 64, 64), 64), :])]
+
+
+def assemble(place, halves, put, out_shape):
+    return pl.pallas_call(
+        functools.partial(assemble_kernel, put),
+        grid_spec=pltpu.PrefetchScalarGridSpec(
+            num_scalar_prefetch=1,
+            grid=(),
+            in_specs=[pl.BlockSpec(memory_space=pl.ANY)] * 10,
+            out_specs=[pl.BlockSpec(memory_space=pltpu.VMEM)] * len(out_shape),
+            scratch_shapes=[pltpu.SemaphoreType.DMA],
+        ),
+        out_shape=out_shape,
+        compiler_params=pltpu.CompilerParams(vmem_limit_bytes=32 * 2**20),
+        cost_estimate=pl.CostEstimate(flops=0, bytes_accessed=2 * 8 * 2**20, transcendentals=0),
+        name="assemble",
+    )(place, *halves[0], *halves[1])
+
+
+def add_low(a, b):
+    return (a.astype(f32) + b.astype(f32)).astype(bf16)
+
+
+def take(array, at, axis):
+    return lax.dynamic_index_in_dim(array, at, axis, keepdims=False)
+
+
+def reduce_half(grads, place, x_first):
+    z, y, c, x = place
+    g = add_low(take(grads, c, 2), send(take(grads, 1 - c, 2), OVER_C))
+    if x_first:
+        g = add_low(take(g, x, 2), send(take(g, 1 - x, 2), OVER_X))
+        g = add_low(take(g, y, 1), send(take(g, 1 - y, 1), OVER_Y))
+    else:
+        g = add_low(take(g, y, 1), send(take(g, 1 - y, 1), OVER_Y))
+        g = add_low(take(g, x, 1), send(take(g, 1 - x, 1), OVER_X))
+    total = take(g, z, 0).astype(f32)
+    for k in (1, 2, 3):
+        total = total + send(take(g, (z + k) % 4, 0), OVER_Z[k]).astype(f32)
+    return total
+
+
+def reduce_pair(left, right, place, x_first):
+    both = jnp.concatenate(
+        [left.reshape(4, 2, 2, 2, 32, 1024), right.reshape(4, 2, 2, 2, 32, 1024)], axis=4
+    )
+    total = reduce_half(both, place, x_first)
+    return total[:32], total[32:]
+
+
+def all_sum(v, place):
+    v = v + send(v, OVER_C)
+    v = v + send(v, OVER_X)
+    v = v + send(v, OVER_Y)
+    return v + send(v, OVER_Z[1]) + send(v, OVER_Z[2]) + send(v, OVER_Z[3])
+
+
+def slope_table():
+    slopes = np.exp2(-8.0 * (np.arange(H) + 1.0) / H).astype(np.float32)
+    pieces, rest = [], slopes
+    for _ in range(3):
+        low = rest.astype(ml_dtypes.bfloat16).astype(np.float32)
+        pieces.append(low)
+        rest = rest - low
+    return slopes, np.stack(pieces, axis=1).reshape(-1)
+
+
+def fast_shards(
+    tokens,
+    ln1_gain,
+    ln1_bias,
+    qkv_weight,
+    qkv_bias,
+    dense_weight,
+    dense_bias,
+    ln2_gain,
+    ln2_bias,
+    up_weight,
+    up_bias,
+    down_weight,
+    down_bias,
+    cotangent,
+    seq_lengths,
+    slot_order,
+):
+    rows, width = tokens.shape
+    dp, seq = lax.axis_index("dp"), lax.axis_index("seq")
+    place = (dp // 4, (dp // 2) % 2, dp % 2, seq)
+    place_vec = jnp.stack([p.astype(jnp.int32) for p in place])
+
+    def columns(w):
+        return w.reshape(32, w.shape[1] // 1024, 1024).transpose(1, 0, 2)
+
+    shard_one = jnp.concatenate([columns(qkv_weight), dense_weight[None]]).reshape(2, 2, 32, 1024)
+    shard_two = columns(up_weight).reshape(2, 2, 32, 1024)
+    shard_three = down_weight.reshape(2, 1, 64, 1024)
+    square = [jax.ShapeDtypeStruct((1024, 1024), bf16)] * 4
+    w_q, w_k, w_v, w_dense = assemble(place_vec, gather_stage(shard_one), put_blocks, square)
+    w_up = assemble(place_vec, gather_stage(shard_two), put_blocks, square)
+    (w_down,) = assemble(
+        place_vec, gather_stage(shard_three), put_rows, [jax.ShapeDtypeStruct((4096, 1024), bf16)]
+    )
+
+    slot = dp * SG + seq
+    my_seq = lax.dynamic_index_in_dim(slot_order, slot, 0, keepdims=False)
+    every_seq = jnp.arange(seq_lengths.shape[0], dtype=jnp.int32)
+    length = jnp.sum(jnp.where(every_seq == my_seq, seq_lengths, 0))
+    length_vec = length.reshape(1)
+    valid = (jnp.arange(rows, dtype=jnp.int32) < length).astype(f32)
+    slopes, slopes_split = slope_table()
+
+    inputs = tokens.astype(f32)
+    normed_one, norm_one_back = jax.vjp(layer_norm, inputs, ln1_gain, ln1_bias)
+    a1 = normed_one.astype(bf16)
+    query = (dot(a1, w_q) + qkv_bias[:width]).astype(bf16)
+    key = dot(a1, w_k).astype(bf16)
+    value = (dot(a1, w_v) + qkv_bias[width:]).astype(bf16)
+    context, lse = attn_fwd(length_vec, jnp.asarray(slopes), query, key, value)
+    hidden = inputs + dot(context, w_dense) + dense_bias
+    normed_two, norm_two_back = jax.vjp(layer_norm, hidden, ln2_gain, ln2_bias)
+    a2 = normed_two.astype(bf16)
+    blocks = range(4)
+    before = [dot(a2, w_up[i]) + up_bias[i * 1024 : (i + 1) * 1024] for i in blocks]
+    active, gelu_back = zip(*[jax.vjp(gelu_tanh, b) for b in before])
+    active = [a.astype(bf16) for a in active]
+    grad_out = cotangent.astype(f32) * valid[:, None]
+    grad_low = grad_out.astype(bf16)
+    grad_down_b = jnp.sum(grad_out, axis=0)
+
+    def outer(a, b):
+        return jnp.einsum("rd,rf->df", a, b, preferred_element_type=f32).astype(bf16)
+
+    grad_down_w = [outer(active[i], grad_low) for i in blocks]
+    mlp = sum(dot(active[i], w_down[i * 1024 : (i + 1) * 1024]) for i in blocks)
+    block_output = (hidden + mlp + down_bias).astype(bf16)
+    down_terms = jnp.concatenate(grad_down_w).reshape(4, 2, 2, 2, 2, 64, 1024)
+    owner_down = jnp.concatenate(
+        [
+            reduce_half(down_terms[:, :, :, :, 0], place, True),
+            reduce_half(down_terms[:, :, :, :, 1], place, False),
+        ]
+    )
+    grad_active = [dotnt(grad_low, w_down[i * 1024 : (i + 1) * 1024]) for i in blocks]
+    grad_before = [gelu_back[i](grad_active[i])[0].astype(bf16) for i in blocks]
+    grad_up_w = [outer(a2, grad_before[i]) for i in blocks]
+    up_01 = reduce_pair(grad_up_w[0], grad_up_w[1], place, True)
+    up_23 = reduce_pair(grad_up_w[2], grad_up_w[3], place, False)
+    owner_up = jnp.concatenate(up_01 + up_23, axis=1)
+    grad_up_b = jnp.concatenate([jnp.sum(g.astype(f32), axis=0) for g in grad_before])
+    grad_normed_two = sum(dotnt(grad_before[i], w_up[i]) for i in blocks)
+    grad_hidden_norm, grad_gain_two, grad_shift_two = norm_two_back(grad_normed_two)
+    grad_hidden = grad_out + grad_hidden_norm
+    grad_hidden_low = grad_hidden.astype(bf16)
+    grad_dense_w = outer(context, grad_hidden_low)
+    grad_dense_b = jnp.sum(grad_hidden_low.astype(f32), axis=0)
+    grad_context = dotnt(grad_hidden_low, w_dense).astype(bf16)
+    early = all_sum(
+        jnp.concatenate(
+            [grad_dense_b, grad_gain_two, grad_shift_two, grad_up_b, grad_down_b]
+        ).reshape(8, 1024),
+        place,
+    )
+    grad_q, grad_k, grad_v = attn_bwd(
+        length_vec, jnp.asarray(slopes_split), query, key, value, context, lse, grad_context
+    )
+    owner_q, owner_k = reduce_pair(outer(a1, grad_q), outer(a1, grad_k), place, True)
+    owner_v, owner_dense = reduce_pair(outer(a1, grad_v), grad_dense_w, place, False)
+    grad_qkv_b = [jnp.sum(g.astype(f32), axis=0) for g in (grad_q, grad_v)]
+    grad_normed_one = dotnt(grad_q, w_q) + dotnt(grad_k, w_k) + dotnt(grad_v, w_v)
+    grad_input_norm, grad_gain_one, grad_shift_one = norm_one_back(grad_normed_one)
+    token_grad = (grad_hidden + grad_input_norm).astype(bf16)
+    late = all_sum(jnp.stack(grad_qkv_b + [grad_gain_one, grad_shift_one]), place)
+    return (
+        block_output,
+        token_grad,
+        late[2],
+        late[3],
+        jnp.concatenate([owner_q, owner_k, owner_v], axis=1),
+        late[:2].reshape(2 * width),
+        owner_dense,
+        early[0],
+        early[1],
+        early[2],
+        owner_up,
+        early[3:7].reshape(4 * width),
+        owner_down,
+        early[7],
+    )
+
+
 def solution(mesh):
     in_specs = (
         P(("dp", "seq"), None),
@@ -275,4 +677,5 @@
         P(("dp", "seq"), None),
         P(),
     )
-    return jax.shard_map(shards, mesh=mesh, in_specs=in_specs, out_specs=out_specs, check_vma=False)
+    body = fast_shards if mesh.shape["dp"] == 16 and mesh.shape["seq"] == 2 else generic_shards
+    return jax.shard_map(body, mesh=mesh, in_specs=in_specs, out_specs=out_specs, check_vma=False)

time: 1900 us -> 659 us (0.35)
  waiting for transfers between devices: 1170 us -> 184 us
  matrix products: 468 us -> 164 us
  starting transfers between devices: 1.27 us -> 110 us
  Pallas kernels: 0 us -> 100 us
  local copies, waits for them, and re-layouts: 141 us -> 46.2 us
  blocking collectives: 40.9 us -> 0 us
    reduce_scatter x6 -> x0, waiting for transfers between devices: 954 us -> none  [the longest x1 362 us: shards(): lax.psum_scatter(grad_down_w, ('dp', 'seq'), scatter_dimension=0, tiled=T...]
    dot_general x124 -> x36, matrix products: 468 us -> 164 us  [the longest x12 64.4 us: dotnt(): return lax.dot_general(a, b, NT, preferred_element_type=f32)]
    all_gather x6 -> x0, waiting for transfers between devices: 212 us -> none  [the longest x1 70.6 us: shards(): lax.all_gather(qkv_weight, ('dp', 'seq'), axis=0, tiled=True)]
    ppermute x0 -> x87, waiting for transfers between devices: none -> 184 us  [send(): return lax.ppermute(array, ALL, pairs)]
    ppermute x0 -> x87, starting transfers between devices: none -> 110 us  [send(): return lax.ppermute(array, ALL, pairs)]
    pallas_call x0 -> x5, Pallas kernels: none -> 100 us  [the longest x1 39.3 us: attn_bwd(): pl.pallas_call(attn_bwd_kernel, grid_spec=pltpu.PrefetchScalarGridSpec(nu...]
    psum x1 -> x0, blocking collectives: 40.9 us -> none  [shards(): lax.psum((grad_gain_one, grad_shift_one, grad_qkv_b, grad_dense_b, grad_g...]
    dynamic_update_slice x18 -> x0, local copies, waits for them, and re-layouts: 39.8 us -> none  [the longest x1 19.4 us: shards(): lax.dynamic_update_slice_in_dim(empty_group, merge_heads(grad_values), wi...]
  transfers between devices with their start and end apart: 12 -> 87, of which waited for: 9 -> 28; matrix products, arithmetic and copies ran while one was open for 17% -> 17% of each run, Pallas kernels for 0% -> 7%
where the time goes in v1:
time: 659 us; the launch traced here: 655 us
  waiting for transfers between devices  184 us (28%)
  matrix products  164 us (25%)
  starting transfers between devices  110 us (17%)
  Pallas kernels  100 us (15%)
  other arithmetic  47.8 us (7%)
  local copies, waits for them, and re-layouts  46.2 us (7%)
    ppermute x87, waiting for transfers between devices, send(): return lax.ppermute(array, ALL, pairs)  184 us
    ppermute x87, starting transfers between devices, send(): return lax.ppermute(array, ALL, pairs)  110 us
    dot_general x12, matrix products, dotnt(): return lax.dot_general(a, b, NT, preferred_element_type=f32)  64.4 us
    dot_general x12, matrix products, dot(): return jnp.dot(a, b, preferred_element_type=f32)  55.8 us
    dot_general x12, matrix products, outer(): jnp.einsum('rd,rf->df', a, b, preferred_element_type=f32).astype(bf16)  43.4 us
    pallas_call x1, Pallas kernels, attn_bwd(): pl.pallas_call(attn_bwd_kernel, grid_spec=pltpu.PrefetchScalarGridSpec(nu...  39.3 us
    pallas_call x3, Pallas kernels, assemble(): pl.pallas_call(functools.partial(assemble_kernel, put), grid_spec=pltpu.P...  35.1 us
    unnamed x223, local copies, waits for them, and re-layouts  27.3 us
  transfers between devices with their start and end apart: 87, of which 28 were waited for; matrix products, arithmetic and copies ran while one was open for 17% of the time, Pallas kernels for 7%

profile of v1, /device:TPU:0, one launch (start us, length us, event | category | flops | bytes accessed | tf_op | source)
XLA Modules:
  0.0 654.8 jit_solution(12465578065973635437)
XLA Ops:
  3.2 5.0 collective-permute-start.2
  26.8 6.3 collective-permute-done.1
  33.1 6.9 %collective-permute-start.15 = (bf16[2,2,32,1024]{3,2,1,0:T(8,128)(2,1)S(1)}, bf16[2,2,32,1024]{3,2,1,0:T(8,128)(2,1)S(1)}, u32[]{:S(2)}, u32[]{:S(2)}) collective-permute-start(bf16[2,2,32,1024]{3,2,1,0:T(8,128)(2,1)S(1)} %bitcast.322), channel_id=1, source_target_pairs={{0,24},{1,25},{2,26},{3,27},{4,28},{5,29},{6,30},{7,31},{8,0},{9,1... | collective-permute-start | bytes 786440 | tf_op jit(solution)/shard_map/ppermute | solution.py:398
  41.1 13.1 %collective-permute-start.14 = (bf16[2,2,32,1024]{3,2,1,0:T(8,128)(2,1)S(1)}, bf16[2,2,32,1024]{3,2,1,0:T(8,128)(2,1)S(1)}, u32[]{:S(2)}, u32[]{:S(2)}) collective-permute-start(bf16[2,2,32,1024]{3,2,1,0:T(8,128)(2,1)S(1)} %bitcast.323), channel_id=1, source_target_pairs={{0,16},{1,17},{2,18},{3,19},{4,20},{5,21},{6,22},{7,23},{8,24},{9,... | collective-permute-start | bytes 786440 | tf_op jit(solution)/shard_map/ppermute | solution.py:398
  83.4 27.8 %collective-permute-done.29 = bf16[4,1,64,1024]{3,2,0,1:T(8,128)(2,1)S(1)} collective-permute-done((bf16[4,1,64,1024]{3,2,0,1:T(8,128)(2,1)S(1)}, bf16[4,1,64,1024]{3,2,0,1:T(8,128)(2,1)S(1)}, u32[]{:S(2)}, u32[]{:S(2)}) %collective-permute-start.29) | collective-permute-done | bytes 524320 | tf_op jit(solution)/shard_map/ppermute | solution.py:398
  128.3 9.2 %assemble.3 = (bf16[1024,1024]{1,0:T(8,128)(2,1)S(1)}, bf16[1024,1024]{1,0:T(8,128)(2,1)S(1)}, bf16[1024,1024]{1,0:T(8,128)(2,1)S(1)}, bf16[1024,1024]{1,0:T(8,128)(2,1)S(1)}) custom-call(s32[4]{0:T(128)S(1)} %pad_add_fusion.place_ref, bf16[2,4,2,32,1024]{4,3,2,1,0:T(8,128)(2,1)S(1)} %pad_maximum_fusion.1.refs_0_, ...), custom_call_target="tpu_custom_call" | custom-call | bytes 16777216 | tf_op jit(solution)/shard_map/assemble/pallas_call | solution.py:458
  148.5 26.0 %attn_fwd.1 = (bf16[1024,1024]{1,0:T(8,128)(2,1)S(1)}, f32[1024,1024]{1,0:T(8,128)}) custom-call(s32[1]{0:T(128)} %bitcast.1.len_ref, f32[16]{0:T(128)S(1)} %copy-done.14, bf16[1024,1024]{1,0:T(8,128)(2,1)S(1)} %add_convert_fusion.4.q_ref, bf16[1024,1024]{1,0:T(8,128)(2,1)} %convolution_convert_fusion.13.k_ref, bf16[1024,1024]{1,0:T(8,128)(2,1)} %add_convert_fusion.3.v_ref), custom_call_target="tpu_custom_call" | custom-call | flops 10737418240 | bytes 12582912 | tf_op jit(solution)/shard_map/attn_fwd/pallas_call | solution.py:64
  174.5 5.0 fusion.157
  186.3 19.0 %collective-permute-done.30 = bf16[2,4,1,64,1024]{4,3,1,2,0:T(8,128)(2,1)S(1)} collective-permute-done((bf16[2,4,1,64,1024]{4,3,1,2,0:T(8,128)(2,1)S(1)}, bf16[2,4,1,64,1024]{4,3,1,2,0:T(8,128)(2,1)S(1)}, u32[]{:S(2)}, u32[]{:S(2)}) %collective-permute-start.30) | collective-permute-done | bytes 1048608 | tf_op jit(solution)/shard_map/ppermute | solution.py:398
  207.1 13.3 %assemble.4 = (bf16[1024,1024]{1,0:T(8,128)(2,1)S(1)}, bf16[1024,1024]{1,0:T(8,128)(2,1)S(1)}, bf16[1024,1024]{1,0:T(8,128)(2,1)S(1)}, bf16[1024,1024]{1,0:T(8,128)(2,1)S(1)}) custom-call(s32[4]{0:T(128)S(1)} %pad_add_fusion.place_ref, bf16[2,4,2,32,1024]{4,3,2,1,0:T(8,128)(2,1)S(1)} %pad_maximum_fusion.3.refs_0_, ...), custom_call_target="tpu_custom_call" | custom-call | bytes 16777216 | tf_op jit(solution)/shard_map/assemble/pallas_call | solution.py:458
  227.7 12.7 %assemble.5 = bf16[4096,1024]{1,0:T(8,128)(2,1)S(1)} custom-call(s32[4]{0:T(128)S(1)} %pad_add_fusion.place_ref, bf16[2,4,1,64,1024]{4,3,2,1,0:T(8,128)(2,1)S(1)} %get-tuple-element.98.refs_0_, bf16[2,4,1,64,1024]{4,3,2,1,0:T(8,128)(2,1)S(1)} %bitcast.300, bf16[4,1,64,1024]{3,2,1,0:T(8,128)(2,1)S(1)} %bitcast.302, bf16[4,1,64,1024]{3,2,1,0:T(8,128)(2,1)S(1)} %bitcast.304, ...), custom_call_target="tpu_custom_call" | custom-call | bytes 16777216 | tf_op jit(solution)/shard_map/assemble/pallas_call | solution.py:458
  250.3 6.9 %convert_reduce_fusion.2 = (f32[1024]{0:T(1024)}, bf16[1024,1024]{1,0:T(8,128)(2,1)}) fusion(f32[1024,1024]{1,0:T(8,128)S(1)} %fusion.160, f32[1024]{0:T(1024)S(1)} %get-tuple-element.172, bf16[4096,1024]{1,0:T(8,128)(2,1)S(1)} %assemble.5, bf16[1024,1024]{0,1:T(8,128)(2,1)S(1)} %copy-done.23, f32[1024]{0:T(1024)S(1)} %fusion.118), kind=kOutput, calls=%fused_computation.83 | convolution fusion | flops 2174745600 | bytes 10498048 | tf_op jit(solution)/shard_map/dot_general | solution.py:26
  257.2 8.5 %convert_reduce_fusion.4 = (f32[1024]{0:T(1024)}, bf16[1024,1024]{1,0:T(8,128)(2,1)}) fusion(f32[1024,1024]{1,0:T(8,128)} %fusion.158, f32[1024]{0:T(1024)S(1)} %get-tuple-element.171, bf16[4096,1024]{1,0:T(8,128)(2,1)S(1)} %assemble.5, bf16[1024,1024]{0,1:T(8,128)(2,1)S(1)} %copy-done.23, f32[1024]{0:T(1024)S(1)} %fusion.118), kind=kOutput, calls=%fused_computation.85 | convolution fusion | flops 2174745600 | bytes 10498048 | tf_op jit(solution)/shard_map/dot_general | solution.py:26
  272.8 7.0 %convert_reduce_fusion.3 = (f32[1024]{0:T(1024)}, bf16[1024,1024]{1,0:T(8,128)(2,1)}) fusion(f32[1024,1024]{1,0:T(8,128)S(1)} %fusion.159, f32[1024]{0:T(1024)S(1)} %get-tuple-element.170, bf16[4096,1024]{1,0:T(8,128)(2,1)S(1)} %assemble.5, bf16[1024,1024]{0,1:T(8,128)(2,1)S(1)} %copy-done.23, f32[1024]{0:T(1024)S(1)} %fusion.118), kind=kOutput, calls=%fused_computation.84 | convolution fusion | flops 2174745600 | bytes 10498048 | tf_op jit(solution)/shard_map/dot_general | solution.py:26
  295.3 6.6 %convert_reduce_fusion.1 = (f32[1024]{0:T(1024)S(1)}, bf16[1024,1024]{1,0:T(8,128)(2,1)}) fusion(f32[1024,1024]{1,0:T(8,128)S(1)} %copy-done.87, f32[1024]{0:T(1024)S(1)} %copy-done.75, bf16[4096,1024]{1,0:T(8,128)(2,1)S(1)} %assemble.5, bf16[1024,1024]{0,1:T(8,128)(2,1)S(1)} %copy-done.23, f32[1024]{0:T(1024)S(1)} %fusion.118), kind=kOutput, calls=%fused_computation.82 | convolution fusion | flops 2174745600 | bytes 10498048 | tf_op jit(solution)/shard_map/dot_general | solution.py:26
  301.9 6.8 %multiply_reduce_fusion = (f32[1024]{0:T(1024)S(1)}, f32[1024]{0:T(1024)S(1)}, f32[1024]{0:T(1024)S(1)}, f32[1024,1024]{0,1:T(8,128)S(1)}) fusion(f32[1024,1024]{0,1:T(8,128)S(1)} %copy-done.19, f32[1024]{0:T(1024)S(1)} %fusion.120, f32[1024]{0:T(1024)S(1)} %broadcast_multiply_fusion, f32[1024]{0:T(1024)S(1)} %copy-done.62, f32[1024,1024]{0,1:T(8,128)S(1)} %fusion.164, ...), kind=kOutput, calls=%fused_computation.86 | convolution fusion | flops 2159014912 | bytes 25190400 | tf_op jit(solution)/shard_map/dot_general | solution.py:26
  314.5 39.3 %attn_bwd.1 = (bf16[1024,1024]{1,0:T(8,128)(2,1)S(1)}, bf16[1024,1024]{1,0:T(8,128)(2,1)S(1)}, bf16[1024,1024]{1,0:T(8,128)(2,1)}) custom-call(s32[1]{0:T(128)} %bitcast.1.len_ref, f32[48]{0:T(128)S(1)} %copy-done.13, bf16[1024,1024]{1,0:T(8,128)(2,1)} %copy-done.17, bf16[1024,1024]{1,0:T(8,128)(2,1)} %convolution_convert_fusion.13.k_ref, ...), custom_call_target="tpu_custom_call" | custom-call | flops 26843545600 | bytes 20971520 | tf_op jit(solution)/shard_map/attn_bwd/pallas_call | solution.py:132
  385.3 4.9 convolution_convert_fusion
  390.2 5.4 convolution_convert_fusion.1
  395.6 4.9 convolution_convert_fusion.2
  405.4 5.1 fusion.38
  423.3 12.5 %add_convert_fusion.1 = bf16[1024,1024]{0,1:T(8,128)(2,1)} fusion(f32[1024,1024]{0,1:T(8,128)} %copy-done.18, f32[1024,1024]{0,1:T(8,128)} %fusion.71, f32[1024,1024]{0,1:T(8,128)} %fusion.83, f32[1024,1024]{0,1:T(8,128)} %fusion.77, f32[1024]{0:T(1024)S(1)} %copy-done.83, bf16[4096,1024]{1,0:T(8,128)(2,1)} %copy-done, f32[1024,1024]{1,0:T(8,128)} %fusion.161, ...), kind=kOutput, calls=%fused_computation.98 | convolution fusion | flops 2164260864 | bytes 25174016 | tf_op jit(solution)/shard_map/dot_general | solution.py:22
  499.6 13.0 %collective-permute-done.52 = bf16[4,2,64,1024]{3,2,0,1:T(8,128)(2,1)S(1)} collective-permute-done((bf16[4,2,64,1024]{3,2,0,1:T(8,128)(2,1)S(1)}, bf16[4,2,64,1024]{3,2,0,1:T(8,128)(2,1)S(1)}, u32[]{:S(2)}, u32[]{:S(2)}) %collective-permute-start.52) | collective-permute-done | bytes 1048608 | tf_op jit(solution)/shard_map/ppermute | solution.py:398
  518.0 17.2 %collective-permute-done.70 = bf16[4,2,64,1024]{3,2,0,1:T(8,128)(2,1)S(1)} collective-permute-done((bf16[4,2,64,1024]{3,2,0,1:T(8,128)(2,1)S(1)}, bf16[4,2,64,1024]{3,2,0,1:T(8,128)(2,1)S(1)}, u32[]{:S(2)}, u32[]{:S(2)}) %collective-permute-start.70) | collective-permute-done | bytes 1048608 | tf_op jit(solution)/shard_map/ppermute | solution.py:398
  540.4 17.2 %collective-permute-done.82 = bf16[4,2,64,1024]{3,2,0,1:T(8,128)(2,1)S(1)} collective-permute-done((bf16[4,2,64,1024]{3,2,0,1:T(8,128)(2,1)S(1)}, bf16[4,2,64,1024]{3,2,0,1:T(8,128)(2,1)S(1)}, u32[]{:S(2)}, u32[]{:S(2)}) %collective-permute-start.82) | collective-permute-done | bytes 1048608 | tf_op jit(solution)/shard_map/ppermute | solution.py:398
  562.9 10.2 %collective-permute-done.53 = bf16[4,64,1024]{2,1,0:T(8,128)(2,1)S(1)} collective-permute-done((bf16[4,64,1024]{2,1,0:T(8,128)(2,1)S(1)}, bf16[4,64,1024]{2,1,0:T(8,128)(2,1)S(1)}, u32[]{:S(2)}, u32[]{:S(2)}) %collective-permute-start.53) | collective-permute-done | bytes 524320 | tf_op jit(solution)/shard_map/ppermute | solution.py:398
  576.3 8.0 %collective-permute-done.71 = bf16[4,64,1024]{2,1,0:T(8,128)(2,1)S(1)} collective-permute-done((bf16[4,64,1024]{2,1,0:T(8,128)(2,1)S(1)}, bf16[4,64,1024]{2,1,0:T(8,128)(2,1)S(1)}, u32[]{:S(2)}, u32[]{:S(2)}) %collective-permute-start.71) | collective-permute-done | bytes 524320 | tf_op jit(solution)/shard_map/ppermute | solution.py:398
  587.5 6.8 %collective-permute-done.83 = bf16[4,64,1024]{2,1,0:T(8,128)(2,1)S(1)} collective-permute-done((bf16[4,64,1024]{2,1,0:T(8,128)(2,1)S(1)}, bf16[4,64,1024]{2,1,0:T(8,128)(2,1)S(1)}, u32[]{:S(2)}, u32[]{:S(2)}) %collective-permute-start.83) | collective-permute-done | bytes 524320 | tf_op jit(solution)/shard_map/ppermute | solution.py:398
  602.4 10.1 %collective-permute-done.49 = bf16[64,1024]{1,0:T(8,128)(2,1)S(1)} collective-permute-done((bf16[64,1024]{1,0:T(8,128)(2,1)S(1)}, bf16[64,1024]{1,0:T(8,128)(2,1)S(1)}, u32[]{:S(2)}, u32[]{:S(2)}) %collective-permute-start.49) | collective-permute-done | bytes 131104 | tf_op jit(solution)/shard_map/ppermute | solution.py:398
  612.5 7.6 %collective-permute-start.67 = (bf16[64,1024]{1,0:T(8,128)(2,1)S(1)}, bf16[64,1024]{1,0:T(8,128)(2,1)S(1)}, u32[]{:S(2)}, u32[]{:S(2)}) collective-permute-start(bf16[64,1024]{1,0:T(8,128)(2,1)S(1)} %get-tuple-element.107), channel_id=1, source_target_pairs={{0,16},{1,17},{2,18},{3,19},{4,20},{5,21},{6,22},{7,23},{8,24},{9,... | collective-permute-start | bytes 393224 | tf_op jit(solution)/shard_map/ppermute | solution.py:398
  630.2 6.0 collective-permute-done.67
  640.8 6.6 %collective-permute-done.85 = bf16[64,1024]{1,0:T(8,128)(2,1)S(1)} collective-permute-done((bf16[64,1024]{1,0:T(8,128)(2,1)S(1)}, bf16[64,1024]{1,0:T(8,128)(2,1)S(1)}, u32[]{:S(2)}, u32[]{:S(2)}) %collective-permute-start.85) | collective-permute-done | bytes 131104 | tf_op jit(solution)/shard_map/ppermute | solution.py:398
  (523 shorter events, 297.0 us)
Async XLA Ops:
  8.2 32.9 %collective-permute-start = (bf16[2,2,32,1024]{3,2,1,0:T(8,128)(2,1)}, bf16[2,2,32,1024]{3,2,1,0:T(8,128)(2,1)}, u32[]{:S(2)}, u32[]{:S(2)}) collective-permute-start(bf16[2,2,32,1024]{3,2,1,0:T(8,128)(2,1)} %bitcast.9), channel_id=1, source_target_pairs={{0,8},{1,9},{2,10},{3,11},{4,12},{5,13},{6,14},{7,15},{8,16},{9,17... | collective-permute-start | bytes 786440 | tf_op jit(solution)/shard_map/ppermute | solution.py:398
  9.2 46.1 %collective-permute-start.28 = (bf16[2,1,64,1024]{3,2,0,1:T(8,128)(2,1)}, bf16[2,1,64,1024]{3,2,0,1:T(8,128)(2,1)S(1)}, u32[]{:S(2)}, u32[]{:S(2)}) collective-permute-start(bf16[2,1,64,1024]{3,2,0,1:T(8,128)(2,1)} %bitcast.25), channel_id=1, source_target_pairs={{0,24},{1,25},{2,26},{3,27},{4,28},{5,29},{6,30},{7,31},{8,0},{9,1... | collective-permute-start | bytes 786440 | tf_op jit(solution)/shard_map/ppermute | solution.py:398
  12.0 48.0 %collective-permute-start.27 = (bf16[2,1,64,1024]{3,2,0,1:T(8,128)(2,1)}, bf16[2,1,64,1024]{3,2,0,1:T(8,128)(2,1)}, u32[]{:S(2)}, u32[]{:S(2)}) collective-permute-start(bf16[2,1,64,1024]{3,2,0,1:T(8,128)(2,1)} %bitcast.25), channel_id=1, source_target_pairs={{0,16},{1,17},{2,18},{3,19},{4,20},{5,21},{6,22},{7,23},{8,24},{9,... | collective-permute-start | bytes 786440 | tf_op jit(solution)/shard_map/ppermute | solution.py:398
  22.9 39.7 %collective-permute-start.26 = (bf16[2,1,64,1024]{3,2,0,1:T(8,128)(2,1)}, bf16[2,1,64,1024]{3,2,0,1:T(8,128)(2,1)S(1)}, u32[]{:S(2)}, u32[]{:S(2)}) collective-permute-start(bf16[2,1,64,1024]{3,2,0,1:T(8,128)(2,1)} %bitcast.25), channel_id=1, source_target_pairs={{0,8},{1,9},{2,10},{3,11},{4,12},{5,13},{6,14},{7,15},{8,16},{9,17... | collective-permute-start | bytes 786440 | tf_op jit(solution)/shard_map/ppermute | solution.py:398
  33.1 40.6 %collective-permute-start.15 = (bf16[2,2,32,1024]{3,2,1,0:T(8,128)(2,1)S(1)}, bf16[2,2,32,1024]{3,2,1,0:T(8,128)(2,1)S(1)}, u32[]{:S(2)}, u32[]{:S(2)}) collective-permute-start(bf16[2,2,32,1024]{3,2,1,0:T(8,128)(2,1)S(1)} %bitcast.322), channel_id=1, source_target_pairs={{0,24},{1,25},{2,26},{3,27},{4,28},{5,29},{6,30},{7,31},{8,0},{9,1... | collective-permute-start | bytes 786440 | tf_op jit(solution)/shard_map/ppermute | solution.py:398
  41.1 34.6 %collective-permute-start.14 = (bf16[2,2,32,1024]{3,2,1,0:T(8,128)(2,1)S(1)}, bf16[2,2,32,1024]{3,2,1,0:T(8,128)(2,1)S(1)}, u32[]{:S(2)}, u32[]{:S(2)}) collective-permute-start(bf16[2,2,32,1024]{3,2,1,0:T(8,128)(2,1)S(1)} %bitcast.323), channel_id=1, source_target_pairs={{0,16},{1,17},{2,18},{3,19},{4,20},{5,21},{6,22},{7,23},{8,24},{9,... | collective-permute-start | bytes 786440 | tf_op jit(solution)/shard_map/ppermute | solution.py:398
  72.2 39.5 %collective-permute-start.4 = (bf16[2,4,2,32,1024]{4,3,2,1,0:T(8,128)(2,1)S(1)}, bf16[2,4,2,32,1024]{4,3,2,1,0:T(8,128)(2,1)S(1)}, u32[]{:S(2)}, u32[]{:S(2)}) collective-permute-start(bf16[2,4,2,32,1024]{4,3,2,1,0:T(8,128)(2,1)S(1)} %pad_maximum_fusion.1.refs_0_), channel_id=1, source_target_pairs={{0,4},{1,5},{2,6},{3,7},{4,0},{5,1},{6,2},{7,3},{8,12},{9,13},{10,... | collective-permute-start | bytes 3145736 | tf_op jit(solution)/shard_map/ppermute | solution.py:398
  73.8 37.9 %collective-permute-start.9 = (bf16[2,4,2,32,1024]{4,3,2,1,0:T(8,128)(2,1)S(1)}, bf16[2,4,2,32,1024]{4,3,2,1,0:T(8,128)(2,1)}, u32[]{:S(2)}, u32[]{:S(2)}) collective-permute-start(bf16[2,4,2,32,1024]{4,3,2,1,0:T(8,128)(2,1)S(1)} %pad_maximum_fusion.2.refs_5_), channel_id=1, source_target_pairs={{0,1},{1,0},{2,3},{3,2},{4,5},{5,4},{6,7},{7,6},{8,9},{9,8},{10,11... | collective-permute-start | bytes 3145736 | tf_op jit(solution)/shard_map/ppermute | solution.py:398
  75.7 35.5 %collective-permute-start.29 = (bf16[4,1,64,1024]{3,2,0,1:T(8,128)(2,1)S(1)}, bf16[4,1,64,1024]{3,2,0,1:T(8,128)(2,1)S(1)}, u32[]{:S(2)}, u32[]{:S(2)}) collective-permute-start(bf16[4,1,64,1024]{3,2,0,1:T(8,128)(2,1)S(1)} %get-tuple-element.124), channel_id=1, source_target_pairs={{0,1},{1,0},{2,3},{3,2},{4,5},{5,4},{6,7},{7,6},{8,9},{9,8},{10,11... | collective-permute-start | bytes 1572872 | tf_op jit(solution)/shard_map/ppermute | solution.py:398
  78.3 40.1 %collective-permute-start.34 = (bf16[4,1,64,1024]{3,2,0,1:T(8,128)(2,1)}, bf16[4,1,64,1024]{3,2,0,1:T(8,128)(2,1)}, u32[]{:S(2)}, u32[]{:S(2)}) collective-permute-start(bf16[4,1,64,1024]{3,2,0,1:T(8,128)(2,1)} %get-tuple-element.122), channel_id=1, source_target_pairs={{0,4},{1,5},{2,6},{3,7},{4,0},{5,1},{6,2},{7,3},{8,12},{9,13},{10,... | collective-permute-start | bytes 1572872 | tf_op jit(solution)/shard_map/ppermute | solution.py:398
  82.8 35.7 %collective-permute-start.16 = (bf16[4,2,32,1024]{3,2,1,0:T(8,128)(2,1)}, bf16[4,2,32,1024]{3,2,1,0:T(8,128)(2,1)}, u32[]{:S(2)}, u32[]{:S(2)}) collective-permute-start(bf16[4,2,32,1024]{3,2,1,0:T(8,128)(2,1)} %get-tuple-element.120), channel_id=1, source_target_pairs={{0,1},{1,0},{2,3},{3,2},{4,5},{5,4},{6,7},{7,6},{8,9},{9,8},{10,11... | collective-permute-start | bytes 1572872 | tf_op jit(solution)/shard_map/ppermute | solution.py:398
  125.7 54.0 %collective-permute-start.18 = (bf16[4,2,32,1024]{3,2,1,0:T(8,128)(2,1)}, bf16[4,2,32,1024]{3,2,1,0:T(8,128)(2,1)S(1)}, u32[]{:S(2)}, u32[]{:S(2)}) collective-permute-start(bf16[4,2,32,1024]{3,2,1,0:T(8,128)(2,1)} %get-tuple-element.120), channel_id=1, source_target_pairs={{0,2},{1,3},{2,0},{3,1},{4,6},{5,7},{6,4},{7,5},{8,10},{9,11},{10,... | collective-permute-start | bytes 1572872 | tf_op jit(solution)/shard_map/ppermute | solution.py:398
  126.2 55.0 %collective-permute-start.23 = (bf16[4,2,32,1024]{3,2,1,0:T(8,128)(2,1)}, bf16[4,2,32,1024]{3,2,1,0:T(8,128)(2,1)S(1)}, u32[]{:S(2)}, u32[]{:S(2)}) collective-permute-start(bf16[4,2,32,1024]{3,2,1,0:T(8,128)(2,1)} %get-tuple-element.118), channel_id=1, source_target_pairs={{0,2},{1,3},{2,0},{3,1},{4,6},{5,7},{6,4},{7,5},{8,10},{9,11},{10,... | collective-permute-start | bytes 1572872 | tf_op jit(solution)/shard_map/ppermute | solution.py:398
  126.3 55.5 %collective-permute-start.17 = (bf16[2,4,2,32,1024]{4,3,2,1,0:T(8,128)(2,1)S(1)}, bf16[2,4,2,32,1024]{4,3,2,1,0:T(8,128)(2,1)S(1)}, u32[]{:S(2)}, u32[]{:S(2)}) collective-permute-start(bf16[2,4,2,32,1024]{4,3,2,1,0:T(8,128)(2,1)S(1)} %pad_maximum_fusion.3.refs_0_), channel_id=1, source_target_pairs={{0,4},{1,5},{2,6},{3,7},{4,0},{5,1},{6,2},{7,3},{8,12},{9,13},{10,... | collective-permute-start | bytes 3145736 | tf_op jit(solution)/shard_map/ppermute | solution.py:398
  126.8 55.0 %collective-permute-start.22 = (bf16[2,4,2,32,1024]{4,3,2,1,0:T(8,128)(2,1)S(1)}, bf16[2,4,2,32,1024]{4,3,2,1,0:T(8,128)(2,1)S(1)}, u32[]{:S(2)}, u32[]{:S(2)}) collective-permute-start(bf16[2,4,2,32,1024]{4,3,2,1,0:T(8,128)(2,1)S(1)} %pad_maximum_fusion.4.refs_5_), channel_id=1, source_target_pairs={{0,1},{1,0},{2,3},{3,2},{4,5},{5,4},{6,7},{7,6},{8,9},{9,8},{10,11... | collective-permute-start | bytes 3145736 | tf_op jit(solution)/shard_map/ppermute | solution.py:398
  128.3 54.5 %collective-permute-start.19 = (bf16[4,2,32,1024]{3,2,1,0:T(8,128)(2,1)}, bf16[4,2,32,1024]{3,2,1,0:T(8,128)(2,1)S(1)}, u32[]{:S(2)}, u32[]{:S(2)}) collective-permute-start(bf16[4,2,32,1024]{3,2,1,0:T(8,128)(2,1)} %collective-permute-done.16), channel_id=1, source_target_pairs={{0,2},{1,3},{2,0},{3,1},{4,6},{5,7},{6,4},{7,5},{8,10},{9,11},{10,... | collective-permute-start | bytes 1572872 | tf_op jit(solution)/shard_map/ppermute | solution.py:398
  179.7 25.6 %collective-permute-start.30 = (bf16[2,4,1,64,1024]{4,3,1,2,0:T(8,128)(2,1)S(1)}, bf16[2,4,1,64,1024]{4,3,1,2,0:T(8,128)(2,1)S(1)}, u32[]{:S(2)}, u32[]{:S(2)}) collective-permute-start(bf16[2,4,1,64,1024]{4,3,1,2,0:T(8,128)(2,1)S(1)} %copy-done.49), channel_id=1, source_target_pairs={{0,4},{1,5},{2,6},{3,7},{4,0},{5,1},{6,2},{7,3},{8,12},{9,13},{10,... | collective-permute-start | bytes 3145736 | tf_op jit(solution)/shard_map/ppermute | solution.py:398
  181.3 25.3 %collective-permute-start.35 = (bf16[2,4,1,64,1024]{4,3,2,1,0:T(8,128)(2,1)S(1)}, bf16[2,4,1,64,1024]{4,3,2,1,0:T(8,128)(2,1)S(1)}, u32[]{:S(2)}, u32[]{:S(2)}) collective-permute-start(bf16[2,4,1,64,1024]{4,3,2,1,0:T(8,128)(2,1)S(1)} %pad_maximum_fusion.6.refs_5_), channel_id=1, source_target_pairs={{0,1},{1,0},{2,3},{3,2},{4,5},{5,4},{6,7},{7,6},{8,9},{9,8},{10,11... | collective-permute-start | bytes 3145736 | tf_op jit(solution)/shard_map/ppermute | solution.py:398
  186.2 36.6 %collective-permute-start.31 = (bf16[4,1,64,1024]{3,2,0,1:T(8,128)(2,1)S(1)}, bf16[4,1,64,1024]{3,2,0,1:T(8,128)(2,1)S(1)}, u32[]{:S(2)}, u32[]{:S(2)}) collective-permute-start(bf16[4,1,64,1024]{3,2,0,1:T(8,128)(2,1)S(1)} %copy-done.51), channel_id=1, source_target_pairs={{0,2},{1,3},{2,0},{3,1},{4,6},{5,7},{6,4},{7,5},{8,10},{9,11},{10,... | collective-permute-start | bytes 1572872 | tf_op jit(solution)/shard_map/ppermute | solution.py:398
  420.7 62.7 %collective-permute-start.51 = (bf16[4,2,2,64,1024]{4,3,0,2,1:T(8,128)(2,1)}, bf16[4,2,2,64,1024]{4,3,0,2,1:T(8,128)(2,1)}, u32[]{:S(2)}, u32[]{:S(2)}) collective-permute-start(bf16[4,2,2,64,1024]{4,3,0,2,1:T(8,128)(2,1)} %bitcast.292), channel_id=1, source_target_pairs={{0,2},{1,3},{2,0},{3,1},{4,6},{5,7},{6,4},{7,5},{8,10},{9,11},{10,... | collective-permute-start | bytes 6291464 | tf_op jit(solution)/shard_map/ppermute | solution.py:398
  422.6 63.9 %collective-permute-start.45 = (bf16[4,2,2,64,1024]{4,3,0,1,2:T(8,128)(2,1)}, bf16[4,2,2,64,1024]{4,3,0,1,2:T(8,128)(2,1)}, u32[]{:S(2)}, u32[]{:S(2)}) collective-permute-start(bf16[4,2,2,64,1024]{4,3,0,1,2:T(8,128)(2,1)} %bitcast.293), channel_id=1, source_target_pairs={{0,2},{1,3},{2,0},{3,1},{4,6},{5,7},{6,4},{7,5},{8,10},{9,11},{10,... | collective-permute-start | bytes 6291464 | tf_op jit(solution)/shard_map/ppermute | solution.py:398
  486.6 26.1 %collective-permute-start.52 = (bf16[4,2,64,1024]{3,2,0,1:T(8,128)(2,1)S(1)}, bf16[4,2,64,1024]{3,2,0,1:T(8,128)(2,1)S(1)}, u32[]{:S(2)}, u32[]{:S(2)}) collective-permute-start(bf16[4,2,64,1024]{3,2,0,1:T(8,128)(2,1)S(1)} %dynamic-slice_bitcast_fusion.4), channel_id=1, source_target_pairs={{0,4},{1,5},{2,6},{3,7},{4,0},{5,1},{6,2},{7,3},{8,12},{9,13},{10,... | collective-permute-start | bytes 3145736 | tf_op jit(solution)/shard_map/ppermute | solution.py:398
  490.8 26.1 %collective-permute-start.46 = (bf16[4,2,64,1024]{3,2,0,1:T(8,128)(2,1)S(1)}, bf16[4,2,64,1024]{3,2,0,1:T(8,128)(2,1)S(1)}, u32[]{:S(2)}, u32[]{:S(2)}) collective-permute-start(bf16[4,2,64,1024]{3,2,0,1:T(8,128)(2,1)S(1)} %dynamic-slice_bitcast_fusion.5), channel_id=1, source_target_pairs={{0,1},{1,0},{2,3},{3,2},{4,5},{5,4},{6,7},{7,6},{8,9},{9,8},{10,11... | collective-permute-start | bytes 3145736 | tf_op jit(solution)/shard_map/ppermute | solution.py:398
  492.5 42.6 %collective-permute-start.70 = (bf16[4,2,64,1024]{3,2,0,1:T(8,128)(2,1)S(1)}, bf16[4,2,64,1024]{3,2,0,1:T(8,128)(2,1)S(1)}, u32[]{:S(2)}, u32[]{:S(2)}) collective-permute-start(bf16[4,2,64,1024]{3,2,0,1:T(8,128)(2,1)S(1)} %dynamic-slice_bitcast_fusion.2), channel_id=1, source_target_pairs={{0,4},{1,5},{2,6},{3,7},{4,0},{5,1},{6,2},{7,3},{8,12},{9,13},{10,... | collective-permute-start | bytes 3145736 | tf_op jit(solution)/shard_map/ppermute | solution.py:398
  495.3 44.1 %collective-permute-start.64 = (bf16[4,2,64,1024]{3,2,0,1:T(8,128)(2,1)S(1)}, bf16[4,2,64,1024]{3,2,0,1:T(8,128)(2,1)S(1)}, u32[]{:S(2)}, u32[]{:S(2)}) collective-permute-start(bf16[4,2,64,1024]{3,2,0,1:T(8,128)(2,1)S(1)} %dynamic-slice_bitcast_fusion.3), channel_id=1, source_target_pairs={{0,1},{1,0},{2,3},{3,2},{4,5},{5,4},{6,7},{7,6},{8,9},{9,8},{10,11... | collective-permute-start | bytes 3145736 | tf_op jit(solution)/shard_map/ppermute | solution.py:398
  497.1 60.5 %collective-permute-start.82 = (bf16[4,2,64,1024]{3,2,0,1:T(8,128)(2,1)S(1)}, bf16[4,2,64,1024]{3,2,0,1:T(8,128)(2,1)S(1)}, u32[]{:S(2)}, u32[]{:S(2)}) collective-permute-start(bf16[4,2,64,1024]{3,2,0,1:T(8,128)(2,1)S(1)} %dynamic-slice_bitcast_fusion), channel_id=1, source_target_pairs={{0,4},{1,5},{2,6},{3,7},{4,0},{5,1},{6,2},{7,3},{8,12},{9,13},{10,... | collective-permute-start | bytes 3145736 | tf_op jit(solution)/shard_map/ppermute | solution.py:398
  512.6 49.2 %collective-permute-start.76 = (bf16[4,2,64,1024]{3,2,0,1:T(8,128)(2,1)S(1)}, bf16[4,2,64,1024]{3,2,0,1:T(8,128)(2,1)S(1)}, u32[]{:S(2)}, u32[]{:S(2)}) collective-permute-start(bf16[4,2,64,1024]{3,2,0,1:T(8,128)(2,1)S(1)} %dynamic-slice_bitcast_fusion.1), channel_id=1, source_target_pairs={{0,1},{1,0},{2,3},{3,2},{4,5},{5,4},{6,7},{7,6},{8,9},{9,8},{10,11... | collective-permute-start | bytes 3145736 | tf_op jit(solution)/shard_map/ppermute | solution.py:398
  516.9 56.2 %collective-permute-start.53 = (bf16[4,64,1024]{2,1,0:T(8,128)(2,1)S(1)}, bf16[4,64,1024]{2,1,0:T(8,128)(2,1)S(1)}, u32[]{:S(2)}, u32[]{:S(2)}) collective-permute-start(bf16[4,64,1024]{2,1,0:T(8,128)(2,1)S(1)} %dynamic-slice_bitcast_fusion.10), channel_id=1, source_target_pairs={{0,1},{1,0},{2,3},{3,2},{4,5},{5,4},{6,7},{7,6},{8,9},{9,8},{10,11... | collective-permute-start | bytes 1572872 | tf_op jit(solution)/shard_map/ppermute | solution.py:398
  535.1 38.9 %collective-permute-start.47 = (bf16[4,64,1024]{2,1,0:T(8,128)(2,1)S(1)}, bf16[4,64,1024]{2,1,0:T(8,128)(2,1)S(1)}, u32[]{:S(2)}, u32[]{:S(2)}) collective-permute-start(bf16[4,64,1024]{2,1,0:T(8,128)(2,1)S(1)} %dynamic-slice_bitcast_fusion.11), channel_id=1, source_target_pairs={{0,4},{1,5},{2,6},{3,7},{4,0},{5,1},{6,2},{7,3},{8,12},{9,13},{10,... | collective-permute-start | bytes 1572872 | tf_op jit(solution)/shard_map/ppermute | solution.py:398
  539.4 44.9 %collective-permute-start.71 = (bf16[4,64,1024]{2,1,0:T(8,128)(2,1)S(1)}, bf16[4,64,1024]{2,1,0:T(8,128)(2,1)S(1)}, u32[]{:S(2)}, u32[]{:S(2)}) collective-permute-start(bf16[4,64,1024]{2,1,0:T(8,128)(2,1)S(1)} %dynamic-slice_bitcast_fusion.8), channel_id=1, source_target_pairs={{0,1},{1,0},{2,3},{3,2},{4,5},{5,4},{6,7},{7,6},{8,9},{9,8},{10,11... | collective-permute-start | bytes 1572872 | tf_op jit(solution)/shard_map/ppermute | solution.py:398
  557.6 27.2 %collective-permute-start.65 = (bf16[4,64,1024]{2,1,0:T(8,128)(2,1)S(1)}, bf16[4,64,1024]{2,1,0:T(8,128)(2,1)S(1)}, u32[]{:S(2)}, u32[]{:S(2)}) collective-permute-start(bf16[4,64,1024]{2,1,0:T(8,128)(2,1)S(1)} %dynamic-slice_bitcast_fusion.9), channel_id=1, source_target_pairs={{0,4},{1,5},{2,6},{3,7},{4,0},{5,1},{6,2},{7,3},{8,12},{9,13},{10,... | collective-permute-start | bytes 1572872 | tf_op jit(solution)/shard_map/ppermute | solution.py:398
  561.9 32.4 %collective-permute-start.83 = (bf16[4,64,1024]{2,1,0:T(8,128)(2,1)S(1)}, bf16[4,64,1024]{2,1,0:T(8,128)(2,1)S(1)}, u32[]{:S(2)}, u32[]{:S(2)}) collective-permute-start(bf16[4,64,1024]{2,1,0:T(8,128)(2,1)S(1)} %dynamic-slice_bitcast_fusion.6), channel_id=1, source_target_pairs={{0,1},{1,0},{2,3},{3,2},{4,5},{5,4},{6,7},{7,6},{8,9},{9,8},{10,11... | collective-permute-start | bytes 1572872 | tf_op jit(solution)/shard_map/ppermute | solution.py:398
  (156 other events, 2138.4 us)

commit v2 on v1

--- a/solution.py
+++ b/solution.py
@@ -1,4 +1,5 @@
 import functools
+import itertools
 
 import jax
 import jax.numpy as jnp
@@ -29,7 +30,7 @@
 LOG2E=1.4426950408889634
 
 def attn_fwd_kernel(len_ref, slope_ref, q_ref, k_ref, v_ref, o_ref, lse_ref):
-    pair=pl.program_id(0)
+    pair=pl.program_id(0)+len_ref[1]
     n=q_ref.shape[0]
     length=len_ref[0]
     lane=lax.broadcasted_iota(jnp.int32,(1,128),1)
@@ -58,23 +59,24 @@
         o_ref[i*BQ:(i+1)*BQ,:]=jnp.where(first,outs[0],outs[1]).astype(bf16)
         lse_ref[i*BQ:(i+1)*BQ,:]=jnp.where(first,lses[0],lses[1])
 
-def attn_fwd(length,slopes,q,k,v):
-    n,D=q.shape; np_=D//128
+def attn_fwd(length,slopes,qkv,start,count):
+    n=qkv.shape[0]; D=qkv.shape[1]//3; full=D//128; np_=count; D=128*count
+    length=jnp.stack([length,jnp.int32(start)])
     spec=lambda off: pl.BlockSpec((n,128),lambda p,*_: (0,p+off))
     return pl.pallas_call(attn_fwd_kernel,
         grid_spec=pltpu.PrefetchScalarGridSpec(num_scalar_prefetch=2,grid=(np_,),
-            in_specs=[spec(0)]*3,out_specs=[spec(0),spec(0)]),
+            in_specs=[spec(start),spec(full+start),spec(2*full+start)],out_specs=[spec(0),spec(0)]),
         out_shape=[jax.ShapeDtypeStruct((n,D),bf16),jax.ShapeDtypeStruct((n,D),f32)],
         compiler_params=pltpu.CompilerParams(vmem_limit_bytes=48*2**20),
         cost_estimate=pl.CostEstimate(flops=int(2*2*n*n*D*2.5),bytes_accessed=n*D*12,transcendentals=n*n*10),
-        name="attn_fwd")(length,slopes,q,k,v)
+        name="attn_fwd")(length,slopes,qkv,qkv,qkv)
 
 def split3(x):
     a=x.astype(bf16); r=x-a.astype(f32); b=r.astype(bf16); c=(r-b.astype(f32)).astype(bf16)
     return a,b,c
 
 def attn_bwd_kernel(len_ref, slope_ref, q_ref, k_ref, v_ref, o_ref, lse_ref, do_ref, dq_ref, dk_ref, dv_ref, qa_ref, doa_ref, dqt_ref):
-    pair=pl.program_id(0)
+    pair=pl.program_id(0)+len_ref[1]
     n=q_ref.shape[0]
     nb=n//BQ
     length=len_ref[0]
@@ -126,17 +128,18 @@
         dk_ref[ks,:]=jnp.where(first,dks[0],dks[1]).astype(bf16)
     dq_ref[...]=(dqt_ref[...]*0.125).T.astype(bf16)
 
-def attn_bwd(length,slopes3,q,k,v,o,lse,do):
-    n,D=q.shape; np_=D//128
+def attn_bwd(length,slopes3,qkv,o,lse,do,start,count):
+    n=qkv.shape[0]; D=qkv.shape[1]//3; full=D//128; np_=count; D=128*count
+    length=jnp.stack([length,jnp.int32(start)])
     spec=lambda off: pl.BlockSpec((n,128),lambda p,*_: (0,p+off))
     return pl.pallas_call(attn_bwd_kernel,
         grid_spec=pltpu.PrefetchScalarGridSpec(num_scalar_prefetch=2,grid=(np_,),
-            in_specs=[spec(0)]*6,out_specs=[spec(0)]*3,
+            in_specs=[spec(start),spec(full+start),spec(2*full+start),spec(start),spec(start),spec(start)],out_specs=[spec(0)]*3,
             scratch_shapes=[pltpu.VMEM((2,n,256),bf16),pltpu.VMEM((2,n,256),bf16),pltpu.VMEM((128,n),f32)]),
         out_shape=[jax.ShapeDtypeStruct((n,D),bf16)]*3,
         compiler_params=pltpu.CompilerParams(vmem_limit_bytes=48*2**20),
         cost_estimate=pl.CostEstimate(flops=int(5*2*n*n*D*2.5),bytes_accessed=n*D*20,transcendentals=n*n*10),
-        name="attn_bwd")(length,slopes3,q,k,v,o,lse,do)
+        name="attn_bwd")(length,slopes3,qkv,qkv,qkv,o,lse,do)
 
 
 def layer_norm(values, gain, shift):
@@ -378,6 +381,520 @@
     return ((z * 2 + y) * 2 + c) * 2 + x
 
 
+TN = (((0,), (0,)), ((), ()))
+MIB = 2**20
+
+
+def owner_of(place_ref, half, zr, near, turn, core, turned):
+    z, y, c, x = (place_ref[i] for i in range(4))
+    xr, yr = (near, turn) if half == 0 else (turn, near)
+    za = (z + 4 - zr) % 4 if turned else zr
+    return flat_index(za, y + yr - 2 * y * yr, c + core - 2 * c * core, x + xr - 2 * x * xr)
+
+
+def start_columns(place_ref, pieces, w_ref, sems, turned):
+    for half in range(2):
+        for zr, near, turn, core in itertools.product(range(4), *[range(2)] * 3):
+            d = owner_of(place_ref, half, zr, near, turn, core, turned)
+            rows = pl.ds(pl.multiple_of(d * 32, 32), 32)
+            src = pieces[4 * half + 2 * core + turn].at[near, zr]
+            dst = w_ref.at[2 * half : 2 * half + 2, rows, :]
+            pltpu.make_async_copy(src, dst, sems.at[half]).start()
+
+
+def wait_columns(w_ref, sems, half):
+    part = w_ref.at[2 * half : 2 * half + 2]
+    pltpu.make_async_copy(part, part, sems.at[half]).wait()
+
+
+def start_rows(place_ref, pieces, w_ref, sems):
+    for zr, half, near, turn, core in itertools.product(range(4), *[range(2)] * 4):
+        d = owner_of(place_ref, half, zr, near, turn, core, False)
+        rows = pl.ds(pl.multiple_of(d * 128 + half * 64, 64), 64)
+        src = pieces[4 * half + 2 * core + turn].at[near, zr, 0]
+        pltpu.make_async_copy(src, w_ref.at[rows, :], sems.at[zr]).start()
+
+
+def wait_rows(w_ref, sems, z):
+    part = w_ref.at[pl.ds(pl.multiple_of(z * 1024, 1024), 1024), :]
+    pltpu.make_async_copy(part, part, sems.at[z]).wait()
+
+
+def dottn(a, b):
+    return lax.dot_general(a, b, TN, preferred_element_type=f32)
+
+
+def spec(shape, index):
+    return pl.BlockSpec(shape, index)
+
+
+def params(mib=56):
+    return pltpu.CompilerParams(vmem_limit_bytes=mib * MIB)
+
+
+PIECES = [pl.BlockSpec(memory_space=pltpu.HBM)] * 8
+
+
+def qkv_kernel(place_ref, *refs):
+    pieces, (a_ref, b_ref, o_ref, all_ref, w_ref, sems, out_sems) = refs[:8], refs[8:]
+    step = pl.program_id(0)
+
+    @pl.when(step == 0)
+    def _():
+        start_columns(place_ref, pieces, w_ref, sems, True)
+
+    for half in range(2):
+        part = slice(2 * half, 2 * half + 2)
+        write = pltpu.make_async_copy(w_ref.at[part], all_ref.at[part], out_sems.at[half])
+
+        @pl.when(step == 4 * half)
+        def _():
+            wait_columns(w_ref, sems, half)
+            write.start()
+
+        @pl.when(step == 5)
+        def _():
+            write.wait()
+
+    w = w_ref[step // 2, :, pl.ds(pl.multiple_of(step % 2 * 512, 512), 512)]
+    o_ref[...] = (dot(a_ref[...], w) + b_ref[...]).astype(bf16)
+
+
+def qkv_call(place, pieces, a, b):
+    n, d = a.shape
+    return pl.pallas_call(
+        qkv_kernel,
+        grid_spec=pltpu.PrefetchScalarGridSpec(
+            num_scalar_prefetch=1,
+            grid=(6,),
+            in_specs=PIECES
+            + [spec((n, d), lambda i, *_: (0, 0)), spec((1, 512), lambda i, *_: (0, i))],
+            out_specs=[
+                spec((n, 512), lambda i, *_: (0, i)),
+                pl.BlockSpec(memory_space=pltpu.HBM),
+            ],
+            scratch_shapes=[
+                pltpu.VMEM((4, d, 1024), bf16),
+                pltpu.SemaphoreType.DMA((2,)),
+                pltpu.SemaphoreType.DMA((2,)),
+            ],
+        ),
+        out_shape=[
+            jax.ShapeDtypeStruct((n, 3 * d), bf16),
+            jax.ShapeDtypeStruct((4, d, 1024), bf16),
+        ],
+        compiler_params=params(),
+        cost_estimate=pl.CostEstimate(
+            flops=2 * n * d * 3 * d, bytes_accessed=2 * (n * d + 8 * d * d + 3 * n * d), transcendentals=0
+        ),
+        name="qkv",
+    )(place, *pieces, a, b.reshape(1, 3 * d))
+
+
+def up_kernel(place_ref, *refs):
+    pieces, (a_ref, b_ref, u_ref, s_ref, w_ref, sems) = refs[:8], refs[8:]
+    step = pl.program_id(0)
+
+    @pl.when(step == 0)
+    def _():
+        start_columns(place_ref, pieces, w_ref, sems, False)
+
+    for half in range(2):
+
+        @pl.when(step == 4 * half)
+        def _():
+            wait_columns(w_ref, sems, half)
+
+    c = 0.7978845608028654
+    w = w_ref[step // 2, :, pl.ds(pl.multiple_of(step % 2 * 512, 512), 512)]
+    for r in range(0, a_ref.shape[0], 256):
+        v = dot(a_ref[r : r + 256, :], w) + b_ref[...]
+        square = v * v
+        h = 0.5 + 0.5 * jnp.tanh(v * (c + (c * 0.044715) * square))
+        u = v * h
+        u_ref[r : r + 256, :] = u.astype(bf16)
+        s_ref[r : r + 256, :] = (
+            h + u * (1.0 - h) * (2.0 * c + (2.0 * c * 0.134145) * square)
+        ).astype(bf16)
+
+
+def up_call(place, pieces, a, b):
+    n, d = a.shape
+    ff = b.shape[0]
+    kb = 512
+    return pl.pallas_call(
+        up_kernel,
+        grid_spec=pltpu.PrefetchScalarGridSpec(
+            num_scalar_prefetch=1,
+            grid=(ff // kb,),
+            in_specs=PIECES
+            + [spec((n, d), lambda i, *_: (0, 0)), spec((1, kb), lambda i, *_: (0, i))],
+            out_specs=[spec((n, kb), lambda i, *_: (0, i))] * 2,
+            scratch_shapes=[pltpu.VMEM((4, d, 1024), bf16), pltpu.SemaphoreType.DMA((2,))],
+        ),
+        out_shape=[jax.ShapeDtypeStruct((n, ff), bf16)] * 2,
+        compiler_params=params(),
+        cost_estimate=pl.CostEstimate(
+            flops=2 * n * d * ff, bytes_accessed=2 * (n * d + d * ff + 2 * n * ff), transcendentals=n * ff
+        ),
+        name="up",
+    )(place, *pieces, a, b.reshape(1, ff))
+
+
+def split_kernel(transposed, where_ref, a_ref, g_ref, keep_ref, give_ref, *scratch):
+    core = where_ref[2]
+    if transposed:
+        (acc_ref,) = scratch
+        acc = dottn(a_ref[...], g_ref[...])
+    else:
+        at_ref, acc_ref = scratch
+
+        @pl.when(pl.program_id(0) == 0)
+        def _():
+            at_ref[...] = a_ref[...].T
+
+        acc = dot(at_ref[...], g_ref[...])
+    acc_ref[...] = acc.astype(bf16).reshape(acc_ref.shape)
+    keep_ref[...] = acc_ref[:, pl.ds(core, 1)].reshape(keep_ref.shape)
+    give_ref[...] = acc_ref[:, pl.ds(1 - core, 1)].reshape(give_ref.shape)
+
+
+def down_grad_call(where, u, g):
+    n, ff = u.shape
+    d = g.shape[1]
+    out = spec((1, 256, d), lambda i, *_: (i, 0, 0))
+    return pl.pallas_call(
+        functools.partial(split_kernel, True),
+        grid_spec=pltpu.PrefetchScalarGridSpec(
+            num_scalar_prefetch=1,
+            grid=(8,),
+            in_specs=[spec((n, 512), lambda i, *_: (0, i)), spec((n, d), lambda i, *_: (0, 0))],
+            out_specs=[out, out],
+            scratch_shapes=[pltpu.VMEM((1, 2, 256, d), bf16)],
+        ),
+        out_shape=[jax.ShapeDtypeStruct((8, 256, d), bf16)] * 2,
+        compiler_params=params(),
+        cost_estimate=pl.CostEstimate(
+            flops=2 * n * d * ff, bytes_accessed=2 * (n * d + d * ff + n * ff), transcendentals=0
+        ),
+        name="down_grad",
+    )(where, u, g)
+
+
+def up_grad_call(where, a, g):
+    n, d = a.shape
+    ff = g.shape[1]
+    out = spec((8, 64, 512), lambda i, *_: (0, 0, i))
+    return pl.pallas_call(
+        functools.partial(split_kernel, False),
+        grid_spec=pltpu.PrefetchScalarGridSpec(
+            num_scalar_prefetch=1,
+            grid=(ff // 512,),
+            in_specs=[spec((n, d), lambda i, *_: (0, 0)), spec((n, 512), lambda i, *_: (0, i))],
+            out_specs=[out, out],
+            scratch_shapes=[pltpu.VMEM((d, n), bf16), pltpu.VMEM((8, 2, 64, 512), bf16)],
+        ),
+        out_shape=[jax.ShapeDtypeStruct((8, 64, ff), bf16)] * 2,
+        compiler_params=params(),
+        cost_estimate=pl.CostEstimate(
+            flops=2 * n * d * ff, bytes_accessed=2 * (n * d + d * ff + n * ff), transcendentals=0
+        ),
+        name="up_grad",
+    )(where, a, g)
+
+
+def down_kernel(place_ref, *refs):
+    pieces, (u_ref, h_ref, b_ref, o_ref, acc_ref, w_ref, sems) = refs[:8], refs[8:]
+    step = pl.program_id(0)
+
+    @pl.when(step == 0)
+    def _():
+        start_rows(place_ref, pieces, w_ref, sems)
+
+    wait_rows(w_ref, sems, step)
+    w = w_ref[pl.ds(pl.multiple_of(step * 1024, 1024), 1024), :]
+
+    @pl.when(step == 0)
+    def _():
+        acc_ref[...] = dot(u_ref[...], w)
+
+    @pl.when((step > 0) & (step < 3))
+    def _():
+        acc_ref[...] += dot(u_ref[...], w)
+
+    @pl.when(step == 3)
+    def _():
+        for r in range(0, u_ref.shape[0], 256):
+            rows = slice(r, r + 256)
+            part = acc_ref[rows, :] + dot(u_ref[rows, :], w)
+            o_ref[rows, :] = (h_ref[rows, :] + part + b_ref[...]).astype(bf16)
+
+
+def down_call(place, pieces, u, hidden, bias):
+    n, ff = u.shape
+    d = hidden.shape[1]
+    whole = lambda s: spec(s, lambda i, *_: (0, 0))
+    return pl.pallas_call(
+        down_kernel,
+        grid_spec=pltpu.PrefetchScalarGridSpec(
+            num_scalar_prefetch=1,
+            grid=(4,),
+            in_specs=PIECES
+            + [spec((n, ff // 4), lambda i, *_: (0, i)), whole((n, d)), whole((1, d))],
+            out_specs=whole((n, d)),
+            scratch_shapes=[
+                pltpu.VMEM((n, d), f32),
+                pltpu.VMEM((ff, d), bf16),
+                pltpu.SemaphoreType.DMA((4,)),
+            ],
+        ),
+        out_shape=jax.ShapeDtypeStruct((n, d), bf16),
+        compiler_params=params(),
+        cost_estimate=pl.CostEstimate(
+            flops=2 * n * d * ff, bytes_accessed=2 * (3 * n * d + d * ff + n * ff), transcendentals=0
+        ),
+        name="down",
+    )(place, *pieces, u, hidden, bias.reshape(1, d))
+
+
+def gate_kernel(place_ref, *refs):
+    pieces, (g_ref, s_ref, z_ref, b_ref, w_ref, sems) = refs[:8], refs[8:]
+    step = pl.program_id(0)
+
+    @pl.when(step == 0)
+    def _():
+        start_rows(place_ref, pieces, w_ref, sems)
+
+    wait_rows(w_ref, sems, step)
+    w = w_ref[pl.ds(pl.multiple_of(step * 1024, 1024), 1024), :]
+    total = None
+    for r in range(0, g_ref.shape[0], 256):
+        rows = slice(r, r + 256)
+        v = (dotnt(g_ref[rows, :], w) * s_ref[rows, :].astype(f32)).astype(bf16)
+        z_ref[rows, :] = v
+        part = jnp.sum(v.astype(f32).reshape(32, 8, v.shape[1]), axis=0)
+        total = part if total is None else total + part
+    b_ref[...] = jnp.sum(total, axis=0, keepdims=True)
+
+
+def gate_call(place, pieces, g, slope):
+    n, d = g.shape
+    ff = slope.shape[1]
+    kb = 1024
+    return pl.pallas_call(
+        gate_kernel,
+        grid_spec=pltpu.PrefetchScalarGridSpec(
+            num_scalar_prefetch=1,
+            grid=(ff // kb,),
+            in_specs=PIECES
+            + [spec((n, d), lambda i, *_: (0, 0)), spec((n, kb), lambda i, *_: (0, i))],
+            out_specs=[spec((n, kb), lambda i, *_: (0, i)), spec((1, kb), lambda i, *_: (0, i))],
+            scratch_shapes=[pltpu.VMEM((ff, d), bf16), pltpu.SemaphoreType.DMA((4,))],
+        ),
+        out_shape=[jax.ShapeDtypeStruct((n, ff), bf16), jax.ShapeDtypeStruct((1, ff), f32)],
+        compiler_params=params(),
+        cost_estimate=pl.CostEstimate(
+            flops=2 * n * d * ff, bytes_accessed=2 * (n * d + d * ff + 2 * n * ff), transcendentals=0
+        ),
+        name="gate",
+    )(place, *pieces, g, slope)
+
+
+def norm_back(x_ref, gain_ref, res_ref, acc_ref, out_refs, sums_ref):
+    n, d = x_ref.shape
+
+    def chunk(i, sums):
+        rows = pl.ds(pl.multiple_of(i * 128, 128), 128)
+        grad = acc_ref[rows, :]
+        x = x_ref[rows, :].astype(f32)
+        center = x - jnp.mean(x, axis=1, keepdims=True)
+        rsd = lax.rsqrt(jnp.mean(center * center, axis=1, keepdims=True) + 1e-05)
+        hat = center * rsd
+        e = grad * gain_ref[...]
+        back = rsd * (
+            e - jnp.mean(e, axis=1, keepdims=True) - hat * jnp.mean(e * hat, axis=1, keepdims=True)
+        )
+        result = res_ref[rows, :].astype(f32) + back
+        low = result.astype(bf16)
+        out_refs[0][rows, :] = low
+        if len(out_refs) > 1:
+            out_refs[1][rows, :] = result
+        fold = lambda v: jnp.sum(v.reshape(16, 8, d), axis=0)
+        return sums[0] + fold(grad * hat), sums[1] + fold(grad), sums[2] + fold(low.astype(f32))
+
+    zero = jnp.zeros((8, d), f32)
+    sums = lax.fori_loop(0, n // 128, chunk, (zero, zero, zero))
+    for k in range(3):
+        sums_ref[k : k + 1, :] = jnp.sum(sums[k], axis=0, keepdims=True)
+
+
+def norm_up_kernel(place_ref, *refs):
+    pieces, (g_ref, x_ref, gain_ref, res_ref, low_ref, wide_ref, sums_ref, acc_ref, w_ref, sems) = (
+        refs[:8],
+        refs[8:],
+    )
+    step = pl.program_id(0)
+
+    @pl.when(step == 0)
+    def _():
+        start_columns(place_ref, pieces, w_ref, sems, False)
+
+    for half in range(2):
+
+        @pl.when(step == 2 * half)
+        def _():
+            wait_columns(w_ref, sems, half)
+
+    @pl.when(step == 0)
+    def _():
+        acc_ref[...] = dotnt(g_ref[...], w_ref[0])
+
+    @pl.when(step > 0)
+    def _():
+        acc_ref[...] += dotnt(g_ref[...], w_ref[step])
+
+    @pl.when(step == 3)
+    def _():
+        norm_back(x_ref, gain_ref, res_ref, acc_ref, (low_ref, wide_ref), sums_ref)
+
+
+def norm_up_call(place, pieces, g, x, gain, residual):
+    n, d = x.shape
+    ff = g.shape[1]
+    whole = lambda s: spec(s, lambda i, *_: (0, 0))
+    return pl.pallas_call(
+        norm_up_kernel,
+        grid_spec=pltpu.PrefetchScalarGridSpec(
+            num_scalar_prefetch=1,
+            grid=(4,),
+            in_specs=PIECES
+            + [spec((n, 1024), lambda i, *_: (0, i)), whole((n, d)), whole((1, d)), whole((n, d))],
+            out_specs=[whole((n, d)), whole((n, d)), whole((8, d))],
+            scratch_shapes=[
+                pltpu.VMEM((n, d), f32),
+                pltpu.VMEM((4, d, 1024), bf16),
+                pltpu.SemaphoreType.DMA((2,)),
+            ],
+        ),
+        out_shape=[
+            jax.ShapeDtypeStruct((n, d), bf16),
+            jax.ShapeDtypeStruct((n, d), f32),
+            jax.ShapeDtypeStruct((8, d), f32),
+        ],
+        compiler_params=params(),
+        cost_estimate=pl.CostEstimate(
+            flops=2 * n * d * ff, bytes_accessed=2 * (8 * n * d + 2 * d * ff), transcendentals=0
+        ),
+        name="norm_up",
+    )(place, *pieces, g, x, gain.reshape(1, d), residual)
+
+
+def norm_qkv_kernel(*refs):
+    g_refs = refs[:3]
+    w_ref, x_ref, gain_ref, res_ref, start_ref, low_ref, sums_ref, acc_ref = refs[3:]
+    step = pl.program_id(0)
+    for i in range(3):
+
+        @pl.when(step == i)
+        def _(i=i):
+            before = start_ref[...] if i == 0 else acc_ref[...]
+            acc_ref[...] = before + dotnt(g_refs[i][...], w_ref[0])
+
+    @pl.when(step == 2)
+    def _():
+        norm_back(x_ref, gain_ref, res_ref, acc_ref, (low_ref,), sums_ref)
+
+
+def norm_qkv_call(grads, w, x, gain, residual, start):
+    n, d = x.shape
+    whole = lambda s: spec(s, lambda i: (0, 0))
+    return pl.pallas_call(
+        norm_qkv_kernel,
+        grid=(3,),
+        in_specs=[whole((n, 512))] * 3
+        + [spec((1, d, 512), lambda i: (i, 0, 1))]
+        + [whole((n, d)), whole((1, d)), whole((n, d)), whole((n, d))],
+        out_specs=[whole((n, d)), whole((8, d))],
+        out_shape=[jax.ShapeDtypeStruct((n, d), bf16), jax.ShapeDtypeStruct((8, d), f32)],
+        scratch_shapes=[pltpu.VMEM((n, d), f32)],
+        compiler_params=params(),
+        cost_estimate=pl.CostEstimate(
+            flops=2 * n * d * 1536, bytes_accessed=2 * (8 * n * d + d * 3072), transcendentals=0
+        ),
+        name="norm_qkv",
+    )(*grads, w, x, gain.reshape(1, d), residual, start)
+
+
+def part_kernel(*refs):
+    g_refs, w_ref, o_ref = refs[:-2], refs[-2], refs[-1]
+    step = pl.program_id(0)
+    for i, g_ref in enumerate(g_refs):
+
+        @pl.when(step == i)
+        def _(i=i, g_ref=g_ref):
+            value = dotnt(g_ref[...], w_ref[0])
+            o_ref[...] = value if i == 0 else o_ref[...] + value
+
+
+def part_call(grads, w):
+    n, kb = grads[0].shape
+    d = w.shape[1]
+    return pl.pallas_call(
+        part_kernel,
+        grid=(len(grads),),
+        in_specs=[spec((n, kb), lambda i: (0, 0))] * len(grads)
+        + [spec((1, d, kb), lambda i: (i, 0, 0))],
+        out_specs=spec((n, d), lambda i: (0, 0)),
+        out_shape=jax.ShapeDtypeStruct((n, d), f32),
+        compiler_params=params(),
+        cost_estimate=pl.CostEstimate(
+            flops=2 * n * d * kb * len(grads), bytes_accessed=4 * n * d * 4, transcendentals=0
+        ),
+        name="part",
+    )(*grads, w)
+
+
+def columns_kernel(plan, lefts, where_ref, *refs):
+    left_refs, right_refs = refs[:lefts], refs[lefts : lefts + len(plan)]
+    keep_ref, give_ref, at_ref, acc_ref = refs[-4:]
+    core = where_ref[2]
+    step = pl.program_id(0)
+    for i, left in enumerate(plan):
+
+        @pl.when(step == i)
+        def _(i=i, left=left):
+            if i == 0 or plan[i - 1] != left:
+                at_ref[...] = left_refs[left][...].T
+            acc = dot(at_ref[...], right_refs[i][...])
+            acc_ref[...] = acc.astype(bf16).reshape(acc_ref.shape)
+
+    keep_ref[...] = acc_ref[:, pl.ds(core, 1)].reshape(keep_ref.shape)
+    give_ref[...] = acc_ref[:, pl.ds(1 - core, 1)].reshape(give_ref.shape)
+
+
+def columns_call(where, lefts, rights, plan):
+    n, d = lefts[0].shape
+    wide = 512 * len(rights)
+    out = spec((8, 64, 512), lambda i, *_: (0, 0, i))
+    return pl.pallas_call(
+        functools.partial(columns_kernel, plan, len(lefts)),
+        grid_spec=pltpu.PrefetchScalarGridSpec(
+            num_scalar_prefetch=1,
+            grid=(len(plan),),
+            in_specs=[spec((n, d), lambda i, *_: (0, 0))] * len(lefts)
+            + [spec((n, 512), lambda i, *_, b=b: (0, b)) for _, b in rights],
+            out_specs=[out, out],
+            scratch_shapes=[pltpu.VMEM((d, n), bf16), pltpu.VMEM((8, 2, 64, 512), bf16)],
+        ),
+        out_shape=[jax.ShapeDtypeStruct((8, 64, wide), bf16)] * 2,
+        compiler_params=params(),
+        cost_estimate=pl.CostEstimate(
+            flops=2 * n * d * wide, bytes_accessed=2 * (2 * n * d + d * wide + n * wide), transcendentals=0
+        ),
+        name="columns",
+    )(where, *lefts, *[r for r, _ in rights])
+
+
 def permutation(move):
     pairs = []
     for z in range(4):
@@ -394,81 +911,33 @@
 OVER_Z = [permutation(lambda z, y, c, x, k=k: ((z + k) % 4, y, c, x)) for k in range(4)]
 
 
+Z_GROUPS = [
+    [flat_index(z, y, c, x) for z in range(4)] for y in range(2) for c in range(2) for x in range(2)
+]
+
+
 def send(array, pairs):
     return lax.ppermute(array, ALL, pairs)
 
 
-def gather_half(parts, first, second):
-    own = jnp.stack(parts)
-    own_core = send(own, OVER_C)
-    near = send(own, first)
-    near_core = send(near, OVER_C)
-    both = jnp.stack([own, near])
-    far = send(both, second)
-    far_core = send(far, OVER_C)
-    return both, far, own_core, near_core, far_core
-
-
-def gather_stage(shard):
-    parts = [shard] + [send(shard, OVER_Z[k]) for k in (1, 2, 3)]
-    return (
-        gather_half([p[0] for p in parts], OVER_X, OVER_Y),
-        gather_half([p[1] for p in parts], OVER_Y, OVER_X),
-    )
-
-
-def assemble_kernel(put, place_ref, *refs):
-    outs, sem = refs[10:-1], refs[-1]
-    z, y, c, x = (place_ref[i] for i in range(4))
-
-    def copies(go):
-        for half in range(2):
-            both, far, own_core, near_core, far_core = refs[5 * half : 5 * half + 5]
-            for zr in range(4):
-                za = (z + 4 - zr) % 4
-                for near in range(2):
-                    for turn in range(2):
-                        for core in range(2):
-                            if core == 0:
-                                src = (far if turn else both).at[near, zr]
-                            elif turn:
-                                src = far_core.at[near, zr]
-                            else:
-                                src = (near_core if near else own_core).at[zr]
-                            xr, yr = (near, turn) if half == 0 else (turn, near)
-                            d = flat_index(
-                                za, y + yr - 2 * y * yr, c + core - 2 * c * core, x + xr - 2 * x * xr
-                            )
-                            for b, dst in put(half, d, outs):
-                                go(pltpu.make_async_copy(src.at[b], dst, sem))
-
-    copies(lambda copy: copy.start())
-    copies(lambda copy: copy.wait())
-
-
-def put_blocks(half, d, outs):
-    return [(b, outs[2 * half + b].at[pl.ds(pl.multiple_of(d * 32, 32), 32), :]) for b in range(2)]
-
-
-def put_rows(half, d, outs):
-    return [(0, outs[0].at[pl.ds(pl.multiple_of(d * 128 + half * 64, 64), 64), :])]
-
-
-def assemble(place, halves, put, out_shape):
-    return pl.pallas_call(
-        functools.partial(assemble_kernel, put),
-        grid_spec=pltpu.PrefetchScalarGridSpec(
-            num_scalar_prefetch=1,
-            grid=(),
-            in_specs=[pl.BlockSpec(memory_space=pl.ANY)] * 10,
-            out_specs=[pl.BlockSpec(memory_space=pltpu.VMEM)] * len(out_shape),
-            scratch_shapes=[pltpu.SemaphoreType.DMA],
-        ),
-        out_shape=out_shape,
-        compiler_params=pltpu.CompilerParams(vmem_limit_bytes=32 * 2**20),
-        cost_estimate=pl.CostEstimate(flops=0, bytes_accessed=2 * 8 * 2**20, transcendentals=0),
-        name="assemble",
-    )(place, *halves[0], *halves[1])
+def tie(*trees):
+    return lax.optimization_barrier(trees)
+
+
+def gather_z(shard):
+    return [shard] + [send(shard, OVER_Z[k]) for k in (1, 2, 3)]
+
+
+def halves(parts):
+    return jnp.stack([p[0] for p in parts]), jnp.stack([p[1] for p in parts])
+
+
+def gather_z_line(shard):
+    return lax.all_gather(shard, ALL, axis=0, tiled=False, axis_index_groups=Z_GROUPS)
+
+
+def scatter_z_line(array):
+    return lax.psum_scatter(array, ALL, scatter_dimension=0, tiled=False, axis_index_groups=Z_GROUPS)
 
 
 def add_low(a, b):
@@ -479,34 +948,31 @@
     return lax.dynamic_index_in_dim(array, at, axis, keepdims=False)
 
 
-def reduce_half(grads, place, x_first):
-    z, y, c, x = place
-    g = add_low(take(grads, c, 2), send(take(grads, 1 - c, 2), OVER_C))
-    if x_first:
-        g = add_low(take(g, x, 2), send(take(g, 1 - x, 2), OVER_X))
-        g = add_low(take(g, y, 1), send(take(g, 1 - y, 1), OVER_Y))
-    else:
-        g = add_low(take(g, y, 1), send(take(g, 1 - y, 1), OVER_Y))
-        g = add_low(take(g, x, 1), send(take(g, 1 - x, 1), OVER_X))
-    total = take(g, z, 0).astype(f32)
-    for k in (1, 2, 3):
-        total = total + send(take(g, (z + k) % 4, 0), OVER_Z[k]).astype(f32)
-    return total
-
-
-def reduce_pair(left, right, place, x_first):
-    both = jnp.concatenate(
-        [left.reshape(4, 2, 2, 2, 32, 1024), right.reshape(4, 2, 2, 2, 32, 1024)], axis=4
-    )
-    total = reduce_half(both, place, x_first)
-    return total[:32], total[32:]
-
-
-def all_sum(v, place):
-    v = v + send(v, OVER_C)
-    v = v + send(v, OVER_X)
-    v = v + send(v, OVER_Y)
-    return v + send(v, OVER_Z[1]) + send(v, OVER_Z[2]) + send(v, OVER_Z[3])
+def fold(g, at, axis, pairs):
+    return take(g, at, axis), send(take(g, 1 - at, axis), pairs)
+
+
+def fold_second(a, b, place):
+    return fold(a, place[3], 2, OVER_X), fold(b, place[1], 1, OVER_Y)
+
+
+def fold_third(pair, place):
+    a, b = (add_low(*p) for p in pair)
+    return fold(a, place[1], 1, OVER_Y), fold(b, place[3], 1, OVER_X)
+
+
+def both(pair):
+    return jnp.stack([add_low(*p) for p in pair], axis=1)
+
+
+def fold_z(pair, place):
+    z = place[0]
+    g = both(pair)
+    return [take(g, z, 0)] + [send(take(g, (z + k) % 4, 0), OVER_Z[k]) for k in (1, 2, 3)]
+
+
+def total(parts):
+    return sum(p.astype(f32) for p in parts)
 
 
 def slope_table():
@@ -517,6 +983,12 @@
         pieces.append(low)
         rest = rest - low
     return slopes, np.stack(pieces, axis=1).reshape(-1)
+
+
+def moments(v):
+    mean = jnp.mean(v, axis=-1, keepdims=True)
+    center = v - mean
+    return center, lax.rsqrt(jnp.mean(center * center, axis=-1, keepdims=True) + 1e-05)
 
 
 def fast_shards(
@@ -545,93 +1017,180 @@
     def columns(w):
         return w.reshape(32, w.shape[1] // 1024, 1024).transpose(1, 0, 2)
 
-    shard_one = jnp.concatenate([columns(qkv_weight), dense_weight[None]]).reshape(2, 2, 32, 1024)
-    shard_two = columns(up_weight).reshape(2, 2, 32, 1024)
-    shard_three = down_weight.reshape(2, 1, 64, 1024)
-    square = [jax.ShapeDtypeStruct((1024, 1024), bf16)] * 4
-    w_q, w_k, w_v, w_dense = assemble(place_vec, gather_stage(shard_one), put_blocks, square)
-    w_up = assemble(place_vec, gather_stage(shard_two), put_blocks, square)
-    (w_down,) = assemble(
-        place_vec, gather_stage(shard_three), put_rows, [jax.ShapeDtypeStruct((4096, 1024), bf16)]
-    )
+    one = jnp.concatenate([columns(qkv_weight), dense_weight[None]]).reshape(2, 2, 32, 1024)
+    two = columns(up_weight).reshape(2, 2, 32, 1024)
+    three = down_weight.reshape(2, 1, 64, 1024)
 
     slot = dp * SG + seq
     my_seq = lax.dynamic_index_in_dim(slot_order, slot, 0, keepdims=False)
     every_seq = jnp.arange(seq_lengths.shape[0], dtype=jnp.int32)
     length = jnp.sum(jnp.where(every_seq == my_seq, seq_lengths, 0))
-    length_vec = length.reshape(1)
     valid = (jnp.arange(rows, dtype=jnp.int32) < length).astype(f32)
     slopes, slopes_split = slope_table()
-
-    inputs = tokens.astype(f32)
-    normed_one, norm_one_back = jax.vjp(layer_norm, inputs, ln1_gain, ln1_bias)
-    a1 = normed_one.astype(bf16)
-    query = (dot(a1, w_q) + qkv_bias[:width]).astype(bf16)
-    key = dot(a1, w_k).astype(bf16)
-    value = (dot(a1, w_v) + qkv_bias[width:]).astype(bf16)
-    context, lse = attn_fwd(length_vec, jnp.asarray(slopes), query, key, value)
-    hidden = inputs + dot(context, w_dense) + dense_bias
-    normed_two, norm_two_back = jax.vjp(layer_norm, hidden, ln2_gain, ln2_bias)
-    a2 = normed_two.astype(bf16)
-    blocks = range(4)
-    before = [dot(a2, w_up[i]) + up_bias[i * 1024 : (i + 1) * 1024] for i in blocks]
-    active, gelu_back = zip(*[jax.vjp(gelu_tanh, b) for b in before])
-    active = [a.astype(bf16) for a in active]
-    grad_out = cotangent.astype(f32) * valid[:, None]
-    grad_low = grad_out.astype(bf16)
-    grad_down_b = jnp.sum(grad_out, axis=0)
-
-    def outer(a, b):
-        return jnp.einsum("rd,rf->df", a, b, preferred_element_type=f32).astype(bf16)
-
-    grad_down_w = [outer(active[i], grad_low) for i in blocks]
-    mlp = sum(dot(active[i], w_down[i * 1024 : (i + 1) * 1024]) for i in blocks)
-    block_output = (hidden + mlp + down_bias).astype(bf16)
-    down_terms = jnp.concatenate(grad_down_w).reshape(4, 2, 2, 2, 2, 64, 1024)
-    owner_down = jnp.concatenate(
+    bias_full = jnp.concatenate([qkv_bias[:width], jnp.zeros((width,), f32), qkv_bias[width:]])
+
+    one_z = gather_z(one)
+    center, rsd = moments(tokens.astype(f32))
+    a1 = (center * rsd * ln1_gain + ln1_bias).astype(bf16)
+    grad_low = cotangent * valid[:, None].astype(bf16)
+    one_z, a1, grad_low, two = tie(one_z, a1, grad_low, two)
+
+    a, b = halves(one_z)
+    one_x, one_y = send(a, OVER_X), send(b, OVER_Y)
+    two_z = gather_z_line(two)
+    one_x, one_y = tie(one_x, one_y)
+
+    one_a, one_b = jnp.stack([a, one_x]), jnp.stack([b, one_y])
+    one_xy, one_yx = send(one_a, OVER_Y), send(one_b, OVER_X)
+    one_ca, one_cb = send(one_a, OVER_C), send(one_b, OVER_C)
+    one_xy, one_yx, one_ca, one_cb, two_z, three = tie(one_xy, one_yx, one_ca, one_cb, two_z, three)
+    one_cxy, one_cyx = send(one_xy, OVER_C), send(one_yx, OVER_C)
+    a, b = two_z[:, 0], two_z[:, 1]
+    one_cxy, one_cyx, a, b, three = tie(one_cxy, one_cyx, a, b, three)
+
+    two_x, two_y = send(a, OVER_X), send(b, OVER_Y)
+    three_z = gather_z_line(three)
+    pieces = (one_a, one_xy, one_ca, one_cxy, one_b, one_yx, one_cb, one_cyx)
+    qkv, w_one = qkv_call(place_vec, pieces, a1, bias_full)
+    qkv, two_x, two_y = tie(qkv, two_x, two_y)
+
+    two_a, two_b = jnp.stack([a, two_x]), jnp.stack([b, two_y])
+    two_xy, two_yx = send(two_a, OVER_Y), send(two_b, OVER_X)
+    two_ca, two_cb = send(two_a, OVER_C), send(two_b, OVER_C)
+    context, lse = attn_fwd(length, jnp.asarray(slopes), qkv, 0, 8)
+    context, two_xy, two_yx, two_ca, two_cb, three_z = tie(
+        context, two_xy, two_yx, two_ca, two_cb, three_z
+    )
+
+    two_cxy, two_cyx = send(two_xy, OVER_C), send(two_yx, OVER_C)
+    a, b = three_z[:, 0], three_z[:, 1]
+    three_x, three_y = send(a, OVER_X), send(b, OVER_Y)
+    hidden = tokens.astype(f32) + dot(context, w_one[3]) + dense_bias
+    center, rsd = moments(hidden)
+    a2 = (center * rsd * ln2_gain + ln2_bias).astype(bf16)
+    a2, hidden, two_cxy, two_cyx, three_x, three_y = tie(
+        a2, hidden, two_cxy, two_cyx, three_x, three_y
+    )
+
+    up_pieces = (two_a, two_xy, two_ca, two_cxy, two_b, two_yx, two_cb, two_cyx)
+    three_a, three_b = jnp.stack([a, three_x]), jnp.stack([b, three_y])
+    three_xy, three_yx = send(three_a, OVER_Y), send(three_b, OVER_X)
+    three_ca, three_cb = send(three_a, OVER_C), send(three_b, OVER_C)
+    active, slope = up_call(place_vec, up_pieces, a2, up_bias)
+    active, slope, grad_low = tie(active, slope, grad_low)
+
+    down_keep, down_give = down_grad_call(place_vec, active, grad_low)
+    down_keep, down_give, three_xy, three_yx, three_ca, three_cb, grad_low = tie(
+        down_keep, down_give, three_xy, three_yx, three_ca, three_cb, grad_low
+    )
+    three_cxy, three_cyx = send(three_xy, OVER_C), send(three_yx, OVER_C)
+    down_b = jnp.sum(grad_low.astype(f32), axis=0)
+    active, hidden, down_give, three_cxy, three_cyx, down_b = tie(
+        active, hidden, down_give, three_cxy, three_cyx, down_b
+    )
+
+    down_pieces = (
+        three_a, three_xy, three_ca, three_cxy, three_b, three_yx, three_cb, three_cyx
+    )
+    down_got = send(down_give, OVER_C)
+    block_output = down_call(place_vec, down_pieces, active, hidden, down_bias)
+    block_output, down_got, grad_low = tie(block_output, down_got, grad_low)
+
+    down = add_low(down_keep, down_got).reshape(4, 2, 2, 2, 64, 1024)
+    down = fold_second(down[:, :, :, 0], down[:, :, :, 1], place)
+    grad_before, up_b = gate_call(place_vec, down_pieces, grad_low, slope)
+    grad_before, a2 = tie(grad_before, a2)
+    up_keep, up_give = up_grad_call(place_vec, a2, grad_before)
+    grad_before, up_keep, up_give, down = tie(grad_before, up_keep, up_give, down)
+
+    down = fold_third(down, place)
+    up_got = send(up_give, OVER_C)
+    grad_low_hidden, grad_hidden, sums = norm_up_call(
+        place_vec, up_pieces, grad_before, hidden, ln2_gain, grad_low
+    )
+    grad_low_hidden, grad_hidden, sums, down, up_got = tie(
+        grad_low_hidden, grad_hidden, sums, down, up_got
+    )
+
+    owner_down = scatter_z_line(both(down))
+    early = jnp.concatenate([sums[2], sums[0], sums[1], up_b.reshape(4096), down_b]).reshape(8, 1024)
+    early = lax.all_gather(early, ALL, axis=0, tiled=False)
+    up = add_low(up_keep, up_got).reshape(4, 2, 2, 32, 4096)
+    up = fold_second(up[..., :2048], up[..., 2048:], place)
+    grad_context = dotnt(grad_low_hidden, w_one[3]).astype(bf16)
+    q0, k0, v0 = attn_bwd(length, jnp.asarray(slopes_split), qkv, context, lse, grad_context, 0, 4)
+    qkv, q0, k0, v0, up, a1 = tie(qkv, q0, k0, v0, up, a1)
+
+    up = fold_third(up, place)
+    third_keep, third_give = columns_call(
+        place_vec,
+        [context, a1],
+        [(grad_low_hidden, 0), (grad_low_hidden, 1), (q0, 0), (k0, 0), (v0, 0)],
+        (0, 0, 1, 1, 1),
+    )
+    third_keep, third_give, qkv = tie(third_keep, third_give, qkv)
+
+    third_got = send(third_give, OVER_C)
+    q1, k1, v1 = attn_bwd(length, jnp.asarray(slopes_split), qkv, context, lse, grad_context, 4, 4)
+    q1, k1, v1, third_got, up = tie(q1, k1, v1, third_got, up)
+
+    owner_up = scatter_z_line(both(up))
+    third = add_low(third_keep, third_got).reshape(4, 2, 2, 32, 2560)
+    third = fold_second(third[..., :1280], third[..., 1280:], place)
+    last_keep, last_give = columns_call(place_vec, [a1], [(q1, 0), (k1, 0), (v1, 0)], (0, 0, 0))
+    last_keep, last_give, q0, q1, k1, v1 = tie(last_keep, last_give, q0, q1, k1, v1)
+
+    last_got = send(last_give, OVER_C)
+    part = part_call([q0, k0, v0], w_one)
+    part, last_got, third = tie(part, last_got, third)
+    third = fold_third(third, place)
+    last = add_low(last_keep, last_got).reshape(4, 2, 2, 32, 1536)
+    last = fold_second(last[..., :768], last[..., 768:], place)
+    qkv_b = [jnp.sum(g.astype(f32), axis=0) for g in (q0, q1, v0, v1)]
+    token_grad, sums = norm_qkv_call([q1, k1, v1], w_one, tokens, ln1_gain, grad_hidden, part)
+    token_grad, sums, last, third = tie(token_grad, sums, last, third)
+
+    last = fold_third(last, place)
+    third = fold_z(third, place)
+    late = jnp.concatenate(qkv_b + [sums[0], sums[1]]).reshape(4, 1024)
+    late_c = send(late, OVER_C)
+    last, third, late, late_c = tie(last, third, late, late_c)
+
+    last = fold_z(last, place)
+    late = late + late_c
+    late_x = send(late, OVER_X)
+    third = total(third)
+    third = jnp.concatenate([third[0], third[1]], axis=1)
+    last, late, late_x, third, owner_up, owner_down, early = tie(
+        last, late, late_x, third, owner_up, owner_down, early
+    )
+    late = late + late_x
+    late_y = send(late, OVER_Y)
+    early = jnp.sum(early, axis=0)
+    owner_down = owner_down.astype(f32).reshape(128, 1024)
+    owner_up = owner_up.astype(f32)
+    owner_up = jnp.concatenate([owner_up[0], owner_up[1]], axis=1)
+    late, late_y = tie(late, late_y)
+    late = late + late_y
+    late = late + send(late, OVER_Z[1]) + send(late, OVER_Z[2]) + send(late, OVER_Z[3])
+    last = total(last)
+    last = jnp.concatenate([last[0], last[1]], axis=1)
+    owner_qkv = jnp.concatenate(
         [
-            reduce_half(down_terms[:, :, :, :, 0], place, True),
-            reduce_half(down_terms[:, :, :, :, 1], place, False),
-        ]
-    )
-    grad_active = [dotnt(grad_low, w_down[i * 1024 : (i + 1) * 1024]) for i in blocks]
-    grad_before = [gelu_back[i](grad_active[i])[0].astype(bf16) for i in blocks]
-    grad_up_w = [outer(a2, grad_before[i]) for i in blocks]
-    up_01 = reduce_pair(grad_up_w[0], grad_up_w[1], place, True)
-    up_23 = reduce_pair(grad_up_w[2], grad_up_w[3], place, False)
-    owner_up = jnp.concatenate(up_01 + up_23, axis=1)
-    grad_up_b = jnp.concatenate([jnp.sum(g.astype(f32), axis=0) for g in grad_before])
-    grad_normed_two = sum(dotnt(grad_before[i], w_up[i]) for i in blocks)
-    grad_hidden_norm, grad_gain_two, grad_shift_two = norm_two_back(grad_normed_two)
-    grad_hidden = grad_out + grad_hidden_norm
-    grad_hidden_low = grad_hidden.astype(bf16)
-    grad_dense_w = outer(context, grad_hidden_low)
-    grad_dense_b = jnp.sum(grad_hidden_low.astype(f32), axis=0)
-    grad_context = dotnt(grad_hidden_low, w_dense).astype(bf16)
-    early = all_sum(
-        jnp.concatenate(
-            [grad_dense_b, grad_gain_two, grad_shift_two, grad_up_b, grad_down_b]
-        ).reshape(8, 1024),
-        place,
-    )
-    grad_q, grad_k, grad_v = attn_bwd(
-        length_vec, jnp.asarray(slopes_split), query, key, value, context, lse, grad_context
-    )
-    owner_q, owner_k = reduce_pair(outer(a1, grad_q), outer(a1, grad_k), place, True)
-    owner_v, owner_dense = reduce_pair(outer(a1, grad_v), grad_dense_w, place, False)
-    grad_qkv_b = [jnp.sum(g.astype(f32), axis=0) for g in (grad_q, grad_v)]
-    grad_normed_one = dotnt(grad_q, w_q) + dotnt(grad_k, w_k) + dotnt(grad_v, w_v)
-    grad_input_norm, grad_gain_one, grad_shift_one = norm_one_back(grad_normed_one)
-    token_grad = (grad_hidden + grad_input_norm).astype(bf16)
-    late = all_sum(jnp.stack(grad_qkv_b + [grad_gain_one, grad_shift_one]), place)
+            part
+            for i in range(3)
+            for part in (third[:, 1024 + 512 * i : 1536 + 512 * i], last[:, 512 * i : 512 * i + 512])
+        ],
+        axis=1,
+    )
     return (
         block_output,
         token_grad,
         late[2],
         late[3],
-        jnp.concatenate([owner_q, owner_k, owner_v], axis=1),
+        owner_qkv,
         late[:2].reshape(2 * width),
-        owner_dense,
+        third[:, :1024],
         early[0],
         early[1],
         early[2],

time: 659 us -> 488 us (0.74)
  matrix products: 164 us -> 10.1 us
  Pallas kernels: 100 us -> 235 us
  waiting for transfers between devices: 184 us -> 76.1 us
  starting transfers between devices: 110 us -> 62.9 us
  between operations: 2.71 us -> 15.5 us
  local copies, waits for them, and re-layouts: 46.2 us -> 35.9 us
    pallas_call x3 -> x11, Pallas kernels: 35.1 us -> 170 us  [the longest x1 23.4 us: up_call(): pl.pallas_call(up_kernel, grid_spec=pltpu.PrefetchScalarGridSpec(num_scal...]
    ppermute x87 -> x59, waiting for transfers between devices: 184 us -> 76 us  [send(): return lax.ppermute(array, ALL, pairs)]
    dot_general x12 -> x1, matrix products: 64.4 us -> 5.99 us  [dotnt(): return lax.dot_general(a, b, NT, preferred_element_type=f32)]
    dot_general x12 -> x1, matrix products: 55.8 us -> 4.13 us  [dot(): return jnp.dot(a, b, preferred_element_type=f32)]
    ppermute x87 -> x59, starting transfers between devices: 110 us -> 62.5 us  [send(): return lax.ppermute(array, ALL, pairs)]
    dot_general x12 -> x0, matrix products: 43.4 us -> none  [outer(): jnp.einsum('rd,rf->df', a, b, preferred_element_type=f32).astype(bf16)]
    unnamed x223 -> x145, local copies, waits for them, and re-layouts: 27.3 us -> 12.5 us
    squeeze x18 -> x16, local copies, waits for them, and re-layouts: 0.96 us -> 11.4 us  [take(): return lax.dynamic_index_in_dim(array, at, axis, keepdims=False)]
  transfers between devices with their start and end apart: 87 -> 64, of which waited for: 28 -> 18; matrix products, arithmetic and copies ran while one was open for 17% -> 14% of each run, Pallas kernels for 7% -> 49%
where the time goes in v2:
time: 488 us; the launch traced here: 482 us
  Pallas kernels  235 us (48%)
  waiting for transfers between devices  76.1 us (16%)
  starting transfers between devices  62.9 us (13%)
  other arithmetic  46.6 us (10%)
  local copies, waits for them, and re-layouts  35.9 us (7%)
  between operations  15.5 us (3%)
  matrix products  10.1 us (2%)
    ppermute x59, waiting for transfers between devices, send(): return lax.ppermute(array, ALL, pairs)  76 us
    ppermute x59, starting transfers between devices, send(): return lax.ppermute(array, ALL, pairs)  62.5 us
    pallas_call x2, Pallas kernels, attn_bwd(): pl.pallas_call(attn_bwd_kernel, grid_spec=pltpu.PrefetchScalarGridSpec(nu...  40.2 us
    pallas_call x1, Pallas kernels, attn_fwd(): pl.pallas_call(attn_fwd_kernel, grid_spec=pltpu.PrefetchScalarGridSpec(nu...  24.8 us
    pallas_call x1, Pallas kernels, up_call(): pl.pallas_call(up_kernel, grid_spec=pltpu.PrefetchScalarGridSpec(num_scal...  23.4 us
    pallas_call x1, Pallas kernels, norm_up_call(): pl.pallas_call(norm_up_kernel, grid_spec=pltpu.PrefetchScalarGridSpec(num...  22.7 us
    pallas_call x2, Pallas kernels, columns_call(): pl.pallas_call(functools.partial(columns_kernel, plan, len(lefts)), grid_...  21.2 us
    convert_element_type x12, other arithmetic, add_low(): return (a.astype(f32) + b.astype(f32)).astype(bf16)  20.1 us
  transfers between devices with their start and end apart: 64, of which 18 were waited for; matrix products, arithmetic and copies ran while one was open for 14% of the time, Pallas kernels for 49%

profile of v2, /device:TPU:0, one launch (start us, length us, event | category | flops | bytes accessed | tf_op | source)
XLA Modules:
  0.0 482.2 jit_solution(18433633871909704683)
XLA Ops:
  10.0 3.1 collective-permute-start
  13.0 2.6 collective-permute-start.1
  26.7 6.1 %collective-permute-done.1 = bf16[2,2,32,1024]{3,2,1,0:T(8,128)(2,1)S(1)} collective-permute-done((bf16[2,2,32,1024]{3,2,1,0:T(8,128)(2,1)S(1)}, bf16[2,2,32,1024]{3,2,1,0:T(8,128)(2,1)S(1)}, u32[]{:S(2)}, u32[]{:S(2)}) %collective-permute-start.1) | collective-permute-done | bytes 262176 | tf_op jit(solution)/shard_map/ppermute | solution.py:920
  36.3 10.5 %collective-permute-done.3 = bf16[4,2,32,1024]{3,2,1,0:T(8,128)(2,1)S(1)} collective-permute-done((bf16[4,2,32,1024]{3,2,1,0:T(8,128)(2,1)S(1)}, bf16[4,2,32,1024]{3,2,1,0:T(8,128)(2,1)S(1)}, u32[]{:S(2)}, u32[]{:S(2)}) %collective-permute-start.3) | collective-permute-done | bytes 524320 | tf_op jit(solution)/shard_map/ppermute | solution.py:920
  52.9 20.0 %collective-permute-done.5.refs_1_ = bf16[2,4,2,32,1024]{4,3,2,1,0:T(8,128)(2,1)S(1)} collective-permute-done((bf16[2,4,2,32,1024]{4,3,2,1,0:T(8,128)(2,1)S(1)}, bf16[2,4,2,32,1024]{4,3,2,1,0:T(8,128)(2,1)S(1)}, u32[]{:S(2)}, u32[]{:S(2)}) %collective-permute-start.5) | collective-permute-done | bytes 1048608 | tf_op jit(solution)/shard_map/ppermute | solution.py:920
  72.9 2.6 collective-permute-done.6.refs_5_
  81.5 14.4 %qkv.1 = (bf16[1024,3072]{1,0:T(8,128)(2,1)}, bf16[4,1024,1024]{2,1,0:T(8,128)(2,1)}) custom-call(s32[4]{0:T(128)} %pad_add_fusion.place_ref.where_ref, bf16[2,4,2,32,1024]{4,3,2,1,0:T(8,128)(2,1)} %copy-done.31, bf16[2,4,2,32,1024]{4,3,2,1,0:T(8,128)(2,1)} %copy-done.57, bf16[2,4,2,32,1024]{4,3,2,1,0:T(8,128)(2,1)} %copy-done.58, ...), custom_call_target="tpu_custom_call" | custom-call | flops 6442450944 | bytes 25165824 | tf_op jit(solution)/shard_map/qkv/pallas_call | solution.py:465
  102.3 24.8 %attn_fwd.1 = (bf16[1024,1024]{1,0:T(8,128)(2,1)S(1)}, f32[1024,1024]{1,0:T(8,128)}) custom-call(s32[2]{0:T(128)S(1)} %get-tuple-element.425.len_ref, f32[16]{0:T(128)S(1)} %copy-done.11, bf16[1024,3072]{1,0:T(8,128)(2,1)} %get-tuple-element.264.q_ref.k_ref.v_ref, bf16[1024,3072]{1,0:T(8,128)(2,1)} %get-tuple-element.264.q_ref.k_ref.v_ref, ...), custom_call_target="tpu_custom_call" | custom-call | flops 10737418240 | bytes 12582912 | tf_op jit(solution)/shard_map/attn_fwd/pallas_call | solution.py:66
  132.7 4.1 fusion.59
  139.8 5.9 %collective-permute-done.19 = bf16[4,1,64,1024]{3,2,0,1:T(8,128)(2,1)S(1)} collective-permute-done((bf16[4,1,64,1024]{3,2,0,1:T(8,128)(2,1)S(1)}, bf16[4,1,64,1024]{3,2,0,1:T(8,128)(2,1)S(1)}, u32[]{:S(2)}, u32[]{:S(2)}) %collective-permute-start.19) | collective-permute-done | bytes 524320 | tf_op jit(solution)/shard_map/ppermute | solution.py:920
  148.6 23.4 %up.1 = (bf16[1024,4096]{1,0:T(8,128)(2,1)}, bf16[1024,4096]{1,0:T(8,128)(2,1)}) custom-call(s32[4]{0:T(128)} %pad_add_fusion.place_ref.where_ref, bf16[2,4,2,32,1024]{4,3,2,1,0:T(8,128)(2,1)} %copy-done.29, bf16[2,4,2,32,1024]{4,3,2,1,0:T(8,128)(2,1)} %copy-done.52, bf16[2,4,2,32,1024]{4,3,2,1,0:T(8,128)(2,1)} %copy-done.53, ...), custom_call_target="tpu_custom_call" | custom-call | flops 8589934592 | bytes 27262976 | tf_op jit(solution)/shard_map/up/pallas_call | solution.py:525
  172.1 15.6 %down_grad.1 = (bf16[8,256,1024]{2,1,0:T(8,128)(2,1)}, bf16[8,256,1024]{2,1,0:T(8,128)(2,1)}) custom-call(s32[4]{0:T(128)} %pad_add_fusion.place_ref.where_ref, bf16[1024,4096]{1,0:T(8,128)(2,1)} %get-tuple-element.228.a_ref.refs_8_, bf16[1024,1024]{1,0:T(8,128)(2,1)} %broadcast_multiply_fusion.g_ref.refs_8_.refs_11_), custom_call_target="tpu_custom_call" | custom-call | flops 8589934592 | bytes 18874368 | tf_op jit(solution)/shard_map/down_grad/pallas_call | solution.py:566
  192.6 17.1 %down.1 = bf16[1024,1024]{1,0:T(8,128)(2,1)} custom-call(s32[4]{0:T(128)} %pad_add_fusion.place_ref.where_ref, bf16[2,4,1,64,1024]{4,3,2,1,0:T(8,128)(2,1)} %copy-done.33, bf16[2,4,1,64,1024]{4,3,2,1,0:T(8,128)(2,1)} %copy-done.59, bf16[2,4,1,64,1024]{4,3,2,1,0:T(8,128)(2,1)} %collective-permute-done.23.refs_2_, bf16[2,4,1,64,1024]{4,3,2,1,0:T(8,128)(2,1)} %copy-done.60, ...), custom_call_target="tpu_custom_call" | custom-call | flops 8589934592 | bytes 23068672 | tf_op jit(solution)/shard_map/down/pallas_call | solution.py:637
  209.7 4.3 add_convert_fusion.1
  218.0 16.4 %gate.1 = (bf16[1024,4096]{1,0:T(8,128)(2,1)}, f32[1,4096]{1,0:T(1,128)}) custom-call(s32[4]{0:T(128)} %pad_add_fusion.place_ref.where_ref, bf16[2,4,1,64,1024]{4,3,2,1,0:T(8,128)(2,1)} %copy-done.33, bf16[2,4,1,64,1024]{4,3,2,1,0:T(8,128)(2,1)} %copy-done.59, bf16[2,4,1,64,1024]{4,3,2,1,0:T(8,128)(2,1)} %collective-permute-done.23.refs_2_, ...), custom_call_target="tpu_custom_call" | custom-call | flops 8589934592 | bytes 27262976 | tf_op jit(solution)/shard_map/gate/pallas_call | solution.py:684
  234.4 16.2 %up_grad.1 = (bf16[8,64,4096]{2,1,0:T(8,128)(2,1)}, bf16[8,64,4096]{2,1,0:T(8,128)(2,1)}) custom-call(s32[4]{0:T(128)} %pad_add_fusion.place_ref.where_ref, bf16[1024,1024]{1,0:T(8,128)(2,1)} %add_convert_fusion.3.refs_8_.a_ref, bf16[1024,4096]{1,0:T(8,128)(2,1)} %get-tuple-element.242.g_ref.refs_8_), custom_call_target="tpu_custom_call" | custom-call | flops 8589934592 | bytes 18874368 | tf_op jit(solution)/shard_map/up_grad/pallas_call | solution.py:588
  258.2 22.7 %norm_up.1 = (bf16[1024,1024]{1,0:T(8,128)(2,1)}, f32[1024,1024]{1,0:T(8,128)}, f32[8,1024]{1,0:T(8,128)}) custom-call(s32[4]{0:T(128)} %pad_add_fusion.place_ref.where_ref, bf16[2,4,2,32,1024]{4,3,2,1,0:T(8,128)(2,1)} %copy-done.29, bf16[2,4,2,32,1024]{4,3,2,1,0:T(8,128)(2,1)} %copy-done.52, bf16[2,4,2,32,1024]{4,3,2,1,0:T(8,128)(2,1)} %copy-done.53, ...), custom_call_target="tpu_custom_call" | custom-call | flops 8589934592 | bytes 33554432 | tf_op jit(solution)/shard_map/norm_up/pallas_call | solution.py:765
  282.6 5.0 %add_convert_fusion = bf16[8,64,4096]{2,1,0:T(8,128)(2,1)S(1)} fusion(bf16[8,64,4096]{2,1,0:T(8,128)(2,1)} %collective-permute-done.32, bf16[8,64,4096]{2,1,0:T(8,128)(2,1)} %get-tuple-element.255), kind=kLoop, calls=%fused_computation | loop fusion | flops 8388608 | bytes 12582912 | tf_op jit(solution)/shard_map/convert_element_type | solution.py:944
  296.4 6.0 %fusion.11.do_ref = bf16[1024,1024]{1,0:T(8,128)(2,1)} fusion(bf16[1024,1024]{1,0:T(8,128)(2,1)} %get-tuple-element.251.refs_2_.refs_3_, bf16[4,1024,1024]{2,1,0:T(8,128)(2,1)} %get-tuple-element.202.refs_3_), kind=kOutput, calls=%fused_computation.29 | convolution fusion | flops 2148532224 | bytes 6291456 | tf_op jit(solution)/shard_map/dot_general | solution.py:27
  302.5 20.1 %attn_bwd.2 = (bf16[1024,512]{1,0:T(8,128)(2,1)S(1)}, bf16[1024,512]{1,0:T(8,128)(2,1)S(1)}, bf16[1024,512]{1,0:T(8,128)(2,1)S(1)}) custom-call(s32[2]{0:T(128)S(1)} %get-tuple-element.425.len_ref, f32[48]{0:T(128)S(1)} %copy-done.10, bf16[1024,3072]{1,0:T(8,128)(2,1)} %get-tuple-element.264.q_ref.k_ref.v_ref, ...), custom_call_target="tpu_custom_call" | custom-call | flops 13421772800 | bytes 10485760 | tf_op jit(solution)/shard_map/attn_bwd/pallas_call | solution.py:135
  325.5 12.4 %columns.2 = (bf16[8,64,2560]{2,1,0:T(8,128)(2,1)}, bf16[8,64,2560]{2,1,0:T(8,128)(2,1)}) custom-call(s32[4]{0:T(128)} %pad_add_fusion.place_ref.where_ref, bf16[1024,1024]{1,0:T(8,128)(2,1)} %copy-done.12, bf16[1024,1024]{1,0:T(8,128)(2,1)} %fusion.5.refs_8_.refs_1_.refs_0_, bf16[1024,1024]{1,0:T(8,128)(2,1)} %get-tuple-element.251.refs_2_.refs_3_, ...), custom_call_target="tpu_custom_call" | custom-call | flops 5368709120 | bytes 14680064 | tf_op jit(solution)/shard_map/columns/pallas_call | solution.py:879
  344.5 20.1 %attn_bwd.3 = (bf16[1024,512]{1,0:T(8,128)(2,1)S(1)}, bf16[1024,512]{1,0:T(8,128)(2,1)S(1)}, bf16[1024,512]{1,0:T(8,128)(2,1)S(1)}) custom-call(s32[2]{0:T(128)S(1)} %get-tuple-element.426.len_ref, f32[48]{0:T(128)S(1)} %copy-done.10, bf16[1024,3072]{1,0:T(8,128)(2,1)} %get-tuple-element.264.q_ref.k_ref.v_ref, ...), custom_call_target="tpu_custom_call" | custom-call | flops 13421772800 | bytes 10485760 | tf_op jit(solution)/shard_map/attn_bwd/pallas_call | solution.py:135
  369.6 8.8 %columns.3 = (bf16[8,64,1536]{2,1,0:T(8,128)(2,1)}, bf16[8,64,1536]{2,1,0:T(8,128)(2,1)}) custom-call(s32[4]{0:T(128)} %pad_add_fusion.place_ref.where_ref, bf16[1024,1024]{1,0:T(8,128)(2,1)} %fusion.5.refs_8_.refs_1_.refs_0_, bf16[1024,512]{1,0:T(8,128)(2,1)} %copy-done, bf16[1024,512]{1,0:T(8,128)(2,1)} %copy-done.8, bf16[1024,512]{1,0:T(8,128)(2,1)} %copy-done.2), custom_call_target="tpu_custom_call" | custom-call | flops 3221225472 | bytes 10485760 | tf_op jit(solution)/shard_map/columns/pallas_call | solution.py:879
  385.0 8.5 %part.1.refs_7_ = f32[1024,1024]{1,0:T(8,128)} custom-call(bf16[1024,512]{1,0:T(8,128)(2,1)} %copy-done.4, bf16[1024,512]{1,0:T(8,128)(2,1)} %copy-done.9, bf16[1024,512]{1,0:T(8,128)(2,1)} %copy-done.6, bf16[4,1024,1024]{2,1,0:T(8,128)(2,1)} %get-tuple-element.202.refs_3_), custom_call_target="tpu_custom_call" | custom-call | flops 3221225472 | bytes 16777216 | tf_op jit(solution)/shard_map/part/pallas_call | solution.py:842
  393.6 4.0 collective-permute-done.39
  407.7 14.6 %norm_qkv.1 = (bf16[1024,1024]{1,0:T(8,128)(2,1)}, f32[8,1024]{1,0:T(8,128)}) custom-call(bf16[1024,512]{1,0:T(8,128)(2,1)} %copy-done, bf16[1024,512]{1,0:T(8,128)(2,1)} %copy-done.8, bf16[1024,512]{1,0:T(8,128)(2,1)} %copy-done.2, bf16[4,1024,1024]{2,1,0:T(8,128)(2,1)} %get-tuple-element.202.refs_3_, bf16[1024,1024]{1,0:T(8,128)(2,1)} %refs_4_.1, ...), custom_call_target="tpu_custom_call" | custom-call | flops 3221225472 | bytes 23068672 | tf_op jit(solution)/shard_map/norm_qkv/pallas_call | solution.py:811
  428.7 6.2 %collective-permute-start.47 = (bf16[2,32,1280]{2,1,0:T(8,128)(2,1)S(1)}, bf16[2,32,1280]{2,1,0:T(8,128)(2,1)S(1)}, u32[]{:S(2)}, u32[]{:S(2)}) collective-permute-start(bf16[2,32,1280]{2,1,0:T(8,128)(2,1)S(1)} %get-tuple-element.378), channel_id=1, source_target_pairs={{0,8},{1,9},{2,10},{3,11},{4,12},{5,13},{6,14},{7,15},{8,16},{9,17... | collective-permute-start | bytes 491528 | tf_op jit(solution)/shard_map/ppermute | solution.py:920
  437.4 4.4 collective-permute-done.47
  441.8 6.3 %collective-permute-done.48 = bf16[2,32,1280]{2,1,0:T(8,128)(2,1)S(1)} collective-permute-done((bf16[2,32,1280]{2,1,0:T(8,128)(2,1)S(1)}, bf16[2,32,1280]{2,1,0:T(8,128)(2,1)S(1)}, u32[]{:S(2)}, u32[]{:S(2)}) %collective-permute-start.48) | collective-permute-done | bytes 163872 | tf_op jit(solution)/shard_map/ppermute | solution.py:920
  448.3 4.1 collective-permute-start.51
  464.6 3.5 collective-permute-start.58
  470.0 2.7 collective-permute-done.57
  (372 shorter events, 130.3 us)
Async XLA Ops:
  7.2 68.3 %all-gather.8.cloned.1.call-start = ((), (), s32[]{:S(2)}) async-start(), calls=%async_computation.5 | async-start | bytes 1310720 | tf_op jit(solution)/shard_map/all_gather | solution.py:936
  13.0 19.7 %collective-permute-start.1 = (bf16[2,2,32,1024]{3,2,1,0:T(8,128)(2,1)S(1)}, bf16[2,2,32,1024]{3,2,1,0:T(8,128)(2,1)S(1)}, u32[]{:S(2)}, u32[]{:S(2)}) collective-permute-start(bf16[2,2,32,1024]{3,2,1,0:T(8,128)(2,1)S(1)} %bitcast.223), channel_id=1, source_target_pairs={{0,16},{1,17},{2,18},{3,19},{4,20},{5,21},{6,22},{7,23},{8,24},{9,... | collective-permute-start | bytes 786440 | tf_op jit(solution)/shard_map/ppermute | solution.py:920
  36.2 93.2 %all-gather.10.cloned.1.call-start = ((), (), s32[]{:S(2)}) async-start(), calls=%async_computation.6 | async-start | bytes 1310720 | tf_op jit(solution)/shard_map/all_gather | solution.py:936
  49.0 23.9 %collective-permute-start.5 = (bf16[2,4,2,32,1024]{4,3,2,1,0:T(8,128)(2,1)S(1)}, bf16[2,4,2,32,1024]{4,3,2,1,0:T(8,128)(2,1)S(1)}, u32[]{:S(2)}, u32[]{:S(2)}) collective-permute-start(bf16[2,4,2,32,1024]{4,3,2,1,0:T(8,128)(2,1)S(1)} %pad_maximum_fusion.refs_0_), channel_id=1, source_target_pairs={{0,4},{1,5},{2,6},{3,7},{4,0},{5,1},{6,2},{7,3},{8,12},{9,13},{10,... | collective-permute-start | bytes 3145736 | tf_op jit(solution)/shard_map/ppermute | solution.py:920
  51.8 23.7 %collective-permute-start.6 = (bf16[2,4,2,32,1024]{4,3,2,1,0:T(8,128)(2,1)S(1)}, bf16[2,4,2,32,1024]{4,3,2,1,0:T(8,128)(2,1)}, u32[]{:S(2)}, u32[]{:S(2)}) collective-permute-start(bf16[2,4,2,32,1024]{4,3,2,1,0:T(8,128)(2,1)S(1)} %pad_maximum_fusion.1.refs_4_), channel_id=1, source_target_pairs={{0,1},{1,0},{2,3},{3,2},{4,5},{5,4},{6,7},{7,6},{8,9},{9,8},{10,11... | collective-permute-start | bytes 3145736 | tf_op jit(solution)/shard_map/ppermute | solution.py:920
  52.4 23.1 %collective-permute-start.7 = (bf16[2,4,2,32,1024]{4,3,2,1,0:T(8,128)(2,1)S(1)}, bf16[2,4,2,32,1024]{4,3,2,1,0:T(8,128)(2,1)S(1)}, u32[]{:S(2)}, u32[]{:S(2)}) collective-permute-start(bf16[2,4,2,32,1024]{4,3,2,1,0:T(8,128)(2,1)S(1)} %pad_maximum_fusion.refs_0_), channel_id=1, source_target_pairs={{0,2},{1,3},{2,0},{3,1},{4,6},{5,7},{6,4},{7,5},{8,10},{9,11},{10,... | collective-permute-start | bytes 3145736 | tf_op jit(solution)/shard_map/ppermute | solution.py:920
  52.4 23.1 %collective-permute-start.8 = (bf16[2,4,2,32,1024]{4,3,2,1,0:T(8,128)(2,1)S(1)}, bf16[2,4,2,32,1024]{4,3,2,1,0:T(8,128)(2,1)}, u32[]{:S(2)}, u32[]{:S(2)}) collective-permute-start(bf16[2,4,2,32,1024]{4,3,2,1,0:T(8,128)(2,1)S(1)} %pad_maximum_fusion.1.refs_4_), channel_id=1, source_target_pairs={{0,2},{1,3},{2,0},{3,1},{4,6},{5,7},{6,4},{7,5},{8,10},{9,11},{10,... | collective-permute-start | bytes 3145736 | tf_op jit(solution)/shard_map/ppermute | solution.py:920
  81.3 374.9 %all-gather.6.cloned.1.call-start = ((), (), s32[]{:S(2)}) async-start(), calls=%async_computation.4 | async-start | bytes 1081344 | tf_op jit(solution)/shard_map/all_gather | solution.py:1117
  97.2 29.9 %collective-permute-start.13 = (bf16[2,4,2,32,1024]{4,3,2,1,0:T(8,128)(2,1)S(1)}, bf16[2,4,2,32,1024]{4,3,2,1,0:T(8,128)(2,1)S(1)}, u32[]{:S(2)}, u32[]{:S(2)}) collective-permute-start(bf16[2,4,2,32,1024]{4,3,2,1,0:T(8,128)(2,1)S(1)} %pad_maximum_fusion.2.refs_0_), channel_id=1, source_target_pairs={{0,4},{1,5},{2,6},{3,7},{4,0},{5,1},{6,2},{7,3},{8,12},{9,13},{10,... | collective-permute-start | bytes 3145736 | tf_op jit(solution)/shard_map/ppermute | solution.py:920
  98.6 28.5 %collective-permute-start.15 = (bf16[2,4,2,32,1024]{4,3,2,1,0:T(8,128)(2,1)S(1)}, bf16[2,4,2,32,1024]{4,3,2,1,0:T(8,128)(2,1)S(1)}, u32[]{:S(2)}, u32[]{:S(2)}) collective-permute-start(bf16[2,4,2,32,1024]{4,3,2,1,0:T(8,128)(2,1)S(1)} %pad_maximum_fusion.2.refs_0_), channel_id=1, source_target_pairs={{0,2},{1,3},{2,0},{3,1},{4,6},{5,7},{6,4},{7,5},{8,10},{9,11},{10,... | collective-permute-start | bytes 3145736 | tf_op jit(solution)/shard_map/ppermute | solution.py:920
  99.8 27.3 %collective-permute-start.14 = (bf16[2,4,2,32,1024]{4,3,2,1,0:T(8,128)(2,1)S(1)}, bf16[2,4,2,32,1024]{4,3,2,1,0:T(8,128)(2,1)S(1)}, u32[]{:S(2)}, u32[]{:S(2)}) collective-permute-start(bf16[2,4,2,32,1024]{4,3,2,1,0:T(8,128)(2,1)S(1)} %pad_maximum_fusion.3.refs_4_), channel_id=1, source_target_pairs={{0,1},{1,0},{2,3},{3,2},{4,5},{5,4},{6,7},{7,6},{8,9},{9,8},{10,11... | collective-permute-start | bytes 3145736 | tf_op jit(solution)/shard_map/ppermute | solution.py:920
  101.3 28.1 %collective-permute-start.16 = (bf16[2,4,2,32,1024]{4,3,2,1,0:T(8,128)(2,1)S(1)}, bf16[2,4,2,32,1024]{4,3,2,1,0:T(8,128)(2,1)}, u32[]{:S(2)}, u32[]{:S(2)}) collective-permute-start(bf16[2,4,2,32,1024]{4,3,2,1,0:T(8,128)(2,1)S(1)} %pad_maximum_fusion.3.refs_4_), channel_id=1, source_target_pairs={{0,2},{1,3},{2,0},{3,1},{4,6},{5,7},{6,4},{7,5},{8,10},{9,11},{10,... | collective-permute-start | bytes 3145736 | tf_op jit(solution)/shard_map/ppermute | solution.py:920
  146.1 41.6 %collective-permute-start.21 = (bf16[2,4,1,64,1024]{4,3,2,1,0:T(8,128)(2,1)S(1)}, bf16[2,4,1,64,1024]{4,3,2,1,0:T(8,128)(2,1)S(1)}, u32[]{:S(2)}, u32[]{:S(2)}) collective-permute-start(bf16[2,4,1,64,1024]{4,3,2,1,0:T(8,128)(2,1)S(1)} %pad_maximum_fusion.4.refs_0_), channel_id=1, source_target_pairs={{0,4},{1,5},{2,6},{3,7},{4,0},{5,1},{6,2},{7,3},{8,12},{9,13},{10,... | collective-permute-start | bytes 3145736 | tf_op jit(solution)/shard_map/ppermute | solution.py:920
  146.8 40.9 %collective-permute-start.23 = (bf16[2,4,1,64,1024]{4,3,2,1,0:T(8,128)(2,1)S(1)}, bf16[2,4,1,64,1024]{4,3,2,1,0:T(8,128)(2,1)}, u32[]{:S(2)}, u32[]{:S(2)}) collective-permute-start(bf16[2,4,1,64,1024]{4,3,2,1,0:T(8,128)(2,1)S(1)} %pad_maximum_fusion.4.refs_0_), channel_id=1, source_target_pairs={{0,2},{1,3},{2,0},{3,1},{4,6},{5,7},{6,4},{7,5},{8,10},{9,11},{10,... | collective-permute-start | bytes 3145736 | tf_op jit(solution)/shard_map/ppermute | solution.py:920
  146.9 40.8 %collective-permute-start.22 = (bf16[2,4,1,64,1024]{4,3,2,1,0:T(8,128)(2,1)S(1)}, bf16[2,4,1,64,1024]{4,3,2,1,0:T(8,128)(2,1)}, u32[]{:S(2)}, u32[]{:S(2)}) collective-permute-start(bf16[2,4,1,64,1024]{4,3,2,1,0:T(8,128)(2,1)S(1)} %pad_maximum_fusion.5.refs_4_), channel_id=1, source_target_pairs={{0,1},{1,0},{2,3},{3,2},{4,5},{5,4},{6,7},{7,6},{8,9},{9,8},{10,11... | collective-permute-start | bytes 3145736 | tf_op jit(solution)/shard_map/ppermute | solution.py:920
  148.4 39.3 %collective-permute-start.24 = (bf16[2,4,1,64,1024]{4,3,2,1,0:T(8,128)(2,1)S(1)}, bf16[2,4,1,64,1024]{4,3,2,1,0:T(8,128)(2,1)}, u32[]{:S(2)}, u32[]{:S(2)}) collective-permute-start(bf16[2,4,1,64,1024]{4,3,2,1,0:T(8,128)(2,1)S(1)} %pad_maximum_fusion.5.refs_4_), channel_id=1, source_target_pairs={{0,2},{1,3},{2,0},{3,1},{4,6},{5,7},{6,4},{7,5},{8,10},{9,11},{10,... | collective-permute-start | bytes 3145736 | tf_op jit(solution)/shard_map/ppermute | solution.py:920
  215.8 34.8 %collective-permute-start.28 = (bf16[4,2,64,1024]{3,2,1,0:T(8,128)(2,1)S(1)}, bf16[4,2,64,1024]{3,2,1,0:T(8,128)(2,1)}, u32[]{:S(2)}, u32[]{:S(2)}) collective-permute-start(bf16[4,2,64,1024]{3,2,1,0:T(8,128)(2,1)S(1)} %get-tuple-element.350), channel_id=1, source_target_pairs={{0,1},{1,0},{2,3},{3,2},{4,5},{5,4},{6,7},{7,6},{8,9},{9,8},{10,11... | collective-permute-start | bytes 3145736 | tf_op jit(solution)/shard_map/ppermute | solution.py:920
  216.5 34.0 %collective-permute-start.29 = (bf16[4,2,64,1024]{3,2,1,0:T(8,128)(2,1)S(1)}, bf16[4,2,64,1024]{3,2,1,0:T(8,128)(2,1)}, u32[]{:S(2)}, u32[]{:S(2)}) collective-permute-start(bf16[4,2,64,1024]{3,2,1,0:T(8,128)(2,1)S(1)} %get-tuple-element.348), channel_id=1, source_target_pairs={{0,4},{1,5},{2,6},{3,7},{4,0},{5,1},{6,2},{7,3},{8,12},{9,13},{10,... | collective-permute-start | bytes 3145736 | tf_op jit(solution)/shard_map/ppermute | solution.py:920
  250.6 30.4 %collective-permute-start.32 = (bf16[8,64,4096]{2,1,0:T(8,128)(2,1)}, bf16[8,64,4096]{2,1,0:T(8,128)(2,1)}, u32[]{:S(2)}, u32[]{:S(2)}) collective-permute-start(bf16[8,64,4096]{2,1,0:T(8,128)(2,1)} %get-tuple-element.250), channel_id=1, source_target_pairs={{0,2},{1,3},{2,0},{3,1},{4,6},{5,7},{6,4},{7,5},{8,10},{9,11},{10,... | collective-permute-start | bytes 12582920 | tf_op jit(solution)/shard_map/ppermute | solution.py:920
  253.6 27.3 %collective-permute-start.30 = (bf16[4,64,1024]{2,1,0:T(8,128)(2,1)S(1)}, bf16[4,64,1024]{2,1,0:T(8,128)(2,1)}, u32[]{:S(2)}, u32[]{:S(2)}) collective-permute-start(bf16[4,64,1024]{2,1,0:T(8,128)(2,1)S(1)} %get-tuple-element.364), channel_id=1, source_target_pairs={{0,4},{1,5},{2,6},{3,7},{4,0},{5,1},{6,2},{7,3},{8,12},{9,13},{10,... | collective-permute-start | bytes 1572872 | tf_op jit(solution)/shard_map/ppermute | solution.py:920
  256.8 24.2 %collective-permute-start.31 = (bf16[4,64,1024]{2,1,0:T(8,128)(2,1)S(1)}, bf16[4,64,1024]{2,1,0:T(8,128)(2,1)}, u32[]{:S(2)}, u32[]{:S(2)}) collective-permute-start(bf16[4,64,1024]{2,1,0:T(8,128)(2,1)S(1)} %get-tuple-element.362), channel_id=1, source_target_pairs={{0,1},{1,0},{2,3},{3,2},{4,5},{5,4},{6,7},{7,6},{8,9},{9,8},{10,11... | collective-permute-start | bytes 1572872 | tf_op jit(solution)/shard_map/ppermute | solution.py:920
  282.6 173.7 %reduce-scatter.5.cloned.1.call-start = ((), (), s32[]{:S(2)}) async-start(), calls=%async_computation.3 | async-start | bytes 1310720 | tf_op jit(solution)/shard_map/reduce_scatter | solution.py:940
  289.6 35.9 %collective-permute-start.33 = (bf16[4,2,32,2048]{3,2,1,0:T(8,128)(2,1)}, bf16[4,2,32,2048]{3,2,1,0:T(8,128)(2,1)}, u32[]{:S(2)}, u32[]{:S(2)}) collective-permute-start(bf16[4,2,32,2048]{3,2,1,0:T(8,128)(2,1)} %get-tuple-element.346), channel_id=1, source_target_pairs={{0,1},{1,0},{2,3},{3,2},{4,5},{5,4},{6,7},{7,6},{8,9},{9,8},{10,11... | collective-permute-start | bytes 3145736 | tf_op jit(solution)/shard_map/ppermute | solution.py:920
  291.4 34.1 %collective-permute-start.34 = (bf16[4,2,32,2048]{3,2,1,0:T(8,128)(2,1)}, bf16[4,2,32,2048]{3,2,1,0:T(8,128)(2,1)}, u32[]{:S(2)}, u32[]{:S(2)}) collective-permute-start(bf16[4,2,32,2048]{3,2,1,0:T(8,128)(2,1)} %get-tuple-element.344), channel_id=1, source_target_pairs={{0,4},{1,5},{2,6},{3,7},{4,0},{5,1},{6,2},{7,3},{8,12},{9,13},{10,... | collective-permute-start | bytes 3145736 | tf_op jit(solution)/shard_map/ppermute | solution.py:920
  302.4 153.9 %reduce-scatter.3.cloned.1.call-start = ((), (), s32[]{:S(2)}) async-start(), calls=%async_computation.2 | async-start | bytes 1310720 | tf_op jit(solution)/shard_map/reduce_scatter | solution.py:940
  338.0 29.7 %collective-permute-start.35 = (bf16[8,64,2560]{2,1,0:T(8,128)(2,1)}, bf16[8,64,2560]{2,1,0:T(8,128)(2,1)S(1)}, u32[]{:S(2)}, u32[]{:S(2)}) collective-permute-start(bf16[8,64,2560]{2,1,0:T(8,128)(2,1)} %get-tuple-element.268), channel_id=1, source_target_pairs={{0,2},{1,3},{2,0},{3,1},{4,6},{5,7},{6,4},{7,5},{8,10},{9,11},{10,... | collective-permute-start | bytes 7864328 | tf_op jit(solution)/shard_map/ppermute | solution.py:920
  340.5 27.2 %collective-permute-start.36 = (bf16[4,32,2048]{2,1,0:T(8,128)(2,1)S(1)}, bf16[4,32,2048]{2,1,0:T(8,128)(2,1)S(1)}, u32[]{:S(2)}, u32[]{:S(2)}) collective-permute-start(bf16[4,32,2048]{2,1,0:T(8,128)(2,1)S(1)} %get-tuple-element.360), channel_id=1, source_target_pairs={{0,4},{1,5},{2,6},{3,7},{4,0},{5,1},{6,2},{7,3},{8,12},{9,13},{10,... | collective-permute-start | bytes 1572872 | tf_op jit(solution)/shard_map/ppermute | solution.py:920
  343.0 24.7 %collective-permute-start.37 = (bf16[4,32,2048]{2,1,0:T(8,128)(2,1)S(1)}, bf16[4,32,2048]{2,1,0:T(8,128)(2,1)S(1)}, u32[]{:S(2)}, u32[]{:S(2)}) collective-permute-start(bf16[4,32,2048]{2,1,0:T(8,128)(2,1)S(1)} %get-tuple-element.358), channel_id=1, source_target_pairs={{0,1},{1,0},{2,3},{3,2},{4,5},{5,4},{6,7},{7,6},{8,9},{9,8},{10,11... | collective-permute-start | bytes 1572872 | tf_op jit(solution)/shard_map/ppermute | solution.py:920
  378.4 20.4 %collective-permute-start.38 = (bf16[8,64,1536]{2,1,0:T(8,128)(2,1)}, bf16[8,64,1536]{2,1,0:T(8,128)(2,1)}, u32[]{:S(2)}, u32[]{:S(2)}) collective-permute-start(bf16[8,64,1536]{2,1,0:T(8,128)(2,1)} %get-tuple-element.283), channel_id=1, source_target_pairs={{0,2},{1,3},{2,0},{3,1},{4,6},{5,7},{6,4},{7,5},{8,10},{9,11},{10,... | collective-permute-start | bytes 4718600 | tf_op jit(solution)/shard_map/ppermute | solution.py:920
  401.6 20.7 %collective-permute-start.41 = (bf16[4,2,32,768]{3,2,1,0:T(8,128)(2,1)}, bf16[4,2,32,768]{3,2,1,0:T(8,128)(2,1)}, u32[]{:S(2)}, u32[]{:S(2)}) collective-permute-start(bf16[4,2,32,768]{3,2,1,0:T(8,128)(2,1)} %get-tuple-element.374), channel_id=1, source_target_pairs={{0,1},{1,0},{2,3},{3,2},{4,5},{5,4},{6,7},{7,6},{8,9},{9,8},{10,11... | collective-permute-start | bytes 1179656 | tf_op jit(solution)/shard_map/ppermute | solution.py:920
  423.4 24.7 %collective-permute-start.45 = (bf16[4,32,768]{2,1,0:T(8,128)(2,1)S(1)}, bf16[4,32,768]{2,1,0:T(8,128)(2,1)S(1)}, u32[]{:S(2)}, u32[]{:S(2)}) collective-permute-start(bf16[4,32,768]{2,1,0:T(8,128)(2,1)S(1)} %get-tuple-element.396), channel_id=1, source_target_pairs={{0,4},{1,5},{2,6},{3,7},{4,0},{5,1},{6,2},{7,3},{8,12},{9,13},{10,... | collective-permute-start | bytes 589832 | tf_op jit(solution)/shard_map/ppermute | solution.py:920
  424.9 23.2 %collective-permute-start.46 = (bf16[4,32,768]{2,1,0:T(8,128)(2,1)S(1)}, bf16[4,32,768]{2,1,0:T(8,128)(2,1)S(1)}, u32[]{:S(2)}, u32[]{:S(2)}) collective-permute-start(bf16[4,32,768]{2,1,0:T(8,128)(2,1)S(1)} %get-tuple-element.394), channel_id=1, source_target_pairs={{0,1},{1,0},{2,3},{3,2},{4,5},{5,4},{6,7},{7,6},{8,9},{9,8},{10,11... | collective-permute-start | bytes 589832 | tf_op jit(solution)/shard_map/ppermute | solution.py:920
  (96 other events, 1079.4 us)
Sparse Core Ops, SparseCore 0:
  36.3 30.7 all-gather.7
  81.4 31.8 all-gather.9
  282.7 60.2 all-gather.5
  345.2 24.6 reduce-scatter.4
  407.8 33.2 reduce-scatter.2

commit v3 on v2

--- a/solution.py
+++ b/solution.py
@@ -7,6 +7,7 @@
 import numpy as np
 from jax import lax
 from jax.experimental import pallas as pl
+from jax.experimental.layout import Layout, with_layout_constraint
 from jax.experimental.pallas import tpu as pltpu
 from jax.sharding import PartitionSpec as P
 
@@ -59,15 +60,15 @@
         o_ref[i*BQ:(i+1)*BQ,:]=jnp.where(first,outs[0],outs[1]).astype(bf16)
         lse_ref[i*BQ:(i+1)*BQ,:]=jnp.where(first,lses[0],lses[1])
 
-def attn_fwd(length,slopes,qkv,start,count):
-    n=qkv.shape[0]; D=qkv.shape[1]//3; full=D//128; np_=count; D=128*count
+def attn_fwd(length,slopes,qkv,start):
+    n=qkv.shape[0]; D=qkv.shape[1]//3; np_=D//128
     length=jnp.stack([length,jnp.int32(start)])
     spec=lambda off: pl.BlockSpec((n,128),lambda p,*_: (0,p+off))
     return pl.pallas_call(attn_fwd_kernel,
         grid_spec=pltpu.PrefetchScalarGridSpec(num_scalar_prefetch=2,grid=(np_,),
-            in_specs=[spec(start),spec(full+start),spec(2*full+start)],out_specs=[spec(0),spec(0)]),
+            in_specs=[spec(0),spec(np_),spec(2*np_)],out_specs=[spec(0),spec(0)]),
         out_shape=[jax.ShapeDtypeStruct((n,D),bf16),jax.ShapeDtypeStruct((n,D),f32)],
-        compiler_params=pltpu.CompilerParams(vmem_limit_bytes=48*2**20),
+        compiler_params=pltpu.CompilerParams(vmem_limit_bytes=63*2**20),
         cost_estimate=pl.CostEstimate(flops=int(2*2*n*n*D*2.5),bytes_accessed=n*D*12,transcendentals=n*n*10),
         name="attn_fwd")(length,slopes,qkv,qkv,qkv)
 
@@ -128,13 +129,13 @@
         dk_ref[ks,:]=jnp.where(first,dks[0],dks[1]).astype(bf16)
     dq_ref[...]=(dqt_ref[...]*0.125).T.astype(bf16)
 
-def attn_bwd(length,slopes3,qkv,o,lse,do,start,count):
-    n=qkv.shape[0]; D=qkv.shape[1]//3; full=D//128; np_=count; D=128*count
+def attn_bwd(length,slopes3,qkv,o,lse,do,start):
+    n=qkv.shape[0]; D=qkv.shape[1]//3; np_=D//128
     length=jnp.stack([length,jnp.int32(start)])
     spec=lambda off: pl.BlockSpec((n,128),lambda p,*_: (0,p+off))
     return pl.pallas_call(attn_bwd_kernel,
         grid_spec=pltpu.PrefetchScalarGridSpec(num_scalar_prefetch=2,grid=(np_,),
-            in_specs=[spec(start),spec(full+start),spec(2*full+start),spec(start),spec(start),spec(start)],out_specs=[spec(0)]*3,
+            in_specs=[spec(0),spec(np_),spec(2*np_),spec(0),spec(0),spec(start)],out_specs=[spec(0)]*3,
             scratch_shapes=[pltpu.VMEM((2,n,256),bf16),pltpu.VMEM((2,n,256),bf16),pltpu.VMEM((128,n),f32)]),
         out_shape=[jax.ShapeDtypeStruct((n,D),bf16)]*3,
         compiler_params=pltpu.CompilerParams(vmem_limit_bytes=48*2**20),
@@ -392,26 +393,45 @@
     return flat_index(za, y + yr - 2 * y * yr, c + core - 2 * c * core, x + xr - 2 * x * xr)
 
 
-def start_columns(place_ref, pieces, w_ref, sems, turned):
-    for half in range(2):
-        for zr, near, turn, core in itertools.product(range(4), *[range(2)] * 3):
-            d = owner_of(place_ref, half, zr, near, turn, core, turned)
-            rows = pl.ds(pl.multiple_of(d * 32, 32), 32)
-            src = pieces[4 * half + 2 * core + turn].at[near, zr]
-            dst = w_ref.at[2 * half : 2 * half + 2, rows, :]
-            pltpu.make_async_copy(src, dst, sems.at[half]).start()
-
-
-def wait_columns(w_ref, sems, half):
-    part = w_ref.at[2 * half : 2 * half + 2]
-    pltpu.make_async_copy(part, part, sems.at[half]).wait()
+def start_mixed(place_ref, pieces, w_ref, sem, turned):
+    for half, zr, near, turn, core in itertools.product(range(2), range(4), *[range(2)] * 3):
+        d = owner_of(place_ref, half, zr, near, turn, core, turned)
+        rows = pl.ds(pl.multiple_of(d * 32 + half * 16, 16), 16)
+        src = pieces[4 * half + 2 * core + turn].at[near, zr]
+        pltpu.make_async_copy(src, w_ref.at[:, rows, :], sem).start()
+
+
+def of_half(pieces, half):
+    return [pieces[5 * core + i] for core in range(2) for i in (0, 1, 2, 3 + half)]
+
+
+def piece(pieces, half, zr, xr, yr, core):
+    ref = pieces[4 * core + xr + 2 * yr]
+    return ref.at[zr] if xr and yr else ref.at[zr, half]
+
+
+def owner(place_ref, zr, xr, yr, core):
+    _, y, c, x = (place_ref[i] for i in range(4))
+    return flat_index(zr, y + yr - 2 * y * yr, c + core - 2 * c * core, x + xr - 2 * x * xr)
+
+
+def start_columns(place_ref, pieces, w_ref, sem, half):
+    for zr, xr, yr, core in itertools.product(range(4), *[range(2)] * 3):
+        d = owner(place_ref, zr, xr, yr, core)
+        rows = pl.ds(pl.multiple_of(d * 32, 32), 32)
+        src = piece(pieces, half, zr, xr, yr, core)
+        pltpu.make_async_copy(src, w_ref.at[:, rows, :], sem).start()
+
+
+def wait_all(ref, sem):
+    pltpu.make_async_copy(ref, ref, sem).wait()
 
 
 def start_rows(place_ref, pieces, w_ref, sems):
-    for zr, half, near, turn, core in itertools.product(range(4), *[range(2)] * 4):
-        d = owner_of(place_ref, half, zr, near, turn, core, False)
+    for zr, half, xr, yr, core in itertools.product(range(4), *[range(2)] * 4):
+        d = owner(place_ref, zr, xr, yr, core)
         rows = pl.ds(pl.multiple_of(d * 128 + half * 64, 64), 64)
-        src = pieces[4 * half + 2 * core + turn].at[near, zr, 0]
+        src = piece(of_half(pieces, half), half, zr, xr, yr, core).at[0]
         pltpu.make_async_copy(src, w_ref.at[rows, :], sems.at[zr]).start()
 
 
@@ -432,78 +452,115 @@
     return pltpu.CompilerParams(vmem_limit_bytes=mib * MIB)
 
 
-PIECES = [pl.BlockSpec(memory_space=pltpu.HBM)] * 8
-
-
-def qkv_kernel(place_ref, *refs):
-    pieces, (a_ref, b_ref, o_ref, all_ref, w_ref, sems, out_sems) = refs[:8], refs[8:]
+HBM = pl.BlockSpec(memory_space=pltpu.HBM)
+
+
+def qkv_kernel(turned, place_ref, *refs):
+    pieces, (a_ref, b_ref, o_ref, all_ref, w_ref, sem, out_sem) = refs[:8], refs[8:]
     step = pl.program_id(0)
+    write = pltpu.make_async_copy(w_ref, all_ref, out_sem)
 
     @pl.when(step == 0)
     def _():
-        start_columns(place_ref, pieces, w_ref, sems, True)
-
-    for half in range(2):
-        part = slice(2 * half, 2 * half + 2)
-        write = pltpu.make_async_copy(w_ref.at[part], all_ref.at[part], out_sems.at[half])
-
-        @pl.when(step == 4 * half)
-        def _():
-            wait_columns(w_ref, sems, half)
-            write.start()
-
-        @pl.when(step == 5)
-        def _():
-            write.wait()
-
-    w = w_ref[step // 2, :, pl.ds(pl.multiple_of(step % 2 * 512, 512), 512)]
-    o_ref[...] = (dot(a_ref[...], w) + b_ref[...]).astype(bf16)
-
-
-def qkv_call(place, pieces, a, b):
+        start_mixed(place_ref, pieces, w_ref, sem, turned)
+        wait_all(w_ref, sem)
+        write.start()
+
+    o_ref[...] = (dot(a_ref[...], w_ref[step]) + b_ref[...]).astype(bf16)
+
+    @pl.when(step == 2)
+    def _():
+        write.wait()
+
+
+def qkv_call(place, pieces, a, b, turned):
     n, d = a.shape
+    blocks = pieces[0].shape[2]
     return pl.pallas_call(
-        qkv_kernel,
+        functools.partial(qkv_kernel, turned),
         grid_spec=pltpu.PrefetchScalarGridSpec(
             num_scalar_prefetch=1,
-            grid=(6,),
-            in_specs=PIECES
+            grid=(3,),
+            in_specs=[HBM] * 8
             + [spec((n, d), lambda i, *_: (0, 0)), spec((1, 512), lambda i, *_: (0, i))],
-            out_specs=[
-                spec((n, 512), lambda i, *_: (0, i)),
-                pl.BlockSpec(memory_space=pltpu.HBM),
+            out_specs=[spec((n, 512), lambda i, *_: (0, i)), HBM],
+            scratch_shapes=[
+                pltpu.VMEM((blocks, d, 512), bf16),
+                pltpu.SemaphoreType.DMA,
+                pltpu.SemaphoreType.DMA,
             ],
-            scratch_shapes=[
-                pltpu.VMEM((4, d, 1024), bf16),
-                pltpu.SemaphoreType.DMA((2,)),
-                pltpu.SemaphoreType.DMA((2,)),
-            ],
         ),
         out_shape=[
-            jax.ShapeDtypeStruct((n, 3 * d), bf16),
-            jax.ShapeDtypeStruct((4, d, 1024), bf16),
+            jax.ShapeDtypeStruct((n, 1536), bf16),
+            jax.ShapeDtypeStruct((blocks, d, 512), bf16),
         ],
-        compiler_params=params(),
+        compiler_params=params(63),
         cost_estimate=pl.CostEstimate(
-            flops=2 * n * d * 3 * d, bytes_accessed=2 * (n * d + 8 * d * d + 3 * n * d), transcendentals=0
+            flops=2 * n * d * 1536, bytes_accessed=2 * (n * d + 8 * d * 512 + 1536 * n), transcendentals=0
         ),
         name="qkv",
-    )(place, *pieces, a, b.reshape(1, 3 * d))
-
-
-def up_kernel(place_ref, *refs):
-    pieces, (a_ref, b_ref, u_ref, s_ref, w_ref, sems) = refs[:8], refs[8:]
+    )(place, *pieces, a, b.reshape(1, 1536))
+
+
+def dense_kernel(c0_ref, c1_ref, w0_ref, w1_ref, x_ref, b_ref, g_ref, s_ref, h_ref, a_ref):
+    half = [
+        dot(c0_ref[...], w_ref[0, :512, :]) + dot(c1_ref[...], w_ref[0, 512:, :])
+        for w_ref in (w0_ref, w1_ref)
+    ]
+    hidden = x_ref[...].astype(f32) + jnp.concatenate(half, axis=1) + b_ref[...]
+    h_ref[...] = hidden
+    center = hidden - jnp.mean(hidden, axis=1, keepdims=True)
+    rsd = lax.rsqrt(jnp.mean(center * center, axis=1, keepdims=True) + 1e-05)
+    a_ref[...] = (center * rsd * g_ref[...] + s_ref[...]).astype(bf16)
+
+
+def dense_call(c0, c1, w, x, bias, gain, shift):
+    n, d = x.shape
+    rows = lambda c: spec((256, c), lambda i: (i, 0))
+    vector = spec((1, d), lambda i: (0, 0))
+    return pl.pallas_call(
+        dense_kernel,
+        grid=(n // 256,),
+        in_specs=[rows(512), rows(512)]
+        + [spec((1, d, 512), lambda i, b=b: (b, 0, 0)) for b in (3, 4)]
+        + [rows(d), vector, vector, vector],
+        out_specs=[rows(d), rows(d)],
+        out_shape=[jax.ShapeDtypeStruct((n, d), f32), jax.ShapeDtypeStruct((n, d), bf16)],
+        compiler_params=params(40),
+        cost_estimate=pl.CostEstimate(flops=2 * n * d * d, bytes_accessed=12 * n * d, transcendentals=0),
+        name="dense",
+    )(c0, c1, w, w, x, bias.reshape(1, d), gain.reshape(1, d), shift.reshape(1, d))
+
+
+def dense_back_kernel(g_ref, w0_ref, w1_ref, o_ref):
+    o_ref[...] = (
+        dotnt(g_ref[:, :512], w0_ref[0]) + dotnt(g_ref[:, 512:], w1_ref[0])
+    ).astype(bf16)
+
+
+def dense_back_call(g, w):
+    n, d = g.shape
+    rows = spec((256, d), lambda i: (i, 0))
+    return pl.pallas_call(
+        dense_back_kernel,
+        grid=(n // 256,),
+        in_specs=[rows] + [spec((1, d, 512), lambda i, b=b: (b, 0, 0)) for b in (3, 4)],
+        out_specs=rows,
+        out_shape=jax.ShapeDtypeStruct((n, d), bf16),
+        compiler_params=params(40),
+        cost_estimate=pl.CostEstimate(flops=2 * n * d * d, bytes_accessed=6 * n * d, transcendentals=0),
+        name="dense_back",
+    )(g, w, w)
+
+
+def up_kernel(half, place_ref, *refs):
+    pieces, (a_ref, b_ref, u_ref, s_ref, w_ref, sem) = refs[:8], refs[8:]
     step = pl.program_id(0)
 
     @pl.when(step == 0)
     def _():
-        start_columns(place_ref, pieces, w_ref, sems, False)
-
-    for half in range(2):
-
-        @pl.when(step == 4 * half)
-        def _():
-            wait_columns(w_ref, sems, half)
+        start_columns(place_ref, pieces, w_ref, sem, half)
+        wait_all(w_ref, sem)
 
     c = 0.7978845608028654
     w = w_ref[step // 2, :, pl.ds(pl.multiple_of(step % 2 * 512, 512), 512)]
@@ -518,93 +575,70 @@
         ).astype(bf16)
 
 
-def up_call(place, pieces, a, b):
+def up_call(place, half, pieces, a, b):
     n, d = a.shape
-    ff = b.shape[0]
-    kb = 512
     return pl.pallas_call(
-        up_kernel,
+        functools.partial(up_kernel, half),
         grid_spec=pltpu.PrefetchScalarGridSpec(
             num_scalar_prefetch=1,
-            grid=(ff // kb,),
-            in_specs=PIECES
-            + [spec((n, d), lambda i, *_: (0, 0)), spec((1, kb), lambda i, *_: (0, i))],
-            out_specs=[spec((n, kb), lambda i, *_: (0, i))] * 2,
-            scratch_shapes=[pltpu.VMEM((4, d, 1024), bf16), pltpu.SemaphoreType.DMA((2,))],
-        ),
-        out_shape=[jax.ShapeDtypeStruct((n, ff), bf16)] * 2,
-        compiler_params=params(),
+            grid=(4,),
+            in_specs=[HBM] * 8
+            + [spec((n, d), lambda i, *_: (0, 0)), spec((1, 512), lambda i, *_: (0, 4 * half + i))],
+            out_specs=[spec((n, 512), lambda i, *_: (0, i))] * 2,
+            scratch_shapes=[pltpu.VMEM((2, d, 1024), bf16), pltpu.SemaphoreType.DMA],
+        ),
+        out_shape=[jax.ShapeDtypeStruct((n, 2048), bf16)] * 2,
+        compiler_params=params(40),
         cost_estimate=pl.CostEstimate(
-            flops=2 * n * d * ff, bytes_accessed=2 * (n * d + d * ff + 2 * n * ff), transcendentals=n * ff
+            flops=2 * n * d * 2048, bytes_accessed=2 * (n * d + d * 2048 + 4096 * n), transcendentals=n * 2048
         ),
         name="up",
-    )(place, *pieces, a, b.reshape(1, ff))
-
-
-def split_kernel(transposed, where_ref, a_ref, g_ref, keep_ref, give_ref, *scratch):
-    core = where_ref[2]
-    if transposed:
-        (acc_ref,) = scratch
-        acc = dottn(a_ref[...], g_ref[...])
-    else:
-        at_ref, acc_ref = scratch
-
-        @pl.when(pl.program_id(0) == 0)
-        def _():
-            at_ref[...] = a_ref[...].T
-
-        acc = dot(at_ref[...], g_ref[...])
-    acc_ref[...] = acc.astype(bf16).reshape(acc_ref.shape)
+    )(place, *of_half(pieces, half), a, b.reshape(1, 4096))
+
+
+def divide(acc_ref, keep_ref, give_ref, core):
     keep_ref[...] = acc_ref[:, pl.ds(core, 1)].reshape(keep_ref.shape)
     give_ref[...] = acc_ref[:, pl.ds(1 - core, 1)].reshape(give_ref.shape)
 
 
+def down_grad_kernel(where_ref, u0_ref, u1_ref, g_ref, keep_ref, give_ref, acc_ref):
+    step = pl.program_id(0)
+    for half, u_ref in enumerate((u0_ref, u1_ref)):
+
+        @pl.when(step // 4 == half)
+        def _(u_ref=u_ref):
+            acc_ref[...] = dottn(u_ref[...], g_ref[...]).astype(bf16).reshape(acc_ref.shape)
+
+    divide(acc_ref, keep_ref, give_ref, where_ref[2])
+
+
 def down_grad_call(where, u, g):
-    n, ff = u.shape
-    d = g.shape[1]
+    n, d = g.shape
     out = spec((1, 256, d), lambda i, *_: (i, 0, 0))
     return pl.pallas_call(
-        functools.partial(split_kernel, True),
+        down_grad_kernel,
         grid_spec=pltpu.PrefetchScalarGridSpec(
             num_scalar_prefetch=1,
             grid=(8,),
-            in_specs=[spec((n, 512), lambda i, *_: (0, i)), spec((n, d), lambda i, *_: (0, 0))],
+            in_specs=[
+                spec((n, 512), lambda i, *_: (0, jnp.minimum(i, 3))),
+                spec((n, 512), lambda i, *_: (0, jnp.maximum(i - 4, 0))),
+                spec((n, d), lambda i, *_: (0, 0)),
+            ],
             out_specs=[out, out],
             scratch_shapes=[pltpu.VMEM((1, 2, 256, d), bf16)],
         ),
         out_shape=[jax.ShapeDtypeStruct((8, 256, d), bf16)] * 2,
-        compiler_params=params(),
+        compiler_params=params(40),
         cost_estimate=pl.CostEstimate(
-            flops=2 * n * d * ff, bytes_accessed=2 * (n * d + d * ff + n * ff), transcendentals=0
+            flops=2 * n * d * 4096, bytes_accessed=2 * (n * d + d * 4096 + n * 4096), transcendentals=0
         ),
         name="down_grad",
-    )(where, u, g)
-
-
-def up_grad_call(where, a, g):
-    n, d = a.shape
-    ff = g.shape[1]
-    out = spec((8, 64, 512), lambda i, *_: (0, 0, i))
-    return pl.pallas_call(
-        functools.partial(split_kernel, False),
-        grid_spec=pltpu.PrefetchScalarGridSpec(
-            num_scalar_prefetch=1,
-            grid=(ff // 512,),
-            in_specs=[spec((n, d), lambda i, *_: (0, 0)), spec((n, 512), lambda i, *_: (0, i))],
-            out_specs=[out, out],
-            scratch_shapes=[pltpu.VMEM((d, n), bf16), pltpu.VMEM((8, 2, 64, 512), bf16)],
-        ),
-        out_shape=[jax.ShapeDtypeStruct((8, 64, ff), bf16)] * 2,
-        compiler_params=params(),
-        cost_estimate=pl.CostEstimate(
-            flops=2 * n * d * ff, bytes_accessed=2 * (n * d + d * ff + n * ff), transcendentals=0
-        ),
-        name="up_grad",
-    )(where, a, g)
+    )(where, *u, g)
 
 
 def down_kernel(place_ref, *refs):
-    pieces, (u_ref, h_ref, b_ref, o_ref, acc_ref, w_ref, sems) = refs[:8], refs[8:]
+    pieces, (u0_ref, u1_ref, h_ref, b_ref, o_ref, acc_ref, w_ref, sems) = refs[:10], refs[10:]
     step = pl.program_id(0)
 
     @pl.when(step == 0)
@@ -616,49 +650,57 @@
 
     @pl.when(step == 0)
     def _():
-        acc_ref[...] = dot(u_ref[...], w)
-
-    @pl.when((step > 0) & (step < 3))
-    def _():
-        acc_ref[...] += dot(u_ref[...], w)
+        acc_ref[...] = dot(u0_ref[...], w)
+
+    @pl.when(step == 1)
+    def _():
+        acc_ref[...] += dot(u0_ref[...], w)
+
+    @pl.when(step == 2)
+    def _():
+        acc_ref[...] += dot(u1_ref[...], w)
 
     @pl.when(step == 3)
     def _():
-        for r in range(0, u_ref.shape[0], 256):
+        for r in range(0, u1_ref.shape[0], 256):
             rows = slice(r, r + 256)
-            part = acc_ref[rows, :] + dot(u_ref[rows, :], w)
+            part = acc_ref[rows, :] + dot(u1_ref[rows, :], w)
             o_ref[rows, :] = (h_ref[rows, :] + part + b_ref[...]).astype(bf16)
 
 
 def down_call(place, pieces, u, hidden, bias):
-    n, ff = u.shape
-    d = hidden.shape[1]
+    n, d = hidden.shape
     whole = lambda s: spec(s, lambda i, *_: (0, 0))
     return pl.pallas_call(
         down_kernel,
         grid_spec=pltpu.PrefetchScalarGridSpec(
             num_scalar_prefetch=1,
             grid=(4,),
-            in_specs=PIECES
-            + [spec((n, ff // 4), lambda i, *_: (0, i)), whole((n, d)), whole((1, d))],
+            in_specs=[HBM] * 10
+            + [
+                spec((n, 1024), lambda i, *_: (0, jnp.minimum(i, 1))),
+                spec((n, 1024), lambda i, *_: (0, jnp.maximum(i - 2, 0))),
+                whole((n, d)),
+                whole((1, d)),
+            ],
             out_specs=whole((n, d)),
             scratch_shapes=[
                 pltpu.VMEM((n, d), f32),
-                pltpu.VMEM((ff, d), bf16),
+                pltpu.VMEM((4096, d), bf16),
                 pltpu.SemaphoreType.DMA((4,)),
             ],
         ),
         out_shape=jax.ShapeDtypeStruct((n, d), bf16),
         compiler_params=params(),
         cost_estimate=pl.CostEstimate(
-            flops=2 * n * d * ff, bytes_accessed=2 * (3 * n * d + d * ff + n * ff), transcendentals=0
+            flops=2 * n * d * 4096, bytes_accessed=2 * (3 * n * d + d * 4096 + n * 4096), transcendentals=0
         ),
         name="down",
-    )(place, *pieces, u, hidden, bias.reshape(1, d))
+    )(place, *pieces, *u, hidden, bias.reshape(1, d))
 
 
 def gate_kernel(place_ref, *refs):
-    pieces, (g_ref, s_ref, z_ref, b_ref, w_ref, sems) = refs[:8], refs[8:]
+    pieces, (g_ref, s0_ref, s1_ref, z_ref, b_ref, w_ref, sems) = refs[:10], refs[10:]
     step = pl.program_id(0)
 
     @pl.when(step == 0)
@@ -670,34 +712,40 @@
     total = None
     for r in range(0, g_ref.shape[0], 256):
         rows = slice(r, r + 256)
-        v = (dotnt(g_ref[rows, :], w) * s_ref[rows, :].astype(f32)).astype(bf16)
+        slope = jnp.where(step < 2, s0_ref[rows, :], s1_ref[rows, :])
+        v = (dotnt(g_ref[rows, :], w) * slope.astype(f32)).astype(bf16)
         z_ref[rows, :] = v
         part = jnp.sum(v.astype(f32).reshape(32, 8, v.shape[1]), axis=0)
         total = part if total is None else total + part
     b_ref[...] = jnp.sum(total, axis=0, keepdims=True)
 
 
-def gate_call(place, pieces, g, slope):
+def gate_call(place, pieces, g, slopes):
     n, d = g.shape
-    ff = slope.shape[1]
-    kb = 1024
     return pl.pallas_call(
         gate_kernel,
         grid_spec=pltpu.PrefetchScalarGridSpec(
             num_scalar_prefetch=1,
-            grid=(ff // kb,),
-            in_specs=PIECES
-            + [spec((n, d), lambda i, *_: (0, 0)), spec((n, kb), lambda i, *_: (0, i))],
-            out_specs=[spec((n, kb), lambda i, *_: (0, i)), spec((1, kb), lambda i, *_: (0, i))],
-            scratch_shapes=[pltpu.VMEM((ff, d), bf16), pltpu.SemaphoreType.DMA((4,))],
-        ),
-        out_shape=[jax.ShapeDtypeStruct((n, ff), bf16), jax.ShapeDtypeStruct((1, ff), f32)],
+            grid=(4,),
+            in_specs=[HBM] * 10
+            + [
+                spec((n, d), lambda i, *_: (0, 0)),
+                spec((n, 1024), lambda i, *_: (0, jnp.minimum(i, 1))),
+                spec((n, 1024), lambda i, *_: (0, jnp.maximum(i - 2, 0))),
+            ],
+            out_specs=[
+                spec((n, 1024), lambda i, *_: (0, i)),
+                spec((1, 1024), lambda i, *_: (0, i)),
+            ],
+            scratch_shapes=[pltpu.VMEM((4096, d), bf16), pltpu.SemaphoreType.DMA((4,))],
+        ),
+        out_shape=[jax.ShapeDtypeStruct((n, 4096), bf16), jax.ShapeDtypeStruct((1, 4096), f32)],
         compiler_params=params(),
         cost_estimate=pl.CostEstimate(
-            flops=2 * n * d * ff, bytes_accessed=2 * (n * d + d * ff + 2 * n * ff), transcendentals=0
+            flops=2 * n * d * 4096, bytes_accessed=2 * (n * d + d * 4096 + 8192 * n), transcendentals=0
         ),
         name="gate",
-    )(place, *pieces, g, slope)
+    )(place, *pieces, g, *slopes)
 
 
 def norm_back(x_ref, gain_ref, res_ref, acc_ref, out_refs, sums_ref):
@@ -730,20 +778,22 @@
 
 def norm_up_kernel(place_ref, *refs):
     pieces, (g_ref, x_ref, gain_ref, res_ref, low_ref, wide_ref, sums_ref, acc_ref, w_ref, sems) = (
-        refs[:8],
-        refs[8:],
+        refs[:10],
+        refs[10:],
     )
     step = pl.program_id(0)
 
     @pl.when(step == 0)
     def _():
-        start_columns(place_ref, pieces, w_ref, sems, False)
+        for half in range(2):
+            part = w_ref.at[2 * half : 2 * half + 2]
+            start_columns(place_ref, of_half(pieces, half), part, sems.at[half], half)
 
     for half in range(2):
 
         @pl.when(step == 2 * half)
         def _():
-            wait_columns(w_ref, sems, half)
+            wait_all(w_ref.at[2 * half : 2 * half + 2], sems.at[half])
 
     @pl.when(step == 0)
     def _():
@@ -767,7 +817,7 @@
         grid_spec=pltpu.PrefetchScalarGridSpec(
             num_scalar_prefetch=1,
             grid=(4,),
-            in_specs=PIECES
+            in_specs=[HBM] * 10
             + [spec((n, 1024), lambda i, *_: (0, i)), whole((n, d)), whole((1, d)), whole((n, d))],
             out_specs=[whole((n, d)), whole((n, d)), whole((8, d))],
             scratch_shapes=[
@@ -790,109 +840,120 @@
 
 
 def norm_qkv_kernel(*refs):
-    g_refs = refs[:3]
-    w_ref, x_ref, gain_ref, res_ref, start_ref, low_ref, sums_ref, acc_ref = refs[3:]
+    g_refs = refs[:6]
+    w0_ref, w1_ref, x_ref, gain_ref, res_ref, low_ref, sums_ref, acc_ref = refs[6:]
     step = pl.program_id(0)
     for i in range(3):
 
         @pl.when(step == i)
         def _(i=i):
-            before = start_ref[...] if i == 0 else acc_ref[...]
-            acc_ref[...] = before + dotnt(g_refs[i][...], w_ref[0])
+            part = dotnt(g_refs[i][...], w0_ref[0]) + dotnt(g_refs[3 + i][...], w1_ref[0])
+            acc_ref[...] = part if i == 0 else acc_ref[...] + part
 
     @pl.when(step == 2)
     def _():
         norm_back(x_ref, gain_ref, res_ref, acc_ref, (low_ref,), sums_ref)
 
 
-def norm_qkv_call(grads, w, x, gain, residual, start):
+def norm_qkv_call(grads, w0, w1, x, gain, residual):
     n, d = x.shape
     whole = lambda s: spec(s, lambda i: (0, 0))
     return pl.pallas_call(
         norm_qkv_kernel,
         grid=(3,),
-        in_specs=[whole((n, 512))] * 3
-        + [spec((1, d, 512), lambda i: (i, 0, 1))]
-        + [whole((n, d)), whole((1, d)), whole((n, d)), whole((n, d))],
+        in_specs=[whole((n, 512))] * 6
+        + [spec((1, d, 512), lambda i: (i, 0, 0))] * 2
+        + [whole((n, d)), whole((1, d)), whole((n, d))],
         out_specs=[whole((n, d)), whole((8, d))],
         out_shape=[jax.ShapeDtypeStruct((n, d), bf16), jax.ShapeDtypeStruct((8, d), f32)],
         scratch_shapes=[pltpu.VMEM((n, d), f32)],
         compiler_params=params(),
         cost_estimate=pl.CostEstimate(
-            flops=2 * n * d * 1536, bytes_accessed=2 * (8 * n * d + d * 3072), transcendentals=0
+            flops=2 * n * d * 3072, bytes_accessed=2 * (8 * n * d + d * 3072), transcendentals=0
         ),
         name="norm_qkv",
-    )(*grads, w, x, gain.reshape(1, d), residual, start)
-
-
-def part_kernel(*refs):
-    g_refs, w_ref, o_ref = refs[:-2], refs[-2], refs[-1]
-    step = pl.program_id(0)
-    for i, g_ref in enumerate(g_refs):
-
-        @pl.when(step == i)
-        def _(i=i, g_ref=g_ref):
-            value = dotnt(g_ref[...], w_ref[0])
-            o_ref[...] = value if i == 0 else o_ref[...] + value
-
-
-def part_call(grads, w):
-    n, kb = grads[0].shape
-    d = w.shape[1]
-    return pl.pallas_call(
-        part_kernel,
-        grid=(len(grads),),
-        in_specs=[spec((n, kb), lambda i: (0, 0))] * len(grads)
-        + [spec((1, d, kb), lambda i: (i, 0, 0))],
-        out_specs=spec((n, d), lambda i: (0, 0)),
-        out_shape=jax.ShapeDtypeStruct((n, d), f32),
-        compiler_params=params(),
-        cost_estimate=pl.CostEstimate(
-            flops=2 * n * d * kb * len(grads), bytes_accessed=4 * n * d * 4, transcendentals=0
-        ),
-        name="part",
-    )(*grads, w)
-
-
-def columns_kernel(plan, lefts, where_ref, *refs):
-    left_refs, right_refs = refs[:lefts], refs[lefts : lefts + len(plan)]
-    keep_ref, give_ref, at_ref, acc_ref = refs[-4:]
-    core = where_ref[2]
+    )(*grads, w0, w1, x, gain.reshape(1, d), residual)
+
+
+def columns_kernel(plan, parts, where_ref, *refs):
+    count = sum(parts)
+    left_refs, right_refs = refs[:count], refs[count : count + len(plan)]
+    keep_ref, give_ref, sums_ref, at_ref, acc_ref = refs[-5:]
     step = pl.program_id(0)
     for i, left in enumerate(plan):
 
         @pl.when(step == i)
         def _(i=i, left=left):
             if i == 0 or plan[i - 1] != left:
-                at_ref[...] = left_refs[left][...].T
-            acc = dot(at_ref[...], right_refs[i][...])
+                begin = sum(parts[:left])
+                row = 0
+                for ref in left_refs[begin : begin + parts[left]]:
+                    at_ref[row : row + ref.shape[1], :] = ref[...].T
+                    row += ref.shape[1]
+            right = right_refs[i][...]
+            acc = dot(at_ref[...], right)
             acc_ref[...] = acc.astype(bf16).reshape(acc_ref.shape)
-
-    keep_ref[...] = acc_ref[:, pl.ds(core, 1)].reshape(keep_ref.shape)
-    give_ref[...] = acc_ref[:, pl.ds(1 - core, 1)].reshape(give_ref.shape)
-
-
-def columns_call(where, lefts, rights, plan):
-    n, d = lefts[0].shape
+            total = jnp.sum(right.astype(f32).reshape(-1, 8, right.shape[1]), axis=0)
+            sums_ref[...] = jnp.sum(total, axis=0, keepdims=True)
+
+    divide(acc_ref, keep_ref, give_ref, where_ref[2])
+
+
+def columns_call(where, lefts, rights, plan, name):
+    flat = [a for left in lefts for a in left]
+    n = flat[0].shape[0]
+    d = sum(a.shape[1] for a in lefts[0])
     wide = 512 * len(rights)
     out = spec((8, 64, 512), lambda i, *_: (0, 0, i))
     return pl.pallas_call(
-        functools.partial(columns_kernel, plan, len(lefts)),
+        functools.partial(columns_kernel, plan, [len(left) for left in lefts]),
         grid_spec=pltpu.PrefetchScalarGridSpec(
             num_scalar_prefetch=1,
             grid=(len(plan),),
-            in_specs=[spec((n, d), lambda i, *_: (0, 0))] * len(lefts)
+            in_specs=[spec(a.shape, lambda i, *_: (0, 0)) for a in flat]
             + [spec((n, 512), lambda i, *_, b=b: (0, b)) for _, b in rights],
+            out_specs=[out, out, spec((1, 512), lambda i, *_: (0, i))],
+            scratch_shapes=[pltpu.VMEM((d, n), bf16), pltpu.VMEM((8, 2, 64, 512), bf16)],
+        ),
+        out_shape=[jax.ShapeDtypeStruct((8, 64, wide), bf16)] * 2
+        + [jax.ShapeDtypeStruct((1, wide), f32)],
+        compiler_params=params(40),
+        cost_estimate=pl.CostEstimate(
+            flops=2 * n * d * wide, bytes_accessed=2 * (2 * n * d + d * wide + n * wide), transcendentals=0
+        ),
+        name=name,
+    )(where, *flat, *[r for r, _ in rights])
+
+
+def up_grad_kernel(where_ref, a_ref, g_ref, keep_ref, give_ref, at_ref, acc_ref):
+    @pl.when(pl.program_id(0) == 0)
+    def _():
+        at_ref[...] = a_ref[...].T
+
+    acc_ref[...] = dot(at_ref[...], g_ref[...]).astype(bf16).reshape(acc_ref.shape)
+    divide(acc_ref, keep_ref, give_ref, where_ref[2])
+
+
+def up_grad_call(where, a, g):
+    n, d = a.shape
+    ff = g.shape[1]
+    out = spec((8, 64, 512), lambda i, *_: (0, 0, i))
+    return pl.pallas_call(
+        up_grad_kernel,
+        grid_spec=pltpu.PrefetchScalarGridSpec(
+            num_scalar_prefetch=1,
+            grid=(ff // 512,),
+            in_specs=[spec((n, d), lambda i, *_: (0, 0)), spec((n, 512), lambda i, *_: (0, i))],
             out_specs=[out, out],
             scratch_shapes=[pltpu.VMEM((d, n), bf16), pltpu.VMEM((8, 2, 64, 512), bf16)],
         ),
-        out_shape=[jax.ShapeDtypeStruct((8, 64, wide), bf16)] * 2,
-        compiler_params=params(),
+        out_shape=[jax.ShapeDtypeStruct((8, 64, ff), bf16)] * 2,
+        compiler_params=params(40),
         cost_estimate=pl.CostEstimate(
-            flops=2 * n * d * wide, bytes_accessed=2 * (2 * n * d + d * wide + n * wide), transcendentals=0
-        ),
-        name="columns",
-    )(where, *lefts, *[r for r, _ in rights])
+            flops=2 * n * d * ff, bytes_accessed=2 * (n * d + d * ff + n * ff), transcendentals=0
+        ),
+        name="up_grad",
+    )(where, a, g)
 
 
 def permutation(move):
@@ -908,6 +969,7 @@
 OVER_X = permutation(lambda z, y, c, x: (z, y, c, 1 - x))
 OVER_Y = permutation(lambda z, y, c, x: (z, 1 - y, c, x))
 OVER_C = permutation(lambda z, y, c, x: (z, y, 1 - c, x))
+OVER_CX = permutation(lambda z, y, c, x: (z, y, 1 - c, 1 - x))
 OVER_Z = [permutation(lambda z, y, c, x, k=k: ((z + k) % 4, y, c, x)) for k in range(4)]
 
 
@@ -920,6 +982,10 @@
     return lax.ppermute(array, ALL, pairs)
 
 
+def plain(array):
+    return with_layout_constraint(array, Layout(major_to_minor=tuple(range(array.ndim))))
+
+
 def tie(*trees):
     return lax.optimization_barrier(trees)
 
@@ -933,7 +999,7 @@
 
 
 def gather_z_line(shard):
-    return lax.all_gather(shard, ALL, axis=0, tiled=False, axis_index_groups=Z_GROUPS)
+    return plain(lax.all_gather(shard, ALL, axis=0, tiled=False, axis_index_groups=Z_GROUPS))
 
 
 def scatter_z_line(array):
@@ -1014,11 +1080,13 @@
     place = (dp // 4, (dp // 2) % 2, dp % 2, seq)
     place_vec = jnp.stack([p.astype(jnp.int32) for p in place])
 
-    def columns(w):
-        return w.reshape(32, w.shape[1] // 1024, 1024).transpose(1, 0, 2)
-
-    one = jnp.concatenate([columns(qkv_weight), dense_weight[None]]).reshape(2, 2, 32, 1024)
-    two = columns(up_weight).reshape(2, 2, 32, 1024)
+    def mixed(*blocks):
+        stacked = jnp.stack(blocks).reshape(len(blocks), 2, 16, 512)
+        return stacked.transpose(1, 0, 2, 3)
+
+    w_in = [qkv_weight[:, 512 * i : 512 * i + 512] for i in range(6)]
+    one = mixed(*w_in[0::2], *w_in[1::2], dense_weight[:, :512], dense_weight[:, 512:])
+    two = up_weight.reshape(32, 4, 1024).transpose(1, 0, 2).reshape(2, 2, 32, 1024)
     three = down_weight.reshape(2, 1, 64, 1024)
 
     slot = dp * SG + seq
@@ -1027,83 +1095,97 @@
     length = jnp.sum(jnp.where(every_seq == my_seq, seq_lengths, 0))
     valid = (jnp.arange(rows, dtype=jnp.int32) < length).astype(f32)
     slopes, slopes_split = slope_table()
-    bias_full = jnp.concatenate([qkv_bias[:width], jnp.zeros((width,), f32), qkv_bias[width:]])
+    no_bias = jnp.zeros((512,), f32)
+    bias0 = jnp.concatenate([qkv_bias[:512], no_bias, qkv_bias[1024:1536]])
+    bias1 = jnp.concatenate([qkv_bias[512:1024], no_bias, qkv_bias[1536:]])
 
     one_z = gather_z(one)
+    one_z, two, tokens, cotangent = tie(one_z, two, tokens, cotangent)
+
+    a, b = halves([p[:, :3] for p in one_z])
+    one_x, one_y = send(a, OVER_X), send(b, OVER_Y)
+    two_z = gather_z_line(two)
+    also_za, also_zb = halves([p[:, 3:] for p in one_z])
+    one_x, one_y, also_za, also_zb, tokens, cotangent = tie(
+        one_x, one_y, also_za, also_zb, tokens, cotangent
+    )
+
+    one_a, one_b = jnp.stack([a, one_x]), jnp.stack([b, one_y])
+    one_xy, one_yx = send(one_a, OVER_Y), send(one_b, OVER_X)
+    one_ca, one_cb = send(one_a, OVER_C), send(one_b, OVER_C)
     center, rsd = moments(tokens.astype(f32))
     a1 = (center * rsd * ln1_gain + ln1_bias).astype(bf16)
     grad_low = cotangent * valid[:, None].astype(bf16)
-    one_z, a1, grad_low, two = tie(one_z, a1, grad_low, two)
-
-    a, b = halves(one_z)
-    one_x, one_y = send(a, OVER_X), send(b, OVER_Y)
-    two_z = gather_z_line(two)
-    one_x, one_y = tie(one_x, one_y)
-
-    one_a, one_b = jnp.stack([a, one_x]), jnp.stack([b, one_y])
-    one_xy, one_yx = send(one_a, OVER_Y), send(one_b, OVER_X)
-    one_ca, one_cb = send(one_a, OVER_C), send(one_b, OVER_C)
-    one_xy, one_yx, one_ca, one_cb, two_z, three = tie(one_xy, one_yx, one_ca, one_cb, two_z, three)
+    one_xy, one_yx, one_ca, one_cb, a1, grad_low = tie(
+        one_xy, one_yx, one_ca, one_cb, a1, grad_low
+    )
     one_cxy, one_cyx = send(one_xy, OVER_C), send(one_yx, OVER_C)
-    a, b = two_z[:, 0], two_z[:, 1]
+    a, b = also_za, also_zb
     one_cxy, one_cyx, a, b, three = tie(one_cxy, one_cyx, a, b, three)
 
-    two_x, two_y = send(a, OVER_X), send(b, OVER_Y)
+    also_x, also_y = send(a, OVER_X), send(b, OVER_Y)
+    pieces = (one_a, one_xy, one_ca, one_cxy, one_b, one_yx, one_cb, one_cyx)
+    qkv0, w0 = qkv_call(place_vec, pieces, a1, bias0, True)
+    qkv0, also_x, also_y, two_z = tie(qkv0, also_x, also_y, two_z)
+    also_a, also_b = jnp.stack([a, also_x]), jnp.stack([b, also_y])
+    also_xy, also_yx = send(also_a, OVER_Y), send(also_b, OVER_X)
+    also_ca, also_cb = send(also_a, OVER_C), send(also_b, OVER_C)
     three_z = gather_z_line(three)
-    pieces = (one_a, one_xy, one_ca, one_cxy, one_b, one_yx, one_cb, one_cyx)
-    qkv, w_one = qkv_call(place_vec, pieces, a1, bias_full)
-    qkv, two_x, two_y = tie(qkv, two_x, two_y)
-
-    two_a, two_b = jnp.stack([a, two_x]), jnp.stack([b, two_y])
-    two_xy, two_yx = send(two_a, OVER_Y), send(two_b, OVER_X)
-    two_ca, two_cb = send(two_a, OVER_C), send(two_b, OVER_C)
-    context, lse = attn_fwd(length, jnp.asarray(slopes), qkv, 0, 8)
-    context, two_xy, two_yx, two_ca, two_cb, three_z = tie(
-        context, two_xy, two_yx, two_ca, two_cb, three_z
-    )
-
+    context0, lse0 = attn_fwd(length, jnp.asarray(slopes), qkv0, 0)
+    context0, also_xy, also_yx, also_ca, also_cb, a1 = tie(
+        context0, also_xy, also_yx, also_ca, also_cb, a1
+    )
+
+    also_cxy, also_cyx = send(also_xy, OVER_C), send(also_yx, OVER_C)
+    also_cxy, also_cyx = tie(also_cxy, also_cyx)
+    pieces = (also_a, also_xy, also_ca, also_cxy, also_b, also_yx, also_cb, also_cyx)
+    two_c = send(two_z, OVER_C)
+    two_x, two_y = plain(send(two_z, OVER_X)), plain(send(two_z, OVER_Y))
+    qkv1, w1 = qkv_call(place_vec, pieces, a1, bias1, True)
+    qkv1, two_c, three_z = tie(qkv1, two_c, three_z)
+    context1, lse1 = attn_fwd(length, jnp.asarray(slopes), qkv1, 4)
+    context0, context1, two_x, two_y, three_z = tie(context0, context1, two_x, two_y, three_z)
+
+    two_xy, two_yx = send(two_x[:, 0], OVER_Y), send(two_y[:, 1], OVER_X)
+    two_cx, two_cy = send(two_x, OVER_C), send(two_y, OVER_C)
+    hidden, a2 = dense_call(context0, context1, w1, tokens, dense_bias, ln2_gain, ln2_bias)
+    a2, two_xy, two_yx, two_cx, two_cy, three_z = tie(a2, two_xy, two_yx, two_cx, two_cy, three_z)
     two_cxy, two_cyx = send(two_xy, OVER_C), send(two_yx, OVER_C)
-    a, b = three_z[:, 0], three_z[:, 1]
-    three_x, three_y = send(a, OVER_X), send(b, OVER_Y)
-    hidden = tokens.astype(f32) + dot(context, w_one[3]) + dense_bias
-    center, rsd = moments(hidden)
-    a2 = (center * rsd * ln2_gain + ln2_bias).astype(bf16)
-    a2, hidden, two_cxy, two_cyx, three_x, three_y = tie(
-        a2, hidden, two_cxy, two_cyx, three_x, three_y
-    )
-
-    up_pieces = (two_a, two_xy, two_ca, two_cxy, two_b, two_yx, two_cb, two_cyx)
-    three_a, three_b = jnp.stack([a, three_x]), jnp.stack([b, three_y])
-    three_xy, three_yx = send(three_a, OVER_Y), send(three_b, OVER_X)
-    three_ca, three_cb = send(three_a, OVER_C), send(three_b, OVER_C)
-    active, slope = up_call(place_vec, up_pieces, a2, up_bias)
-    active, slope, grad_low = tie(active, slope, grad_low)
-
-    down_keep, down_give = down_grad_call(place_vec, active, grad_low)
-    down_keep, down_give, three_xy, three_yx, three_ca, three_cb, grad_low = tie(
-        down_keep, down_give, three_xy, three_yx, three_ca, three_cb, grad_low
+    two_cxy, a2, three_z = tie(two_cxy, a2, three_z)
+
+    three_c = send(three_z, OVER_C)
+    three_x, three_y = plain(send(three_z, OVER_X)), plain(send(three_z, OVER_Y))
+    up_pieces = (two_z, two_x, two_y, two_xy, two_yx, two_c, two_cx, two_cy, two_cxy, two_cyx)
+    u0, slope0 = up_call(place_vec, 0, up_pieces, a2, up_bias)
+    u0, a2, two_cyx, three_c = tie(u0, a2, two_cyx, three_c)
+    up_pieces = (two_z, two_x, two_y, two_xy, two_yx, two_c, two_cx, two_cy, two_cxy, two_cyx)
+    u1, slope1 = up_call(place_vec, 1, up_pieces, a2, up_bias)
+    u0, u1, grad_low, three_x, three_y = tie(u0, u1, grad_low, three_x, three_y)
+    three_xy, three_yx = send(three_x[:, 0], OVER_Y), send(three_y[:, 1], OVER_X)
+    three_cx, three_cy = send(three_x, OVER_C), send(three_y, OVER_C)
+
+    down_keep, down_give = down_grad_call(place_vec, (u0, u1), grad_low)
+    down_keep, down_give, grad_low, three_cx, three_cy, three_xy, three_yx = tie(
+        down_keep, down_give, grad_low, three_cx, three_cy, three_xy, three_yx
     )
     three_cxy, three_cyx = send(three_xy, OVER_C), send(three_yx, OVER_C)
     down_b = jnp.sum(grad_low.astype(f32), axis=0)
-    active, hidden, down_give, three_cxy, three_cyx, down_b = tie(
-        active, hidden, down_give, three_cxy, three_cyx, down_b
-    )
-
-    down_pieces = (
-        three_a, three_xy, three_ca, three_cxy, three_b, three_yx, three_cb, three_cyx
+    down_give, three_cxy, three_cyx, down_b, grad_low = tie(
+        down_give, three_cxy, three_cyx, down_b, grad_low
+    )
+
+    pieces = (
+        three_z, three_x, three_y, three_xy, three_yx,
+        three_c, three_cx, three_cy, three_cxy, three_cyx,
     )
     down_got = send(down_give, OVER_C)
-    block_output = down_call(place_vec, down_pieces, active, hidden, down_bias)
-    block_output, down_got, grad_low = tie(block_output, down_got, grad_low)
-
+    grad_before, up_bias_grad = gate_call(place_vec, pieces, grad_low, (slope0, slope1))
+    grad_before, a2, down_got = tie(grad_before, a2, down_got)
     down = add_low(down_keep, down_got).reshape(4, 2, 2, 2, 64, 1024)
     down = fold_second(down[:, :, :, 0], down[:, :, :, 1], place)
-    grad_before, up_b = gate_call(place_vec, down_pieces, grad_low, slope)
-    grad_before, a2 = tie(grad_before, a2)
     up_keep, up_give = up_grad_call(place_vec, a2, grad_before)
-    grad_before, up_keep, up_give, down = tie(grad_before, up_keep, up_give, down)
-
-    down = fold_third(down, place)
+    grad_before, up_keep, up_give = tie(grad_before, up_keep, up_give)
+
     up_got = send(up_give, OVER_C)
     grad_low_hidden, grad_hidden, sums = norm_up_call(
         place_vec, up_pieces, grad_before, hidden, ln2_gain, grad_low
@@ -1112,69 +1194,83 @@
         grad_low_hidden, grad_hidden, sums, down, up_got
     )
 
-    owner_down = scatter_z_line(both(down))
-    early = jnp.concatenate([sums[2], sums[0], sums[1], up_b.reshape(4096), down_b]).reshape(8, 1024)
-    early = lax.all_gather(early, ALL, axis=0, tiled=False)
+    down = fold_third(down, place)
     up = add_low(up_keep, up_got).reshape(4, 2, 2, 32, 4096)
     up = fold_second(up[..., :2048], up[..., 2048:], place)
-    grad_context = dotnt(grad_low_hidden, w_one[3]).astype(bf16)
-    q0, k0, v0 = attn_bwd(length, jnp.asarray(slopes_split), qkv, context, lse, grad_context, 0, 4)
-    qkv, q0, k0, v0, up, a1 = tie(qkv, q0, k0, v0, up, a1)
-
+    early = jnp.concatenate(
+        [sums[2], sums[0], sums[1], up_bias_grad.reshape(4096), down_b]
+    ).reshape(8, 1024)
+    grad_context = dense_back_call(grad_low_hidden, w1)
+    q0, k0, v0 = attn_bwd(
+        length, jnp.asarray(slopes_split), qkv0, context0, lse0, grad_context, 0
+    )
+    q0, k0, v0, down, up, a1, early = tie(q0, k0, v0, down, up, a1, early)
+
+    owner_down = scatter_z_line(both(down))
     up = fold_third(up, place)
-    third_keep, third_give = columns_call(
+    third_keep, third_give, sums0 = columns_call(
         place_vec,
-        [context, a1],
+        [(context0, context1), (a1,)],
         [(grad_low_hidden, 0), (grad_low_hidden, 1), (q0, 0), (k0, 0), (v0, 0)],
         (0, 0, 1, 1, 1),
-    )
-    third_keep, third_give, qkv = tie(third_keep, third_give, qkv)
-
+        "dense_grad",
+    )
+    third_keep, third_give, qkv1, up = tie(third_keep, third_give, qkv1, up)
     third_got = send(third_give, OVER_C)
-    q1, k1, v1 = attn_bwd(length, jnp.asarray(slopes_split), qkv, context, lse, grad_context, 4, 4)
-    q1, k1, v1, third_got, up = tie(q1, k1, v1, third_got, up)
-
-    owner_up = scatter_z_line(both(up))
+    up = both(up)
+    third_got, up, qkv1 = tie(third_got, up, qkv1)
+
+    owner_up = scatter_z_line(up)
     third = add_low(third_keep, third_got).reshape(4, 2, 2, 32, 2560)
     third = fold_second(third[..., :1280], third[..., 1280:], place)
-    last_keep, last_give = columns_call(place_vec, [a1], [(q1, 0), (k1, 0), (v1, 0)], (0, 0, 0))
-    last_keep, last_give, q0, q1, k1, v1 = tie(last_keep, last_give, q0, q1, k1, v1)
-
+    q1, k1, v1 = attn_bwd(
+        length, jnp.asarray(slopes_split), qkv1, context1, lse1, grad_context, 4
+    )
+    q1, k1, v1, third = tie(q1, k1, v1, third)
+
+    third = fold_third(third, place)
+    last_keep, last_give, sums1 = columns_call(
+        place_vec, [(a1,)], [(q1, 0), (k1, 0), (v1, 0)], (0, 0, 0), "heads_grad"
+    )
+    last_keep, last_give, third, q0 = tie(last_keep, last_give, third, q0)
     last_got = send(last_give, OVER_C)
-    part = part_call([q0, k0, v0], w_one)
-    part, last_got, third = tie(part, last_got, third)
-    third = fold_third(third, place)
+    third = both(third)
+    last_got, third, q0, tokens = tie(last_got, third, q0, tokens)
+
     last = add_low(last_keep, last_got).reshape(4, 2, 2, 32, 1536)
     last = fold_second(last[..., :768], last[..., 768:], place)
-    qkv_b = [jnp.sum(g.astype(f32), axis=0) for g in (q0, q1, v0, v1)]
-    token_grad, sums = norm_qkv_call([q1, k1, v1], w_one, tokens, ln1_gain, grad_hidden, part)
-    token_grad, sums, last, third = tie(token_grad, sums, last, third)
+    third = scatter_z_line(third)
+    token_grad, sums = norm_qkv_call(
+        [q0, k0, v0, q1, k1, v1], w0, w1, tokens, ln1_gain, grad_hidden
+    )
+    token_grad, sums, last, u0 = tie(token_grad, sums, last, u0)
 
     last = fold_third(last, place)
-    third = fold_z(third, place)
-    late = jnp.concatenate(qkv_b + [sums[0], sums[1]]).reshape(4, 1024)
-    late_c = send(late, OVER_C)
-    last, third, late, late_c = tie(last, third, late, late_c)
-
+    vectors = [sums0[0, 1024:1536], sums1[0, :512], sums0[0, 2048:], sums1[0, 1024:]]
+    late = jnp.concatenate(vectors + [sums[0], sums[1]]).reshape(4, 1024)
+    late = jnp.concatenate([late, early])
+    late_near = [send(late, pairs) for pairs in (OVER_C, OVER_X, OVER_CX)]
+    block_output = down_call(place_vec, pieces, (u0, u1), hidden, down_bias)
+    block_output, last, late, late_near = tie(block_output, last, late, late_near)
+
+    late = late + sum(late_near)
+    late_y = send(late, OVER_Y)
     last = fold_z(last, place)
-    late = late + late_c
-    late_x = send(late, OVER_X)
-    third = total(third)
+    late, late_y, owner_up, owner_down, third = tie(late, late_y, owner_up, owner_down, third)
+    late = late + late_y
+    late_z = [send(late, OVER_Z[k]) for k in (1, 2, 3)]
+    third = third.astype(f32)
     third = jnp.concatenate([third[0], third[1]], axis=1)
-    last, late, late_x, third, owner_up, owner_down, early = tie(
-        last, late, late_x, third, owner_up, owner_down, early
-    )
-    late = late + late_x
-    late_y = send(late, OVER_Y)
-    early = jnp.sum(early, axis=0)
     owner_down = owner_down.astype(f32).reshape(128, 1024)
     owner_up = owner_up.astype(f32)
     owner_up = jnp.concatenate([owner_up[0], owner_up[1]], axis=1)
-    late, late_y = tie(late, late_y)
-    late = late + late_y
-    late = late + send(late, OVER_Z[1]) + send(late, OVER_Z[2]) + send(late, OVER_Z[3])
+    late, late_z, last, owner_up, owner_down, third = tie(
+        late, late_z, last, owner_up, owner_down, third
+    )
     last = total(last)
     last = jnp.concatenate([last[0], last[1]], axis=1)
+    late = late + sum(late_z)
+    early = late[4:]
     owner_qkv = jnp.concatenate(
         [
             part

time: 488 us -> 456 us (0.934)
  waiting for transfers between devices: 76.1 us -> 38.5 us
  local copies, waits for them, and re-layouts: 35.9 us -> 48.9 us
  matrix products: 10.1 us -> 0 us
    ppermute x59 -> x67, waiting for transfers between devices: 76 us -> 37.6 us  [send(): return lax.ppermute(array, ALL, pairs)]
    unnamed x145 -> x200, local copies, waits for them, and re-layouts: 12.5 us -> 25 us
    dot_general x2 -> x0, matrix products: 10.1 us -> none  [the longest x1 5.99 us: dotnt(): return lax.dot_general(a, b, NT, preferred_element_type=f32)]
    another operation x10 -> x11, other arithmetic: 6.12 us -> 10.3 us  [both(): return jnp.stack([add_low(*p) for p in pair], axis=1)]
    pallas_call x1 -> x2, Pallas kernels: 24.8 us -> 27.5 us  [attn_fwd(): pl.pallas_call(attn_fwd_kernel, grid_spec=pltpu.PrefetchScalarGridSpec(nu...]
    ppermute x59 -> x67, starting transfers between devices: 62.5 us -> 60 us  [send(): return lax.ppermute(array, ALL, pairs)]
    pallas_call x8 -> x11, Pallas kernels: 114 us -> 114 us  [the longest x2 26.4 us: up_call(): pl.pallas_call(functools.partial(up_kernel, half), grid_spec=pltpu.Prefet...]
  transfers between devices with their start and end apart: 64 -> 72, of which waited for: 18 -> 20; matrix products, arithmetic and copies ran while one was open for 14% -> 13% of each run, Pallas kernels for 49% -> 50%
where the time goes in v3:
time: 456 us; the launch traced here: 450 us
  Pallas kernels  239 us (52%)
  starting transfers between devices  61 us (13%)
  local copies, waits for them, and re-layouts  48.9 us (11%)
  other arithmetic  46.7 us (10%)
  waiting for transfers between devices  38.5 us (8%)
  between operations  15.5 us (3%)
    ppermute x67, starting transfers between devices, send(): return lax.ppermute(array, ALL, pairs)  60 us
    pallas_call x2, Pallas kernels, attn_bwd(): pl.pallas_call(attn_bwd_kernel, grid_spec=pltpu.PrefetchScalarGridSpec(nu...  39.9 us
    ppermute x67, waiting for transfers between devices, send(): return lax.ppermute(array, ALL, pairs)  37.6 us
    pallas_call x2, Pallas kernels, attn_fwd(): pl.pallas_call(attn_fwd_kernel, grid_spec=pltpu.PrefetchScalarGridSpec(nu...  27.5 us
    pallas_call x2, Pallas kernels, up_call(): pl.pallas_call(functools.partial(up_kernel, half), grid_spec=pltpu.Prefet...  26.4 us
    unnamed x200, local copies, waits for them, and re-layouts  25 us
    pallas_call x1, Pallas kernels, norm_up_call(): pl.pallas_call(norm_up_kernel, grid_spec=pltpu.PrefetchScalarGridSpec(num...  23.2 us
    pallas_call x2, Pallas kernels, qkv_call(): pl.pallas_call(functools.partial(qkv_kernel, turned), grid_spec=pltpu.Pre...  18.9 us
  transfers between devices with their start and end apart: 72, of which 20 were waited for; matrix products, arithmetic and copies ran while one was open for 13% of the time, Pallas kernels for 50%

profile of v3, /device:TPU:0, one launch (start us, length us, event | category | flops | bytes accessed | tf_op | source)
XLA Modules:
  0.0 450.1 jit_solution(15724312143147202773)
XLA Ops:
  9.0 3.1 collective-permute-start
  12.0 2.6 collective-permute-start.1
  21.5 10.3 %collective-permute-done.1 = bf16[2,8,16,512]{3,2,1,0:T(8,128)(2,1)S(1)} collective-permute-done((bf16[2,8,16,512]{3,2,1,0:T(8,128)(2,1)S(1)}, bf16[2,8,16,512]{3,2,1,0:T(8,128)(2,1)S(1)}, u32[]{:S(2)}, u32[]{:S(2)}) %collective-permute-start.1) | collective-permute-done | bytes 262176 | tf_op jit(solution)/shard_map/ppermute | solution.py:982
  36.5 3.1 collective-permute-done.4
  39.6 2.0 collective-permute-done.3
  48.5 2.1 fusion.5.refs_8_.refs_2_.refs_0_
  52.5 4.2 collective-permute-done.5.refs_1_
  61.4 9.1 %qkv.2 = (bf16[1024,1536]{1,0:T(8,128)(2,1)}, bf16[3,1024,512]{2,1,0:T(8,128)(2,1)}) custom-call(s32[4]{0:T(128)} %pad_add_fusion.place_ref.where_ref, bf16[2,4,3,16,512]{4,3,2,1,0:T(8,128)(2,1)} %copy-done.61, bf16[2,4,3,16,512]{4,3,2,1,0:T(8,128)(2,1)} %copy-done.82, bf16[2,4,3,16,512]{4,3,2,1,0:T(8,128)(2,1)} %copy-done.83, ...), custom_call_target="tpu_custom_call" | custom-call | flops 3221225472 | bytes 13631488 | tf_op jit(solution)/shard_map/qkv/pallas_call | solution.py:479
  70.6 2.0 pad_maximum_fusion.3.refs_4_
  78.7 13.7 %attn_fwd.2 = (bf16[1024,512]{1,0:T(8,128)(2,1)}, f32[1024,512]{1,0:T(8,128)}) custom-call(s32[2]{0:T(128)} %get-tuple-element.509.len_ref, f32[16]{0:T(128)} %constant.191.clone.slope_ref, bf16[1024,1536]{1,0:T(8,128)(2,1)} %get-tuple-element.235.q_ref.k_ref.v_ref, bf16[1024,1536]{1,0:T(8,128)(2,1)} %get-tuple-element.235.q_ref.k_ref.v_ref, ...), custom_call_target="tpu_custom_call" | custom-call | flops 5368709120 | bytes 6291456 | tf_op jit(solution)/shard_map/attn_fwd/pallas_call | solution.py:67
  96.4 9.9 %qkv.3 = (bf16[1024,1536]{1,0:T(8,128)(2,1)}, bf16[5,1024,512]{2,1,0:T(8,128)(2,1)}) custom-call(s32[4]{0:T(128)} %pad_add_fusion.place_ref.where_ref, bf16[2,4,5,16,512]{4,3,2,1,0:T(8,128)(2,1)} %copy-done.59, bf16[2,4,5,16,512]{4,3,2,1,0:T(8,128)(2,1)} %collective-permute-done.13.refs_1_, bf16[2,4,5,16,512]{4,3,2,1,0:T(8,128)(2,1)} %collective-permute-done.15.refs_2_, ...), custom_call_target="tpu_custom_call" | custom-call | flops 3221225472 | bytes 13631488 | tf_op jit(solution)/shard_map/qkv/pallas_call | solution.py:479
  107.1 13.8 %attn_fwd.3 = (bf16[1024,512]{1,0:T(8,128)(2,1)}, f32[1024,512]{1,0:T(8,128)}) custom-call(s32[2]{0:T(128)} %get-tuple-element.510.len_ref, f32[16]{0:T(128)} %constant.191.clone.slope_ref, bf16[1024,1536]{1,0:T(8,128)(2,1)} %get-tuple-element.339.q_ref.k_ref.v_ref, bf16[1024,1536]{1,0:T(8,128)(2,1)} %get-tuple-element.339.q_ref.k_ref.v_ref, ...), custom_call_target="tpu_custom_call" | custom-call | flops 5368709120 | bytes 6291456 | tf_op jit(solution)/shard_map/attn_fwd/pallas_call | solution.py:67
  129.2 5.6 %dense.1 = (f32[1024,1024]{1,0:T(8,128)S(1)}, bf16[1024,1024]{1,0:T(8,128)(2,1)S(1)}) custom-call(bf16[1024,512]{1,0:T(8,128)(2,1)S(1)} %copy-done.16, bf16[1024,512]{1,0:T(8,128)(2,1)S(1)} %copy-done.13, bf16[5,1024,512]{2,1,0:T(8,128)(2,1)} %get-tuple-element.255.w0_ref.w1_ref.refs_7_, bf16[5,1024,512]{2,1,0:T(8,128)(2,1)} %get-tuple-element.255.w0_ref.w1_ref.refs_7_, ...), custom_call_target="tpu_custom_call" | custom-call | flops 2147483648 | bytes 12582912 | tf_op jit(solution)/shard_map/dense/pallas_call | solution.py:521
  143.0 13.1 %up.2 = (bf16[1024,2048]{1,0:T(8,128)(2,1)S(1)}, bf16[1024,2048]{1,0:T(8,128)(2,1)}) custom-call(s32[4]{0:T(128)S(1)} %copy-done.22, bf16[4,2,2,32,1024]{4,3,2,1,0:T(8,128)(2,1)} %bitcast.22.refs_0_, bf16[4,2,2,32,1024]{4,3,2,1,0:T(8,128)(2,1)} %collective-permute-done.20.refs_1_, bf16[4,2,2,32,1024]{4,3,2,1,0:T(8,128)(2,1)} %collective-permute-done.21.refs_2_, ...), custom_call_target="tpu_custom_call" | custom-call | flops 4294967296 | bytes 14680064 | tf_op jit(solution)/shard_map/up/pallas_call | solution.py:580
  157.2 13.3 %up.3 = (bf16[1024,2048]{1,0:T(8,128)(2,1)S(1)}, bf16[1024,2048]{1,0:T(8,128)(2,1)}) custom-call(s32[4]{0:T(128)S(1)} %copy-done.22, bf16[4,2,2,32,1024]{4,3,2,1,0:T(8,128)(2,1)} %bitcast.22.refs_0_, bf16[4,2,2,32,1024]{4,3,2,1,0:T(8,128)(2,1)} %collective-permute-done.20.refs_1_, bf16[4,2,2,32,1024]{4,3,2,1,0:T(8,128)(2,1)} %collective-permute-done.21.refs_2_, ...), custom_call_target="tpu_custom_call" | custom-call | flops 4294967296 | bytes 14680064 | tf_op jit(solution)/shard_map/up/pallas_call | solution.py:580
  170.5 2.0 copy-done.49
  176.4 13.4 %down_grad.1 = (bf16[8,256,1024]{2,1,0:T(8,128)(2,1)S(1)}, bf16[8,256,1024]{2,1,0:T(8,128)(2,1)S(1)}) custom-call(s32[4]{0:T(128)S(1)} %copy-done.22, bf16[1024,2048]{1,0:T(8,128)(2,1)} %copy-done.48, bf16[1024,2048]{1,0:T(8,128)(2,1)} %copy-done.49, bf16[1024,1024]{1,0:T(8,128)(2,1)S(1)} %copy-done.2), custom_call_target="tpu_custom_call" | custom-call | flops 8589934592 | bytes 18874368 | tf_op jit(solution)/shard_map/down_grad/pallas_call | solution.py:618
  195.3 17.3 %gate.1 = (bf16[1024,4096]{1,0:T(8,128)(2,1)}, f32[1,4096]{1,0:T(1,128)}) custom-call(s32[4]{0:T(128)} %pad_add_fusion.place_ref.where_ref, bf16[4,2,1,64,1024]{4,3,2,1,0:T(8,128)(2,1)} %bitcast.27.refs_0_, bf16[4,2,1,64,1024]{4,3,2,1,0:T(8,128)(2,1)} %copy-done.66, bf16[4,2,1,64,1024]{4,3,2,1,0:T(8,128)(2,1)} %collective-permute-done.30.refs_2_, ...), custom_call_target="tpu_custom_call" | custom-call | flops 8589934592 | bytes 27262976 | tf_op jit(solution)/shard_map/gate/pallas_call | solution.py:725
  212.7 14.7 %up_grad.1 = (bf16[8,64,4096]{2,1,0:T(8,128)(2,1)S(1)}, bf16[8,64,4096]{2,1,0:T(8,128)(2,1)}) custom-call(s32[4]{0:T(128)S(1)} %copy-done.23, bf16[1024,1024]{1,0:T(8,128)(2,1)S(1)} %get-tuple-element.299.refs_8_.a_ref, bf16[1024,4096]{1,0:T(8,128)(2,1)} %get-tuple-element.302.g_ref.refs_10_), custom_call_target="tpu_custom_call" | custom-call | flops 8589934592 | bytes 18874368 | tf_op jit(solution)/shard_map/up_grad/pallas_call | solution.py:941
  229.4 5.6 %add_convert_fusion.1 = bf16[8,256,1024]{2,1,0:T(8,128)(2,1)S(1)} fusion(bf16[8,256,1024]{2,1,0:T(8,128)(2,1)} %collective-permute-done.37, bf16[8,256,1024]{2,1,0:T(8,128)(2,1)} %copy-done.5), kind=kLoop, calls=%fused_computation.1 | loop fusion | flops 8388608 | bytes 12582912 | tf_op jit(solution)/shard_map/convert_element_type | solution.py:1010
  240.4 23.2 %norm_up.1 = (bf16[1024,1024]{1,0:T(8,128)(2,1)}, f32[1024,1024]{1,0:T(8,128)}, f32[8,1024]{1,0:T(8,128)}) custom-call(s32[4]{0:T(128)} %pad_add_fusion.place_ref.where_ref, bf16[4,2,2,32,1024]{4,3,2,1,0:T(8,128)(2,1)} %bitcast.22.refs_0_, bf16[4,2,2,32,1024]{4,3,2,1,0:T(8,128)(2,1)} %collective-permute-done.20.refs_1_, ...), custom_call_target="tpu_custom_call" | custom-call | flops 8589934592 | bytes 33554432 | tf_op jit(solution)/shard_map/norm_up/pallas_call | solution.py:815
  264.3 4.1 add_convert_fusion
  278.4 3.0 dense_back.1.do_ref
  282.8 20.0 %attn_bwd.2 = (bf16[1024,512]{1,0:T(8,128)(2,1)S(1)}, bf16[1024,512]{1,0:T(8,128)(2,1)S(1)}, bf16[1024,512]{1,0:T(8,128)(2,1)S(1)}) custom-call(s32[2]{0:T(128)S(1)} %copy-done.26, f32[48]{0:T(128)S(1)} %copy-done.35, bf16[1024,1536]{1,0:T(8,128)(2,1)} %get-tuple-element.235.q_ref.k_ref.v_ref, bf16[1024,1536]{1,0:T(8,128)(2,1)} %get-tuple-element.235.q_ref.k_ref.v_ref, ...), custom_call_target="tpu_custom_call" | custom-call | flops 13421772800 | bytes 10485760 | tf_op jit(solution)/shard_map/attn_bwd/pallas_call | solution.py:136
  314.3 8.6 %dense_grad.1 = (bf16[8,64,2560]{2,1,0:T(8,128)(2,1)S(1)}, bf16[8,64,2560]{2,1,0:T(8,128)(2,1)}, f32[1,2560]{1,0:T(1,128)S(1)}) custom-call(s32[4]{0:T(128)S(1)} %copy-done.24, bf16[1024,512]{1,0:T(8,128)(2,1)S(1)} %copy-done.18, bf16[1024,512]{1,0:T(8,128)(2,1)S(1)} %copy-done.14, bf16[1024,1024]{1,0:T(8,128)(2,1)S(1)} %copy-done.9, ...), custom_call_target="tpu_custom_call" | custom-call | flops 5368709120 | bytes 14680064 | tf_op jit(solution)/shard_map/dense_grad/pallas_call | solution.py:908
  333.0 2.4 add_convert_fusion.2
  337.7 19.9 %attn_bwd.3 = (bf16[1024,512]{1,0:T(8,128)(2,1)S(1)}, bf16[1024,512]{1,0:T(8,128)(2,1)S(1)}, bf16[1024,512]{1,0:T(8,128)(2,1)S(1)}) custom-call(s32[2]{0:T(128)S(1)} %copy-done.25, f32[48]{0:T(128)S(1)} %copy-done.35, bf16[1024,1536]{1,0:T(8,128)(2,1)} %get-tuple-element.339.q_ref.k_ref.v_ref, bf16[1024,1536]{1,0:T(8,128)(2,1)} %get-tuple-element.339.q_ref.k_ref.v_ref, ...), custom_call_target="tpu_custom_call" | custom-call | flops 13421772800 | bytes 10485760 | tf_op jit(solution)/shard_map/attn_bwd/pallas_call | solution.py:136
  365.9 5.6 %heads_grad.1 = (bf16[8,64,1536]{2,1,0:T(8,128)(2,1)S(1)}, bf16[8,64,1536]{2,1,0:T(8,128)(2,1)}, f32[1,1536]{1,0:T(1,128)S(1)}) custom-call(s32[4]{0:T(128)S(1)} %copy-done.24, bf16[1024,1024]{1,0:T(8,128)(2,1)S(1)} %copy-done.10, bf16[1024,512]{1,0:T(8,128)(2,1)S(1)} %copy-done.43, bf16[1024,512]{1,0:T(8,128)(2,1)S(1)} %copy-done.45, ...), custom_call_target="tpu_custom_call" | custom-call | flops 3221225472 | bytes 10485760 | tf_op jit(solution)/shard_map/heads_grad/pallas_call | solution.py:908
  379.3 17.9 %norm_qkv.1 = (bf16[1024,1024]{1,0:T(8,128)(2,1)}, f32[8,1024]{1,0:T(8,128)}) custom-call(bf16[1024,512]{1,0:T(8,128)(2,1)} %copy-done.36, bf16[1024,512]{1,0:T(8,128)(2,1)} %copy-done.38, bf16[1024,512]{1,0:T(8,128)(2,1)} %copy-done.40, bf16[1024,512]{1,0:T(8,128)(2,1)} %copy-done.42, bf16[1024,512]{1,0:T(8,128)(2,1)} %copy-done.44, ...), custom_call_target="tpu_custom_call" | custom-call | flops 6442450944 | bytes 23068672 | tf_op jit(solution)/shard_map/norm_qkv/pallas_call | solution.py:861
  403.1 17.5 %down.1 = bf16[1024,1024]{1,0:T(8,128)(2,1)} custom-call(s32[4]{0:T(128)} %pad_add_fusion.place_ref.where_ref, bf16[4,2,1,64,1024]{4,3,2,1,0:T(8,128)(2,1)} %bitcast.27.refs_0_, bf16[4,2,1,64,1024]{4,3,2,1,0:T(8,128)(2,1)} %copy-done.66, bf16[4,2,1,64,1024]{4,3,2,1,0:T(8,128)(2,1)} %collective-permute-done.30.refs_2_, bf16[4,1,64,1024]{3,2,1,0:T(8,128)(2,1)} %copy-done.77, ...), custom_call_target="tpu_custom_call" | custom-call | flops 8589934592 | bytes 23068672 | tf_op jit(solution)/shard_map/down/pallas_call | solution.py:674
  421.5 5.4 %collective-permute-start.64 = (bf16[2,32,768]{2,1,0:T(8,128)(2,1)S(1)}, bf16[2,32,768]{2,1,0:T(8,128)(2,1)S(1)}, u32[]{:S(2)}, u32[]{:S(2)}) collective-permute-start(bf16[2,32,768]{2,1,0:T(8,128)(2,1)S(1)} %get-tuple-element.450), channel_id=1, source_target_pairs={{0,8},{1,9},{2,10},{3,11},{4,12},{5,13},{6,14},{7,15},{8,16},{9,17... | collective-permute-start | bytes 294920 | tf_op jit(solution)/shard_map/ppermute | solution.py:982
  437.1 3.5 collective-permute-done.62
  (443 shorter events, 142.9 us)
Async XLA Ops:
  7.2 63.4 %all-gather.5.cloned.1.call-start = ((), (), s32[]{:S(2)}) async-start(), calls=%async_computation.6 | async-start | bytes 1310720 | tf_op jit(solution)/shard_map/all_gather | solution.py:1002
  12.0 19.7 %collective-permute-start.1 = (bf16[2,8,16,512]{3,2,1,0:T(8,128)(2,1)S(1)}, bf16[2,8,16,512]{3,2,1,0:T(8,128)(2,1)S(1)}, u32[]{:S(2)}, u32[]{:S(2)}) collective-permute-start(bf16[2,8,16,512]{3,2,1,0:T(8,128)(2,1)S(1)} %bitcast.217), channel_id=1, source_target_pairs={{0,16},{1,17},{2,18},{3,19},{4,20},{5,21},{6,22},{7,23},{8,24},{9,... | collective-permute-start | bytes 786440 | tf_op jit(solution)/shard_map/ppermute | solution.py:982
  36.3 70.8 %all-gather.7.cloned.1.call-start = ((), (), s32[]{:S(2)}) async-start(), calls=%async_computation.7 | async-start | bytes 1310720 | tf_op jit(solution)/shard_map/all_gather | solution.py:1002
  72.6 19.8 %collective-permute-start.14 = (bf16[2,4,5,16,512]{4,3,2,1,0:T(8,128)(2,1)}, bf16[2,4,5,16,512]{4,3,2,1,0:T(8,128)(2,1)}, u32[]{:S(2)}, u32[]{:S(2)}) collective-permute-start(bf16[2,4,5,16,512]{4,3,2,1,0:T(8,128)(2,1)} %pad_maximum_fusion.3.refs_4_), channel_id=1, source_target_pairs={{0,1},{1,0},{2,3},{3,2},{4,5},{5,4},{6,7},{7,6},{8,9},{9,8},{10,11... | collective-permute-start | bytes 1966088 | tf_op jit(solution)/shard_map/ppermute | solution.py:982
  74.0 18.3 %collective-permute-start.16 = (bf16[2,4,5,16,512]{4,3,2,1,0:T(8,128)(2,1)}, bf16[2,4,5,16,512]{4,3,2,1,0:T(8,128)(2,1)}, u32[]{:S(2)}, u32[]{:S(2)}) collective-permute-start(bf16[2,4,5,16,512]{4,3,2,1,0:T(8,128)(2,1)} %pad_maximum_fusion.3.refs_4_), channel_id=1, source_target_pairs={{0,2},{1,3},{2,0},{3,1},{4,6},{5,7},{6,4},{7,5},{8,10},{9,11},{10,... | collective-permute-start | bytes 1966088 | tf_op jit(solution)/shard_map/ppermute | solution.py:982
  76.9 352.4 %reduce-scatter.6.cloned.1.call-start = ((), (), s32[]{:S(2)}) async-start(), calls=%async_computation.4 | async-start | bytes 1310720 | tf_op jit(solution)/shard_map/reduce_scatter | solution.py:1006
  78.4 28.7 %collective-permute-start.19 = (bf16[4,2,2,32,1024]{4,3,2,1,0:T(8,128)(2,1)}, bf16[4,2,2,32,1024]{4,3,2,1,0:T(8,128)(2,1)}, u32[]{:S(2)}, u32[]{:S(2)}) collective-permute-start(bf16[4,2,2,32,1024]{4,3,2,1,0:T(8,128)(2,1)} %bitcast.22.refs_0_), channel_id=1, source_target_pairs={{0,2},{1,3},{2,0},{3,1},{4,6},{5,7},{6,4},{7,5},{8,10},{9,11},{10,... | collective-permute-start | bytes 3145736 | tf_op jit(solution)/shard_map/ppermute | solution.py:982
  93.0 27.9 %collective-permute-start.20 = (bf16[4,2,2,32,1024]{4,3,2,1,0:T(8,128)(2,1)}, bf16[4,2,2,32,1024]{4,3,2,1,0:T(8,128)(2,1)}, u32[]{:S(2)}, u32[]{:S(2)}) collective-permute-start(bf16[4,2,2,32,1024]{4,3,2,1,0:T(8,128)(2,1)} %bitcast.22.refs_0_), channel_id=1, source_target_pairs={{0,1},{1,0},{2,3},{3,2},{4,5},{5,4},{6,7},{7,6},{8,9},{9,8},{10,11... | collective-permute-start | bytes 3145736 | tf_op jit(solution)/shard_map/ppermute | solution.py:982
  93.5 27.4 %collective-permute-start.21 = (bf16[4,2,2,32,1024]{4,3,2,1,0:T(8,128)(2,1)}, bf16[4,2,2,32,1024]{4,3,2,1,0:T(8,128)(2,1)}, u32[]{:S(2)}, u32[]{:S(2)}) collective-permute-start(bf16[4,2,2,32,1024]{4,3,2,1,0:T(8,128)(2,1)} %bitcast.22.refs_0_), channel_id=1, source_target_pairs={{0,4},{1,5},{2,6},{3,7},{4,0},{5,1},{6,2},{7,3},{8,12},{9,13},{10,... | collective-permute-start | bytes 3145736 | tf_op jit(solution)/shard_map/ppermute | solution.py:982
  141.0 31.5 %collective-permute-start.29 = (bf16[4,2,1,64,1024]{4,3,2,1,0:T(8,128)(2,1)}, bf16[4,2,1,64,1024]{4,3,2,1,0:T(8,128)(2,1)S(1)}, u32[]{:S(2)}, u32[]{:S(2)}) collective-permute-start(bf16[4,2,1,64,1024]{4,3,2,1,0:T(8,128)(2,1)} %bitcast.27.refs_0_), channel_id=1, source_target_pairs={{0,1},{1,0},{2,3},{3,2},{4,5},{5,4},{6,7},{7,6},{8,9},{9,8},{10,11... | collective-permute-start | bytes 3145736 | tf_op jit(solution)/shard_map/ppermute | solution.py:982
  142.4 30.1 %collective-permute-start.30 = (bf16[4,2,1,64,1024]{4,3,2,1,0:T(8,128)(2,1)}, bf16[4,2,1,64,1024]{4,3,2,1,0:T(8,128)(2,1)}, u32[]{:S(2)}, u32[]{:S(2)}) collective-permute-start(bf16[4,2,1,64,1024]{4,3,2,1,0:T(8,128)(2,1)} %bitcast.27.refs_0_), channel_id=1, source_target_pairs={{0,4},{1,5},{2,6},{3,7},{4,0},{5,1},{6,2},{7,3},{8,12},{9,13},{10,... | collective-permute-start | bytes 3145736 | tf_op jit(solution)/shard_map/ppermute | solution.py:982
  172.5 19.3 %collective-permute-start.31 = (bf16[4,2,1,64,1024]{4,3,2,1,0:T(8,128)(2,1)S(1)}, bf16[4,2,1,64,1024]{4,3,2,1,0:T(8,128)(2,1)S(1)}, u32[]{:S(2)}, u32[]{:S(2)}) collective-permute-start(bf16[4,2,1,64,1024]{4,3,2,1,0:T(8,128)(2,1)S(1)} %collective-permute-done.29.refs_1_), channel_id=1, source_target_pairs={{0,2},{1,3},{2,0},{3,1},{4,6},{5,7},{6,4},{7,5},{8,10},{9,11},{10,... | collective-permute-start | bytes 3145736 | tf_op jit(solution)/shard_map/ppermute | solution.py:982
  173.1 18.7 %collective-permute-start.32 = (bf16[4,2,1,64,1024]{4,3,2,1,0:T(8,128)(2,1)}, bf16[4,2,1,64,1024]{4,3,2,1,0:T(8,128)(2,1)S(1)}, u32[]{:S(2)}, u32[]{:S(2)}) collective-permute-start(bf16[4,2,1,64,1024]{4,3,2,1,0:T(8,128)(2,1)} %collective-permute-done.30.refs_2_), channel_id=1, source_target_pairs={{0,2},{1,3},{2,0},{3,1},{4,6},{5,7},{6,4},{7,5},{8,10},{9,11},{10,... | collective-permute-start | bytes 3145736 | tf_op jit(solution)/shard_map/ppermute | solution.py:982
  173.2 18.6 %collective-permute-start.33 = (bf16[4,1,64,1024]{3,2,1,0:T(8,128)(2,1)S(1)}, bf16[4,1,64,1024]{3,2,1,0:T(8,128)(2,1)S(1)}, u32[]{:S(2)}, u32[]{:S(2)}) collective-permute-start(bf16[4,1,64,1024]{3,2,1,0:T(8,128)(2,1)S(1)} %slice_bitcast_fusion.1), channel_id=1, source_target_pairs={{0,4},{1,5},{2,6},{3,7},{4,0},{5,1},{6,2},{7,3},{8,12},{9,13},{10,... | collective-permute-start | bytes 1572872 | tf_op jit(solution)/shard_map/ppermute | solution.py:982
  229.3 35.0 %collective-permute-start.40 = (bf16[8,64,4096]{2,1,0:T(8,128)(2,1)}, bf16[8,64,4096]{2,1,0:T(8,128)(2,1)}, u32[]{:S(2)}, u32[]{:S(2)}) collective-permute-start(bf16[8,64,4096]{2,1,0:T(8,128)(2,1)} %get-tuple-element.309), channel_id=1, source_target_pairs={{0,2},{1,3},{2,0},{3,1},{4,6},{5,7},{6,4},{7,5},{8,10},{9,11},{10,... | collective-permute-start | bytes 12582920 | tf_op jit(solution)/shard_map/ppermute | solution.py:982
  237.2 26.5 %collective-permute-start.39 = (bf16[4,2,64,1024]{3,2,1,0:T(8,128)(2,1)}, bf16[4,2,64,1024]{3,2,1,0:T(8,128)(2,1)S(1)}, u32[]{:S(2)}, u32[]{:S(2)}) collective-permute-start(bf16[4,2,64,1024]{3,2,1,0:T(8,128)(2,1)} %get-tuple-element.420), channel_id=1, source_target_pairs={{0,4},{1,5},{2,6},{3,7},{4,0},{5,1},{6,2},{7,3},{8,12},{9,13},{10,... | collective-permute-start | bytes 3145736 | tf_op jit(solution)/shard_map/ppermute | solution.py:982
  239.0 25.4 %collective-permute-start.38 = (bf16[4,2,64,1024]{3,2,1,0:T(8,128)(2,1)}, bf16[4,2,64,1024]{3,2,1,0:T(8,128)(2,1)S(1)}, u32[]{:S(2)}, u32[]{:S(2)}) collective-permute-start(bf16[4,2,64,1024]{3,2,1,0:T(8,128)(2,1)} %get-tuple-element.422), channel_id=1, source_target_pairs={{0,1},{1,0},{2,3},{3,2},{4,5},{5,4},{6,7},{7,6},{8,9},{9,8},{10,11... | collective-permute-start | bytes 3145736 | tf_op jit(solution)/shard_map/ppermute | solution.py:982
  269.9 38.5 %collective-permute-start.44 = (bf16[4,2,32,2048]{3,2,1,0:T(8,128)(2,1)}, bf16[4,2,32,2048]{3,2,1,0:T(8,128)(2,1)}, u32[]{:S(2)}, u32[]{:S(2)}) collective-permute-start(bf16[4,2,32,2048]{3,2,1,0:T(8,128)(2,1)} %get-tuple-element.416), channel_id=1, source_target_pairs={{0,4},{1,5},{2,6},{3,7},{4,0},{5,1},{6,2},{7,3},{8,12},{9,13},{10,... | collective-permute-start | bytes 3145736 | tf_op jit(solution)/shard_map/ppermute | solution.py:982
  272.6 35.9 %collective-permute-start.43 = (bf16[4,2,32,2048]{3,2,1,0:T(8,128)(2,1)}, bf16[4,2,32,2048]{3,2,1,0:T(8,128)(2,1)S(1)}, u32[]{:S(2)}, u32[]{:S(2)}) collective-permute-start(bf16[4,2,32,2048]{3,2,1,0:T(8,128)(2,1)} %get-tuple-element.418), channel_id=1, source_target_pairs={{0,1},{1,0},{2,3},{3,2},{4,5},{5,4},{6,7},{7,6},{8,9},{9,8},{10,11... | collective-permute-start | bytes 3145736 | tf_op jit(solution)/shard_map/ppermute | solution.py:982
  275.6 32.9 %collective-permute-start.42 = (bf16[4,64,1024]{2,1,0:T(8,128)(2,1)}, bf16[4,64,1024]{2,1,0:T(8,128)(2,1)}, u32[]{:S(2)}, u32[]{:S(2)}) collective-permute-start(bf16[4,64,1024]{2,1,0:T(8,128)(2,1)} %get-tuple-element.434), channel_id=1, source_target_pairs={{0,1},{1,0},{2,3},{3,2},{4,5},{5,4},{6,7},{7,6},{8,9},{9,8},{10,11... | collective-permute-start | bytes 1572872 | tf_op jit(solution)/shard_map/ppermute | solution.py:982
  277.8 30.6 %collective-permute-start.41 = (bf16[4,64,1024]{2,1,0:T(8,128)(2,1)}, bf16[4,64,1024]{2,1,0:T(8,128)(2,1)}, u32[]{:S(2)}, u32[]{:S(2)}) collective-permute-start(bf16[4,64,1024]{2,1,0:T(8,128)(2,1)} %get-tuple-element.436), channel_id=1, source_target_pairs={{0,4},{1,5},{2,6},{3,7},{4,0},{5,1},{6,2},{7,3},{8,12},{9,13},{10,... | collective-permute-start | bytes 1572872 | tf_op jit(solution)/shard_map/ppermute | solution.py:982
  329.1 100.2 %reduce-scatter.4.cloned.1.call-start = ((), (), s32[]{:S(2)}) async-start(), calls=%async_computation.3 | async-start | bytes 1310720 | tf_op jit(solution)/shard_map/reduce_scatter | solution.py:1006
  335.9 21.8 %collective-permute-start.49 = (bf16[4,2,32,1280]{3,2,1,0:T(8,128)(2,1)S(1)}, bf16[4,2,32,1280]{3,2,1,0:T(8,128)(2,1)S(1)}, u32[]{:S(2)}, u32[]{:S(2)}) collective-permute-start(bf16[4,2,32,1280]{3,2,1,0:T(8,128)(2,1)S(1)} %get-tuple-element.426), channel_id=1, source_target_pairs={{0,4},{1,5},{2,6},{3,7},{4,0},{5,1},{6,2},{7,3},{8,12},{9,13},{10,... | collective-permute-start | bytes 1966088 | tf_op jit(solution)/shard_map/ppermute | solution.py:982
  336.6 21.1 %collective-permute-start.48 = (bf16[4,2,32,1280]{3,2,1,0:T(8,128)(2,1)S(1)}, bf16[4,2,32,1280]{3,2,1,0:T(8,128)(2,1)S(1)}, u32[]{:S(2)}, u32[]{:S(2)}) collective-permute-start(bf16[4,2,32,1280]{3,2,1,0:T(8,128)(2,1)S(1)} %get-tuple-element.428), channel_id=1, source_target_pairs={{0,1},{1,0},{2,3},{3,2},{4,5},{5,4},{6,7},{7,6},{8,9},{9,8},{10,11... | collective-permute-start | bytes 1966088 | tf_op jit(solution)/shard_map/ppermute | solution.py:982
  361.7 67.6 %reduce-scatter.8.cloned.1.call-start = ((), (), s32[]{:S(2)}) async-start(), calls=%async_computation.5 | async-start | bytes 819200 | tf_op jit(solution)/shard_map/reduce_scatter | solution.py:1006
  377.7 19.6 %collective-permute-start.54 = (bf16[4,2,32,768]{3,2,1,0:T(8,128)(2,1)S(1)}, bf16[4,2,32,768]{3,2,1,0:T(8,128)(2,1)S(1)}, u32[]{:S(2)}, u32[]{:S(2)}) collective-permute-start(bf16[4,2,32,768]{3,2,1,0:T(8,128)(2,1)S(1)} %get-tuple-element.438), channel_id=1, source_target_pairs={{0,4},{1,5},{2,6},{3,7},{4,0},{5,1},{6,2},{7,3},{8,12},{9,13},{10,... | collective-permute-start | bytes 1179656 | tf_op jit(solution)/shard_map/ppermute | solution.py:982
  378.3 18.9 %collective-permute-start.53 = (bf16[4,2,32,768]{3,2,1,0:T(8,128)(2,1)S(1)}, bf16[4,2,32,768]{3,2,1,0:T(8,128)(2,1)S(1)}, u32[]{:S(2)}, u32[]{:S(2)}) collective-permute-start(bf16[4,2,32,768]{3,2,1,0:T(8,128)(2,1)S(1)} %get-tuple-element.440), channel_id=1, source_target_pairs={{0,1},{1,0},{2,3},{3,2},{4,5},{5,4},{6,7},{7,6},{8,9},{9,8},{10,11... | collective-permute-start | bytes 1179656 | tf_op jit(solution)/shard_map/ppermute | solution.py:982
  398.2 22.5 %collective-permute-start.57 = (f32[12,1024]{1,0:T(8,128)S(1)}, f32[12,1024]{1,0:T(8,128)S(1)}, u32[]{:S(2)}, u32[]{:S(2)}) collective-permute-start(f32[12,1024]{1,0:T(8,128)S(1)} %pad_maximum_fusion.14), channel_id=1, source_target_pairs={{0,2},{1,3},{2,0},{3,1},{4,6},{5,7},{6,4},{7,5},{8,10},{9,11},{10,... | collective-permute-start | bytes 147464 | tf_op jit(solution)/shard_map/ppermute | solution.py:982
  398.2 22.4 %collective-permute-start.58 = (f32[12,1024]{1,0:T(8,128)S(1)}, f32[12,1024]{1,0:T(8,128)S(1)}, u32[]{:S(2)}, u32[]{:S(2)}) collective-permute-start(f32[12,1024]{1,0:T(8,128)S(1)} %pad_maximum_fusion.14), channel_id=1, source_target_pairs={{0,1},{1,0},{2,3},{3,2},{4,5},{5,4},{6,7},{7,6},{8,9},{9,8},{10,11... | collective-permute-start | bytes 147464 | tf_op jit(solution)/shard_map/ppermute | solution.py:982
  399.4 21.3 %collective-permute-start.59 = (f32[12,1024]{1,0:T(8,128)S(1)}, f32[12,1024]{1,0:T(8,128)S(1)}, u32[]{:S(2)}, u32[]{:S(2)}) collective-permute-start(f32[12,1024]{1,0:T(8,128)S(1)} %pad_maximum_fusion.14), channel_id=1, source_target_pairs={{0,3},{1,2},{2,1},{3,0},{4,7},{5,6},{6,5},{7,4},{8,11},{9,10},{10,... | collective-permute-start | bytes 147464 | tf_op jit(solution)/shard_map/ppermute | solution.py:982
  400.2 20.4 %collective-permute-start.56 = (bf16[4,32,768]{2,1,0:T(8,128)(2,1)S(1)}, bf16[4,32,768]{2,1,0:T(8,128)(2,1)S(1)}, u32[]{:S(2)}, u32[]{:S(2)}) collective-permute-start(bf16[4,32,768]{2,1,0:T(8,128)(2,1)S(1)} %get-tuple-element.452), channel_id=1, source_target_pairs={{0,1},{1,0},{2,3},{3,2},{4,5},{5,4},{6,7},{7,6},{8,9},{9,8},{10,11... | collective-permute-start | bytes 589832 | tf_op jit(solution)/shard_map/ppermute | solution.py:982
  401.6 19.1 %collective-permute-start.55 = (bf16[4,32,768]{2,1,0:T(8,128)(2,1)S(1)}, bf16[4,32,768]{2,1,0:T(8,128)(2,1)S(1)}, u32[]{:S(2)}, u32[]{:S(2)}) collective-permute-start(bf16[4,32,768]{2,1,0:T(8,128)(2,1)S(1)} %get-tuple-element.454), channel_id=1, source_target_pairs={{0,4},{1,5},{2,6},{3,7},{4,0},{5,1},{6,2},{7,3},{8,12},{9,13},{10,... | collective-permute-start | bytes 589832 | tf_op jit(solution)/shard_map/ppermute | solution.py:982
  (128 other events, 931.9 us)
Sparse Core Ops, SparseCore 0:
  36.4 30.7 all-gather.4
  77.1 30.0 all-gather.6
  329.3 29.2 reduce-scatter.5
  361.9 28.8 reduce-scatter.3
  392.8 20.8 reduce-scatter.7

commit v4 on v3

--- a/solution.py
+++ b/solution.py
@@ -36,23 +36,28 @@
     length=len_ref[0]
     lane=lax.broadcasted_iota(jnp.int32,(1,128),1)
     first=lane<64
-    place=lax.broadcasted_iota(jnp.int32,(1,n),1)
-    ones=jnp.ones((n,128),bf16)
-    vaug=jnp.concatenate([v_ref[...],ones],axis=1)
-    k=k_ref[...]
+    place=lax.broadcasted_iota(jnp.int32,(n,128),0)
+    hi=(place//8*8).astype(f32); lo=(place%8).astype(f32)
+    kf=jnp.where(lane<6,jnp.where(lane%2==0,hi,lo),jnp.where(lane==6,jnp.where(place<length,0.0,-1e30),0.0)).astype(bf16)
+    kaug=jnp.concatenate([k_ref[...],kf],axis=1)
+    vaug=jnp.concatenate([v_ref[...],jnp.ones((n,128),bf16)],axis=1)
     diag=lax.broadcasted_iota(jnp.int32,(BQ,BQ),1)<=lax.broadcasted_iota(jnp.int32,(BQ,BQ),0)
-    bias=[jnp.where(place<length, place.astype(f32)*(slope_ref[2*pair+h]*LOG2E), -1e30) for h in range(2)]
+    feats=[]
+    for h in range(2):
+        j=3*(2*pair+h)
+        mf=jnp.where(lane<2,slope_ref[j],jnp.where(lane<4,slope_ref[j+1],jnp.where(lane<6,slope_ref[j+2],jnp.where(lane==6,1.0,0.0)))).astype(bf16)
+        feats.append(jnp.broadcast_to(mf,(BQ,128)))
     for i in range(n//BQ):
         nk=(i+1)*BQ
         q=q_ref[i*BQ:(i+1)*BQ,:]*jnp.array(0.125,bf16)
         outs=[];lses=[]
         for h in range(2):
-            qh=jnp.where(first if h==0 else ~first, q, jnp.zeros_like(q))
-            s=dotnt(qh,k[:nk])*LOG2E+bias[h][:,:nk]
+            qa=jnp.concatenate([jnp.where(first if h==0 else ~first, q, jnp.zeros_like(q)),feats[h]],axis=1)
+            s=dotnt(qa,kaug[:nk])
             sd=jnp.where(diag,s[:,nk-BQ:],-1e30)
             s=sd if i==0 else jnp.concatenate([s[:,:nk-BQ],sd],axis=1)
-            m=jnp.max(s,axis=1,keepdims=True)
-            p=jnp.exp2(s-m).astype(bf16)
+            m=jnp.max(s,axis=1,keepdims=True)*LOG2E
+            p=jnp.exp2(s*LOG2E-m).astype(bf16)
             o=dot(p,vaug[:nk])
             tot=o[:,128:]
             outs.append(o[:,:128]/tot)
@@ -427,12 +432,16 @@
     pltpu.make_async_copy(ref, ref, sem).wait()
 
 
-def start_rows(place_ref, pieces, w_ref, sems):
-    for zr, half, xr, yr, core in itertools.product(range(4), *[range(2)] * 4):
-        d = owner(place_ref, zr, xr, yr, core)
-        rows = pl.ds(pl.multiple_of(d * 128 + half * 64, 64), 64)
-        src = piece(of_half(pieces, half), half, zr, xr, yr, core).at[0]
-        pltpu.make_async_copy(src, w_ref.at[rows, :], sems.at[zr]).start()
+def start_rows(place_ref, pieces, w_ref, sems, step):
+    for zr in range(4):
+
+        @pl.when(step == max(zr - 1, 0))
+        def _(zr=zr):
+            for half, xr, yr, core in itertools.product(range(2), repeat=4):
+                d = owner(place_ref, zr, xr, yr, core)
+                rows = pl.ds(pl.multiple_of(d * 128 + half * 64, 64), 64)
+                src = piece(of_half(pieces, half), half, zr, xr, yr, core).at[0]
+                pltpu.make_async_copy(src, w_ref.at[rows, :], sems.at[zr]).start()
 
 
 def wait_rows(w_ref, sems, z):
@@ -553,47 +562,66 @@
     )(g, w, w)
 
 
-def up_kernel(half, place_ref, *refs):
-    pieces, (a_ref, b_ref, u_ref, s_ref, w_ref, sem) = refs[:8], refs[8:]
+def up_kernel(place_ref, *refs):
+    pieces, (a_ref, b_ref, u0_ref, u1_ref, s0_ref, s1_ref, w_ref, sems) = refs[:10], refs[10:]
     step = pl.program_id(0)
-
-    @pl.when(step == 0)
+    for half in range(2):
+        part = w_ref.at[2 * half : 2 * half + 2]
+
+        @pl.when(step == half)
+        def _(half=half, part=part):
+            start_columns(place_ref, of_half(pieces, half), part, sems.at[half], half)
+
+        @pl.when(step == 4 * half)
+        def _(half=half, part=part):
+            wait_all(part, sems.at[half])
+
+    c = 0.7978845608028654
+
+    def block(u_ref, s_ref):
+        w = w_ref[step // 2, :, pl.ds(pl.multiple_of(step % 2 * 512, 512), 512)]
+        for r in range(0, a_ref.shape[0], 256):
+            v = dot(a_ref[r : r + 256, :], w) + b_ref[...]
+            square = v * v
+            h = 0.5 + 0.5 * jnp.tanh(v * (c + (c * 0.044715) * square))
+            u = v * h
+            u_ref[r : r + 256, :] = u.astype(bf16)
+            s_ref[r : r + 256, :] = (
+                h + u * (1.0 - h) * (2.0 * c + (2.0 * c * 0.134145) * square)
+            ).astype(bf16)
+
+    @pl.when(step < 4)
     def _():
-        start_columns(place_ref, pieces, w_ref, sem, half)
-        wait_all(w_ref, sem)
-
-    c = 0.7978845608028654
-    w = w_ref[step // 2, :, pl.ds(pl.multiple_of(step % 2 * 512, 512), 512)]
-    for r in range(0, a_ref.shape[0], 256):
-        v = dot(a_ref[r : r + 256, :], w) + b_ref[...]
-        square = v * v
-        h = 0.5 + 0.5 * jnp.tanh(v * (c + (c * 0.044715) * square))
-        u = v * h
-        u_ref[r : r + 256, :] = u.astype(bf16)
-        s_ref[r : r + 256, :] = (
-            h + u * (1.0 - h) * (2.0 * c + (2.0 * c * 0.134145) * square)
-        ).astype(bf16)
-
-
-def up_call(place, half, pieces, a, b):
+        block(u0_ref, s0_ref)
+
+    @pl.when(step >= 4)
+    def _():
+        block(u1_ref, s1_ref)
+
+
+def up_call(place, pieces, a, b):
     n, d = a.shape
+    outs = [
+        spec((n, 512), lambda i, *_: (0, jnp.minimum(i, 3))),
+        spec((n, 512), lambda i, *_: (0, jnp.maximum(i - 4, 0))),
+    ]
     return pl.pallas_call(
-        functools.partial(up_kernel, half),
+        up_kernel,
         grid_spec=pltpu.PrefetchScalarGridSpec(
             num_scalar_prefetch=1,
-            grid=(4,),
-            in_specs=[HBM] * 8
-            + [spec((n, d), lambda i, *_: (0, 0)), spec((1, 512), lambda i, *_: (0, 4 * half + i))],
-            out_specs=[spec((n, 512), lambda i, *_: (0, i))] * 2,
-            scratch_shapes=[pltpu.VMEM((2, d, 1024), bf16), pltpu.SemaphoreType.DMA],
-        ),
-        out_shape=[jax.ShapeDtypeStruct((n, 2048), bf16)] * 2,
-        compiler_params=params(40),
+            grid=(8,),
+            in_specs=[HBM] * 10
+            + [spec((n, d), lambda i, *_: (0, 0)), spec((1, 512), lambda i, *_: (0, i))],
+            out_specs=outs + outs,
+            scratch_shapes=[pltpu.VMEM((4, d, 1024), bf16), pltpu.SemaphoreType.DMA((2,))],
+        ),
+        out_shape=[jax.ShapeDtypeStruct((n, 2048), bf16)] * 4,
+        compiler_params=params(),
         cost_estimate=pl.CostEstimate(
-            flops=2 * n * d * 2048, bytes_accessed=2 * (n * d + d * 2048 + 4096 * n), transcendentals=n * 2048
+            flops=2 * n * d * 4096, bytes_accessed=2 * (n * d + d * 4096 + 8192 * n), transcendentals=n * 4096
         ),
         name="up",
-    )(place, *of_half(pieces, half), a, b.reshape(1, 4096))
+    )(place, *pieces, a, b.reshape(1, 4096))
 
 
 def divide(acc_ref, keep_ref, give_ref, core):
@@ -641,10 +669,7 @@
     pieces, (u0_ref, u1_ref, h_ref, b_ref, o_ref, acc_ref, w_ref, sems) = refs[:10], refs[10:]
     step = pl.program_id(0)
 
-    @pl.when(step == 0)
-    def _():
-        start_rows(place_ref, pieces, w_ref, sems)
-
+    start_rows(place_ref, pieces, w_ref, sems, step)
     wait_rows(w_ref, sems, step)
     w = w_ref[pl.ds(pl.multiple_of(step * 1024, 1024), 1024), :]
 
@@ -703,10 +728,7 @@
     pieces, (g_ref, s0_ref, s1_ref, z_ref, b_ref, w_ref, sems) = refs[:10], refs[10:]
     step = pl.program_id(0)
 
-    @pl.when(step == 0)
-    def _():
-        start_rows(place_ref, pieces, w_ref, sems)
-
+    start_rows(place_ref, pieces, w_ref, sems, step)
     wait_rows(w_ref, sems, step)
     w = w_ref[pl.ds(pl.multiple_of(step * 1024, 1024), 1024), :]
     total = None
@@ -783,9 +805,10 @@
     )
     step = pl.program_id(0)
 
-    @pl.when(step == 0)
-    def _():
-        for half in range(2):
+    for half in range(2):
+
+        @pl.when(step == half)
+        def _(half=half):
             part = w_ref.at[2 * half : 2 * half + 2]
             start_columns(place_ref, of_half(pieces, half), part, sems.at[half], half)
 
@@ -1048,7 +1071,7 @@
         low = rest.astype(ml_dtypes.bfloat16).astype(np.float32)
         pieces.append(low)
         rest = rest - low
-    return slopes, np.stack(pieces, axis=1).reshape(-1)
+    return np.stack(pieces, axis=1).reshape(-1)
 
 
 def moments(v):
@@ -1094,7 +1117,7 @@
     every_seq = jnp.arange(seq_lengths.shape[0], dtype=jnp.int32)
     length = jnp.sum(jnp.where(every_seq == my_seq, seq_lengths, 0))
     valid = (jnp.arange(rows, dtype=jnp.int32) < length).astype(f32)
-    slopes, slopes_split = slope_table()
+    slopes_split = slope_table()
     no_bias = jnp.zeros((512,), f32)
     bias0 = jnp.concatenate([qkv_bias[:512], no_bias, qkv_bias[1024:1536]])
     bias1 = jnp.concatenate([qkv_bias[512:1024], no_bias, qkv_bias[1536:]])
@@ -1131,7 +1154,7 @@
     also_xy, also_yx = send(also_a, OVER_Y), send(also_b, OVER_X)
     also_ca, also_cb = send(also_a, OVER_C), send(also_b, OVER_C)
     three_z = gather_z_line(three)
-    context0, lse0 = attn_fwd(length, jnp.asarray(slopes), qkv0, 0)
+    context0, lse0 = attn_fwd(length, jnp.asarray(slopes_split), qkv0, 0)
     context0, also_xy, also_yx, also_ca, also_cb, a1 = tie(
         context0, also_xy, also_yx, also_ca, also_cb, a1
     )
@@ -1143,7 +1166,7 @@
     two_x, two_y = plain(send(two_z, OVER_X)), plain(send(two_z, OVER_Y))
     qkv1, w1 = qkv_call(place_vec, pieces, a1, bias1, True)
     qkv1, two_c, three_z = tie(qkv1, two_c, three_z)
-    context1, lse1 = attn_fwd(length, jnp.asarray(slopes), qkv1, 4)
+    context1, lse1 = attn_fwd(length, jnp.asarray(slopes_split), qkv1, 4)
     context0, context1, two_x, two_y, three_z = tie(context0, context1, two_x, two_y, three_z)
 
     two_xy, two_yx = send(two_x[:, 0], OVER_Y), send(two_y[:, 1], OVER_X)
@@ -1151,16 +1174,15 @@
     hidden, a2 = dense_call(context0, context1, w1, tokens, dense_bias, ln2_gain, ln2_bias)
     a2, two_xy, two_yx, two_cx, two_cy, three_z = tie(a2, two_xy, two_yx, two_cx, two_cy, three_z)
     two_cxy, two_cyx = send(two_xy, OVER_C), send(two_yx, OVER_C)
-    two_cxy, a2, three_z = tie(two_cxy, a2, three_z)
+    two_cxy, two_cyx, a2, three_z = tie(two_cxy, two_cyx, a2, three_z)
 
     three_c = send(three_z, OVER_C)
     three_x, three_y = plain(send(three_z, OVER_X)), plain(send(three_z, OVER_Y))
     up_pieces = (two_z, two_x, two_y, two_xy, two_yx, two_c, two_cx, two_cy, two_cxy, two_cyx)
-    u0, slope0 = up_call(place_vec, 0, up_pieces, a2, up_bias)
-    u0, a2, two_cyx, three_c = tie(u0, a2, two_cyx, three_c)
-    up_pieces = (two_z, two_x, two_y, two_xy, two_yx, two_c, two_cx, two_cy, two_cxy, two_cyx)
-    u1, slope1 = up_call(place_vec, 1, up_pieces, a2, up_bias)
-    u0, u1, grad_low, three_x, three_y = tie(u0, u1, grad_low, three_x, three_y)
+    u0, u1, slope0, slope1 = up_call(place_vec, up_pieces, a2, up_bias)
+    u0, u1, grad_low, three_x, three_y, three_c = tie(
+        u0, u1, grad_low, three_x, three_y, three_c
+    )
     three_xy, three_yx = send(three_x[:, 0], OVER_Y), send(three_y[:, 1], OVER_X)
     three_cx, three_cy = send(three_x, OVER_C), send(three_y, OVER_C)
 

time: 456 us -> 452 us (level)
    pallas_call x2 -> x1, Pallas kernels: 26.4 us -> 25.2 us  [up_call(): pl.pallas_call(up_kernel, grid_spec=pltpu.PrefetchScalarGridSpec(num_scal...]
    unnamed x200 -> x202, local copies, waits for them, and re-layouts: 25 us -> 23.9 us
  transfers between devices with their start and end apart: 72 -> 72, of which waited for: 20 -> 22; matrix products, arithmetic and copies ran while one was open for 13% -> 12% of each run, Pallas kernels for 50% -> 50%
where the time goes in v4:
time: 452 us; the launch traced here: 446 us
  Pallas kernels  237 us (52%)
  starting transfers between devices  62.3 us (14%)
  local copies, waits for them, and re-layouts  46.8 us (10%)
  other arithmetic  46.7 us (10%)
  waiting for transfers between devices  37.6 us (8%)
  between operations  15.6 us (3%)
    ppermute x67, starting transfers between devices, send(): return lax.ppermute(array, ALL, pairs)  61.3 us
    pallas_call x2, Pallas kernels, attn_bwd(): pl.pallas_call(attn_bwd_kernel, grid_spec=pltpu.PrefetchScalarGridSpec(nu...  39.9 us
    ppermute x67, waiting for transfers between devices, send(): return lax.ppermute(array, ALL, pairs)  36.7 us
    pallas_call x2, Pallas kernels, attn_fwd(): pl.pallas_call(attn_fwd_kernel, grid_spec=pltpu.PrefetchScalarGridSpec(nu...  25.7 us
    pallas_call x1, Pallas kernels, up_call(): pl.pallas_call(up_kernel, grid_spec=pltpu.PrefetchScalarGridSpec(num_scal...  25.2 us
    unnamed x202, local copies, waits for them, and re-layouts  23.9 us
    pallas_call x1, Pallas kernels, norm_up_call(): pl.pallas_call(norm_up_kernel, grid_spec=pltpu.PrefetchScalarGridSpec(num...  23.6 us
    pallas_call x2, Pallas kernels, qkv_call(): pl.pallas_call(functools.partial(qkv_kernel, turned), grid_spec=pltpu.Pre...  18.9 us
  transfers between devices with their start and end apart: 72, of which 22 were waited for; matrix products, arithmetic and copies ran while one was open for 12% of the time, Pallas kernels for 50%

profile of v4, /device:TPU:0, one launch (start us, length us, event | category | flops | bytes accessed | tf_op | source)
XLA Modules:
  0.0 445.8 jit_solution(3205685438371664408)
XLA Ops:
  9.0 3.1 collective-permute-start
  12.0 2.6 collective-permute-start.1
  18.9 1.9 fusion.25
  21.5 10.3 %collective-permute-done.1 = bf16[2,8,16,512]{3,2,1,0:T(8,128)(2,1)S(1)} collective-permute-done((bf16[2,8,16,512]{3,2,1,0:T(8,128)(2,1)S(1)}, bf16[2,8,16,512]{3,2,1,0:T(8,128)(2,1)S(1)}, u32[]{:S(2)}, u32[]{:S(2)}) %collective-permute-start.1) | collective-permute-done | bytes 262176 | tf_op jit(solution)/shard_map/ppermute | solution.py:1005
  36.5 3.1 collective-permute-done.4
  39.6 2.0 collective-permute-done.3
  48.5 2.1 fusion.5.refs_8_.refs_2_.refs_0_
  52.5 4.2 collective-permute-done.5.refs_1_
  61.4 9.0 %qkv.2 = (bf16[1024,1536]{1,0:T(8,128)(2,1)}, bf16[3,1024,512]{2,1,0:T(8,128)(2,1)}) custom-call(s32[4]{0:T(128)} %pad_add_fusion.place_ref.where_ref, bf16[2,4,3,16,512]{4,3,2,1,0:T(8,128)(2,1)} %copy-done.54, bf16[2,4,3,16,512]{4,3,2,1,0:T(8,128)(2,1)} %copy-done.83, bf16[2,4,3,16,512]{4,3,2,1,0:T(8,128)(2,1)} %copy-done.84, ...), custom_call_target="tpu_custom_call" | custom-call | flops 3221225472 | bytes 13631488 | tf_op jit(solution)/shard_map/qkv/pallas_call | solution.py:488
  70.6 2.0 pad_maximum_fusion.3.refs_4_
  78.8 12.8 %attn_fwd.2 = (bf16[1024,512]{1,0:T(8,128)(2,1)}, f32[1024,512]{1,0:T(8,128)}) custom-call(s32[2]{0:T(128)} %get-tuple-element.505.len_ref, f32[48]{0:T(128)} %constant.189.clone.slope_ref, bf16[1024,1536]{1,0:T(8,128)(2,1)} %get-tuple-element.233.q_ref.k_ref.v_ref, bf16[1024,1536]{1,0:T(8,128)(2,1)} %get-tuple-element.233.q_ref.k_ref.v_ref, ...), custom_call_target="tpu_custom_call" | custom-call | flops 5368709120 | bytes 6291456 | tf_op jit(solution)/shard_map/attn_fwd/pallas_call | solution.py:72
  96.5 9.9 %qkv.3 = (bf16[1024,1536]{1,0:T(8,128)(2,1)}, bf16[5,1024,512]{2,1,0:T(8,128)(2,1)}) custom-call(s32[4]{0:T(128)} %pad_add_fusion.place_ref.where_ref, bf16[2,4,5,16,512]{4,3,2,1,0:T(8,128)(2,1)} %copy-done.52, bf16[2,4,5,16,512]{4,3,2,1,0:T(8,128)(2,1)} %collective-permute-done.13.refs_1_, bf16[2,4,5,16,512]{4,3,2,1,0:T(8,128)(2,1)} %collective-permute-done.15.refs_2_, ...), custom_call_target="tpu_custom_call" | custom-call | flops 3221225472 | bytes 13631488 | tf_op jit(solution)/shard_map/qkv/pallas_call | solution.py:488
  107.1 12.9 %attn_fwd.3 = (bf16[1024,512]{1,0:T(8,128)(2,1)}, f32[1024,512]{1,0:T(8,128)}) custom-call(s32[2]{0:T(128)} %get-tuple-element.506.len_ref, f32[48]{0:T(128)} %constant.189.clone.slope_ref, bf16[1024,1536]{1,0:T(8,128)(2,1)} %get-tuple-element.335.q_ref.k_ref.v_ref, bf16[1024,1536]{1,0:T(8,128)(2,1)} %get-tuple-element.335.q_ref.k_ref.v_ref, ...), custom_call_target="tpu_custom_call" | custom-call | flops 5368709120 | bytes 6291456 | tf_op jit(solution)/shard_map/attn_fwd/pallas_call | solution.py:72
  128.4 5.6 %dense.1 = (f32[1024,1024]{1,0:T(8,128)S(1)}, bf16[1024,1024]{1,0:T(8,128)(2,1)S(1)}) custom-call(bf16[1024,512]{1,0:T(8,128)(2,1)S(1)} %copy-done.16, bf16[1024,512]{1,0:T(8,128)(2,1)S(1)} %copy-done.13, bf16[5,1024,512]{2,1,0:T(8,128)(2,1)} %get-tuple-element.253.w0_ref.w1_ref.refs_7_, bf16[5,1024,512]{2,1,0:T(8,128)(2,1)} %get-tuple-element.253.w0_ref.w1_ref.refs_7_, ...), custom_call_target="tpu_custom_call" | custom-call | flops 2147483648 | bytes 12582912 | tf_op jit(solution)/shard_map/dense/pallas_call | solution.py:530
  134.0 1.9 copy-done.27
  143.6 25.2 %up.1 = (bf16[1024,2048]{1,0:T(8,128)(2,1)}, bf16[1024,2048]{1,0:T(8,128)(2,1)}, bf16[1024,2048]{1,0:T(8,128)(2,1)}, bf16[1024,2048]{1,0:T(8,128)(2,1)}) custom-call(s32[4]{0:T(128)} %pad_add_fusion.place_ref.where_ref, bf16[4,2,2,32,1024]{4,3,2,1,0:T(8,128)(2,1)} %bitcast.22.refs_0_, bf16[4,2,2,32,1024]{4,3,2,1,0:T(8,128)(2,1)} %collective-permute-done.20.refs_1_, ...), custom_call_target="tpu_custom_call" | custom-call | flops 8589934592 | bytes 27262976 | tf_op jit(solution)/shard_map/up/pallas_call | solution.py:608
  171.8 13.2 %down_grad.1 = (bf16[8,256,1024]{2,1,0:T(8,128)(2,1)S(1)}, bf16[8,256,1024]{2,1,0:T(8,128)(2,1)S(1)}) custom-call(s32[4]{0:T(128)S(1)} %copy-done.22, bf16[1024,2048]{1,0:T(8,128)(2,1)} %get-tuple-element.365.u0_ref.refs_10_, bf16[1024,2048]{1,0:T(8,128)(2,1)} %get-tuple-element.275.u1_ref.refs_11_, bf16[1024,1024]{1,0:T(8,128)(2,1)S(1)} %copy-done.2), custom_call_target="tpu_custom_call" | custom-call | flops 8589934592 | bytes 18874368 | tf_op jit(solution)/shard_map/down_grad/pallas_call | solution.py:646
  190.5 17.5 %gate.1 = (bf16[1024,4096]{1,0:T(8,128)(2,1)}, f32[1,4096]{1,0:T(1,128)}) custom-call(s32[4]{0:T(128)} %pad_add_fusion.place_ref.where_ref, bf16[4,2,1,64,1024]{4,3,2,1,0:T(8,128)(2,1)} %bitcast.252, bf16[4,2,1,64,1024]{4,3,2,1,0:T(8,128)(2,1)} %copy-done.59, bf16[4,2,1,64,1024]{4,3,2,1,0:T(8,128)(2,1)} %copy-done.60, bf16[4,1,64,1024]{3,2,1,0:T(8,128)(2,1)} %copy-done.74, ...), custom_call_target="tpu_custom_call" | custom-call | flops 8589934592 | bytes 27262976 | tf_op jit(solution)/shard_map/gate/pallas_call | solution.py:747
  208.1 14.3 %up_grad.1 = (bf16[8,64,4096]{2,1,0:T(8,128)(2,1)S(1)}, bf16[8,64,4096]{2,1,0:T(8,128)(2,1)}) custom-call(s32[4]{0:T(128)S(1)} %copy-done.23, bf16[1024,1024]{1,0:T(8,128)(2,1)S(1)} %copy-done.29, bf16[1024,4096]{1,0:T(8,128)(2,1)} %get-tuple-element.298.g_ref.refs_10_), custom_call_target="tpu_custom_call" | custom-call | flops 8589934592 | bytes 18874368 | tf_op jit(solution)/shard_map/up_grad/pallas_call | solution.py:964
  224.6 5.6 %add_convert_fusion.1 = bf16[8,256,1024]{2,1,0:T(8,128)(2,1)S(1)} fusion(bf16[8,256,1024]{2,1,0:T(8,128)(2,1)} %collective-permute-done.37, bf16[8,256,1024]{2,1,0:T(8,128)(2,1)} %copy-done.5), kind=kLoop, calls=%fused_computation.1 | loop fusion | flops 8388608 | bytes 12582912 | tf_op jit(solution)/shard_map/convert_element_type | solution.py:1033
  235.6 23.6 %norm_up.1 = (bf16[1024,1024]{1,0:T(8,128)(2,1)}, f32[1024,1024]{1,0:T(8,128)}, f32[8,1024]{1,0:T(8,128)}) custom-call(s32[4]{0:T(128)} %pad_add_fusion.place_ref.where_ref, bf16[4,2,2,32,1024]{4,3,2,1,0:T(8,128)(2,1)} %bitcast.22.refs_0_, bf16[4,2,2,32,1024]{4,3,2,1,0:T(8,128)(2,1)} %collective-permute-done.20.refs_1_, ...), custom_call_target="tpu_custom_call" | custom-call | flops 8589934592 | bytes 33554432 | tf_op jit(solution)/shard_map/norm_up/pallas_call | solution.py:838
  260.1 4.1 add_convert_fusion
  274.1 3.0 dense_back.1.do_ref
  278.5 20.0 %attn_bwd.2 = (bf16[1024,512]{1,0:T(8,128)(2,1)S(1)}, bf16[1024,512]{1,0:T(8,128)(2,1)S(1)}, bf16[1024,512]{1,0:T(8,128)(2,1)S(1)}) custom-call(s32[2]{0:T(128)S(1)} %copy-done.26, f32[48]{0:T(128)S(1)} %copy-done.30, bf16[1024,1536]{1,0:T(8,128)(2,1)} %get-tuple-element.233.q_ref.k_ref.v_ref, bf16[1024,1536]{1,0:T(8,128)(2,1)} %get-tuple-element.233.q_ref.k_ref.v_ref, ...), custom_call_target="tpu_custom_call" | custom-call | flops 13421772800 | bytes 10485760 | tf_op jit(solution)/shard_map/attn_bwd/pallas_call | solution.py:141
  309.9 8.6 %dense_grad.1 = (bf16[8,64,2560]{2,1,0:T(8,128)(2,1)S(1)}, bf16[8,64,2560]{2,1,0:T(8,128)(2,1)}, f32[1,2560]{1,0:T(1,128)S(1)}) custom-call(s32[4]{0:T(128)S(1)} %copy-done.24, bf16[1024,512]{1,0:T(8,128)(2,1)S(1)} %copy-done.18, bf16[1024,512]{1,0:T(8,128)(2,1)S(1)} %copy-done.14, bf16[1024,1024]{1,0:T(8,128)(2,1)S(1)} %copy-done.9, ...), custom_call_target="tpu_custom_call" | custom-call | flops 5368709120 | bytes 14680064 | tf_op jit(solution)/shard_map/dense_grad/pallas_call | solution.py:931
  328.3 2.4 add_convert_fusion.2
  333.4 19.9 %attn_bwd.3 = (bf16[1024,512]{1,0:T(8,128)(2,1)S(1)}, bf16[1024,512]{1,0:T(8,128)(2,1)S(1)}, bf16[1024,512]{1,0:T(8,128)(2,1)S(1)}) custom-call(s32[2]{0:T(128)S(1)} %copy-done.25, f32[48]{0:T(128)S(1)} %copy-done.30, bf16[1024,1536]{1,0:T(8,128)(2,1)} %get-tuple-element.335.q_ref.k_ref.v_ref, bf16[1024,1536]{1,0:T(8,128)(2,1)} %get-tuple-element.335.q_ref.k_ref.v_ref, ...), custom_call_target="tpu_custom_call" | custom-call | flops 13421772800 | bytes 10485760 | tf_op jit(solution)/shard_map/attn_bwd/pallas_call | solution.py:141
  361.5 5.6 %heads_grad.1 = (bf16[8,64,1536]{2,1,0:T(8,128)(2,1)S(1)}, bf16[8,64,1536]{2,1,0:T(8,128)(2,1)}, f32[1,1536]{1,0:T(1,128)S(1)}) custom-call(s32[4]{0:T(128)S(1)} %copy-done.24, bf16[1024,1024]{1,0:T(8,128)(2,1)S(1)} %copy-done.10, bf16[1024,512]{1,0:T(8,128)(2,1)S(1)} %copy-done.38, bf16[1024,512]{1,0:T(8,128)(2,1)S(1)} %copy-done.40, ...), custom_call_target="tpu_custom_call" | custom-call | flops 3221225472 | bytes 10485760 | tf_op jit(solution)/shard_map/heads_grad/pallas_call | solution.py:931
  375.2 17.9 %norm_qkv.1 = (bf16[1024,1024]{1,0:T(8,128)(2,1)}, f32[8,1024]{1,0:T(8,128)}) custom-call(bf16[1024,512]{1,0:T(8,128)(2,1)} %copy-done.31, bf16[1024,512]{1,0:T(8,128)(2,1)} %copy-done.33, bf16[1024,512]{1,0:T(8,128)(2,1)} %copy-done.35, bf16[1024,512]{1,0:T(8,128)(2,1)} %copy-done.37, bf16[1024,512]{1,0:T(8,128)(2,1)} %copy-done.39, ...), custom_call_target="tpu_custom_call" | custom-call | flops 6442450944 | bytes 23068672 | tf_op jit(solution)/shard_map/norm_qkv/pallas_call | solution.py:884
  398.8 17.7 %down.1 = bf16[1024,1024]{1,0:T(8,128)(2,1)} custom-call(s32[4]{0:T(128)} %pad_add_fusion.place_ref.where_ref, bf16[4,2,1,64,1024]{4,3,2,1,0:T(8,128)(2,1)} %bitcast.253, bf16[4,2,1,64,1024]{4,3,2,1,0:T(8,128)(2,1)} %copy-done.59, bf16[4,2,1,64,1024]{4,3,2,1,0:T(8,128)(2,1)} %copy-done.60, bf16[4,1,64,1024]{3,2,1,0:T(8,128)(2,1)} %copy-done.74, ...), custom_call_target="tpu_custom_call" | custom-call | flops 8589934592 | bytes 23068672 | tf_op jit(solution)/shard_map/down/pallas_call | solution.py:699
  417.3 5.2 %collective-permute-start.64 = (bf16[2,32,768]{2,1,0:T(8,128)(2,1)S(1)}, bf16[2,32,768]{2,1,0:T(8,128)(2,1)S(1)}, u32[]{:S(2)}, u32[]{:S(2)}) collective-permute-start(bf16[2,32,768]{2,1,0:T(8,128)(2,1)S(1)} %get-tuple-element.446), channel_id=1, source_target_pairs={{0,8},{1,9},{2,10},{3,11},{4,12},{5,13},{6,14},{7,15},{8,16},{9,17... | collective-permute-start | bytes 294920 | tf_op jit(solution)/shard_map/ppermute | solution.py:1005
  432.8 3.5 collective-permute-done.62
  (444 shorter events, 139.4 us)
Async XLA Ops:
  7.2 63.4 %all-gather.5.cloned.1.call-start = ((), (), s32[]{:S(2)}) async-start(), calls=%async_computation.6 | async-start | bytes 1310720 | tf_op jit(solution)/shard_map/all_gather | solution.py:1025
  12.0 19.7 %collective-permute-start.1 = (bf16[2,8,16,512]{3,2,1,0:T(8,128)(2,1)S(1)}, bf16[2,8,16,512]{3,2,1,0:T(8,128)(2,1)S(1)}, u32[]{:S(2)}, u32[]{:S(2)}) collective-permute-start(bf16[2,8,16,512]{3,2,1,0:T(8,128)(2,1)S(1)} %bitcast.215), channel_id=1, source_target_pairs={{0,16},{1,17},{2,18},{3,19},{4,20},{5,21},{6,22},{7,23},{8,24},{9,... | collective-permute-start | bytes 786440 | tf_op jit(solution)/shard_map/ppermute | solution.py:1005
  36.3 70.8 %all-gather.7.cloned.1.call-start = ((), (), s32[]{:S(2)}) async-start(), calls=%async_computation.7 | async-start | bytes 1310720 | tf_op jit(solution)/shard_map/all_gather | solution.py:1025
  72.5 19.1 %collective-permute-start.14 = (bf16[2,4,5,16,512]{4,3,2,1,0:T(8,128)(2,1)}, bf16[2,4,5,16,512]{4,3,2,1,0:T(8,128)(2,1)}, u32[]{:S(2)}, u32[]{:S(2)}) collective-permute-start(bf16[2,4,5,16,512]{4,3,2,1,0:T(8,128)(2,1)} %pad_maximum_fusion.3.refs_4_), channel_id=1, source_target_pairs={{0,1},{1,0},{2,3},{3,2},{4,5},{5,4},{6,7},{7,6},{8,9},{9,8},{10,11... | collective-permute-start | bytes 1966088 | tf_op jit(solution)/shard_map/ppermute | solution.py:1005
  76.9 348.0 %reduce-scatter.6.cloned.1.call-start = ((), (), s32[]{:S(2)}) async-start(), calls=%async_computation.4 | async-start | bytes 1310720 | tf_op jit(solution)/shard_map/reduce_scatter | solution.py:1029
  78.5 28.6 %collective-permute-start.19 = (bf16[4,2,2,32,1024]{4,3,2,1,0:T(8,128)(2,1)}, bf16[4,2,2,32,1024]{4,3,2,1,0:T(8,128)(2,1)}, u32[]{:S(2)}, u32[]{:S(2)}) collective-permute-start(bf16[4,2,2,32,1024]{4,3,2,1,0:T(8,128)(2,1)} %bitcast.22.refs_0_), channel_id=1, source_target_pairs={{0,2},{1,3},{2,0},{3,1},{4,6},{5,7},{6,4},{7,5},{8,10},{9,11},{10,... | collective-permute-start | bytes 3145736 | tf_op jit(solution)/shard_map/ppermute | solution.py:1005
  92.9 27.1 %collective-permute-start.20 = (bf16[4,2,2,32,1024]{4,3,2,1,0:T(8,128)(2,1)}, bf16[4,2,2,32,1024]{4,3,2,1,0:T(8,128)(2,1)}, u32[]{:S(2)}, u32[]{:S(2)}) collective-permute-start(bf16[4,2,2,32,1024]{4,3,2,1,0:T(8,128)(2,1)} %bitcast.22.refs_0_), channel_id=1, source_target_pairs={{0,1},{1,0},{2,3},{3,2},{4,5},{5,4},{6,7},{7,6},{8,9},{9,8},{10,11... | collective-permute-start | bytes 3145736 | tf_op jit(solution)/shard_map/ppermute | solution.py:1005
  93.5 26.6 %collective-permute-start.21 = (bf16[4,2,2,32,1024]{4,3,2,1,0:T(8,128)(2,1)}, bf16[4,2,2,32,1024]{4,3,2,1,0:T(8,128)(2,1)}, u32[]{:S(2)}, u32[]{:S(2)}) collective-permute-start(bf16[4,2,2,32,1024]{4,3,2,1,0:T(8,128)(2,1)} %bitcast.22.refs_0_), channel_id=1, source_target_pairs={{0,4},{1,5},{2,6},{3,7},{4,0},{5,1},{6,2},{7,3},{8,12},{9,13},{10,... | collective-permute-start | bytes 3145736 | tf_op jit(solution)/shard_map/ppermute | solution.py:1005
  120.1 17.9 %collective-permute-start.24 = (bf16[4,2,2,32,1024]{4,3,2,1,0:T(8,128)(2,1)}, bf16[4,2,2,32,1024]{4,3,2,1,0:T(8,128)(2,1)S(1)}, u32[]{:S(2)}, u32[]{:S(2)}) collective-permute-start(bf16[4,2,2,32,1024]{4,3,2,1,0:T(8,128)(2,1)} %collective-permute-done.20.refs_1_), channel_id=1, source_target_pairs={{0,2},{1,3},{2,0},{3,1},{4,6},{5,7},{6,4},{7,5},{8,10},{9,11},{10,... | collective-permute-start | bytes 3145736 | tf_op jit(solution)/shard_map/ppermute | solution.py:1005
  141.6 27.2 %collective-permute-start.28 = (bf16[4,2,1,64,1024]{4,3,2,1,0:T(8,128)(2,1)S(1)}, bf16[4,2,1,64,1024]{4,3,2,1,0:T(8,128)(2,1)S(1)}, u32[]{:S(2)}, u32[]{:S(2)}) collective-permute-start(bf16[4,2,1,64,1024]{4,3,2,1,0:T(8,128)(2,1)S(1)} %bitcast.254), channel_id=1, source_target_pairs={{0,1},{1,0},{2,3},{3,2},{4,5},{5,4},{6,7},{7,6},{8,9},{9,8},{10,11... | collective-permute-start | bytes 3145736 | tf_op jit(solution)/shard_map/ppermute | solution.py:1005
  143.0 25.8 %collective-permute-start.29 = (bf16[4,2,1,64,1024]{4,3,2,1,0:T(8,128)(2,1)S(1)}, bf16[4,2,1,64,1024]{4,3,2,1,0:T(8,128)(2,1)S(1)}, u32[]{:S(2)}, u32[]{:S(2)}) collective-permute-start(bf16[4,2,1,64,1024]{4,3,2,1,0:T(8,128)(2,1)S(1)} %bitcast.255), channel_id=1, source_target_pairs={{0,4},{1,5},{2,6},{3,7},{4,0},{5,1},{6,2},{7,3},{8,12},{9,13},{10,... | collective-permute-start | bytes 3145736 | tf_op jit(solution)/shard_map/ppermute | solution.py:1005
  143.6 25.3 %collective-permute-start.30 = (bf16[4,2,1,64,1024]{4,3,2,1,0:T(8,128)(2,1)S(1)}, bf16[4,2,1,64,1024]{4,3,2,1,0:T(8,128)(2,1)S(1)}, u32[]{:S(2)}, u32[]{:S(2)}) collective-permute-start(bf16[4,2,1,64,1024]{4,3,2,1,0:T(8,128)(2,1)S(1)} %bitcast.256), channel_id=1, source_target_pairs={{0,2},{1,3},{2,0},{3,1},{4,6},{5,7},{6,4},{7,5},{8,10},{9,11},{10,... | collective-permute-start | bytes 3145736 | tf_op jit(solution)/shard_map/ppermute | solution.py:1005
  168.9 18.1 %collective-permute-start.31 = (bf16[4,2,1,64,1024]{4,3,2,1,0:T(8,128)(2,1)S(1)}, bf16[4,2,1,64,1024]{4,3,2,1,0:T(8,128)(2,1)S(1)}, u32[]{:S(2)}, u32[]{:S(2)}) collective-permute-start(bf16[4,2,1,64,1024]{4,3,2,1,0:T(8,128)(2,1)S(1)} %collective-permute-done.28.refs_1_), channel_id=1, source_target_pairs={{0,2},{1,3},{2,0},{3,1},{4,6},{5,7},{6,4},{7,5},{8,10},{9,11},{10,... | collective-permute-start | bytes 3145736 | tf_op jit(solution)/shard_map/ppermute | solution.py:1005
  189.7 18.4 %collective-permute-start.37 = (bf16[8,256,1024]{2,1,0:T(8,128)(2,1)S(1)}, bf16[8,256,1024]{2,1,0:T(8,128)(2,1)}, u32[]{:S(2)}, u32[]{:S(2)}) collective-permute-start(bf16[8,256,1024]{2,1,0:T(8,128)(2,1)S(1)} %get-tuple-element.293), channel_id=1, source_target_pairs={{0,2},{1,3},{2,0},{3,1},{4,6},{5,7},{6,4},{7,5},{8,10},{9,11},{10,... | collective-permute-start | bytes 12582920 | tf_op jit(solution)/shard_map/ppermute | solution.py:1005
  224.4 35.8 %collective-permute-start.40 = (bf16[8,64,4096]{2,1,0:T(8,128)(2,1)}, bf16[8,64,4096]{2,1,0:T(8,128)(2,1)}, u32[]{:S(2)}, u32[]{:S(2)}) collective-permute-start(bf16[8,64,4096]{2,1,0:T(8,128)(2,1)} %get-tuple-element.305), channel_id=1, source_target_pairs={{0,2},{1,3},{2,0},{3,1},{4,6},{5,7},{6,4},{7,5},{8,10},{9,11},{10,... | collective-permute-start | bytes 12582920 | tf_op jit(solution)/shard_map/ppermute | solution.py:1005
  232.3 26.8 %collective-permute-start.39 = (bf16[4,2,64,1024]{3,2,1,0:T(8,128)(2,1)}, bf16[4,2,64,1024]{3,2,1,0:T(8,128)(2,1)S(1)}, u32[]{:S(2)}, u32[]{:S(2)}) collective-permute-start(bf16[4,2,64,1024]{3,2,1,0:T(8,128)(2,1)} %get-tuple-element.416), channel_id=1, source_target_pairs={{0,4},{1,5},{2,6},{3,7},{4,0},{5,1},{6,2},{7,3},{8,12},{9,13},{10,... | collective-permute-start | bytes 3145736 | tf_op jit(solution)/shard_map/ppermute | solution.py:1005
  235.0 25.1 %collective-permute-start.38 = (bf16[4,2,64,1024]{3,2,1,0:T(8,128)(2,1)}, bf16[4,2,64,1024]{3,2,1,0:T(8,128)(2,1)S(1)}, u32[]{:S(2)}, u32[]{:S(2)}) collective-permute-start(bf16[4,2,64,1024]{3,2,1,0:T(8,128)(2,1)} %get-tuple-element.418), channel_id=1, source_target_pairs={{0,1},{1,0},{2,3},{3,2},{4,5},{5,4},{6,7},{7,6},{8,9},{9,8},{10,11... | collective-permute-start | bytes 3145736 | tf_op jit(solution)/shard_map/ppermute | solution.py:1005
  265.7 38.1 %collective-permute-start.44 = (bf16[4,2,32,2048]{3,2,1,0:T(8,128)(2,1)}, bf16[4,2,32,2048]{3,2,1,0:T(8,128)(2,1)}, u32[]{:S(2)}, u32[]{:S(2)}) collective-permute-start(bf16[4,2,32,2048]{3,2,1,0:T(8,128)(2,1)} %get-tuple-element.412), channel_id=1, source_target_pairs={{0,4},{1,5},{2,6},{3,7},{4,0},{5,1},{6,2},{7,3},{8,12},{9,13},{10,... | collective-permute-start | bytes 3145736 | tf_op jit(solution)/shard_map/ppermute | solution.py:1005
  267.7 36.2 %collective-permute-start.43 = (bf16[4,2,32,2048]{3,2,1,0:T(8,128)(2,1)}, bf16[4,2,32,2048]{3,2,1,0:T(8,128)(2,1)S(1)}, u32[]{:S(2)}, u32[]{:S(2)}) collective-permute-start(bf16[4,2,32,2048]{3,2,1,0:T(8,128)(2,1)} %get-tuple-element.414), channel_id=1, source_target_pairs={{0,1},{1,0},{2,3},{3,2},{4,5},{5,4},{6,7},{7,6},{8,9},{9,8},{10,11... | collective-permute-start | bytes 3145736 | tf_op jit(solution)/shard_map/ppermute | solution.py:1005
  270.6 33.3 %collective-permute-start.42 = (bf16[4,64,1024]{2,1,0:T(8,128)(2,1)}, bf16[4,64,1024]{2,1,0:T(8,128)(2,1)}, u32[]{:S(2)}, u32[]{:S(2)}) collective-permute-start(bf16[4,64,1024]{2,1,0:T(8,128)(2,1)} %get-tuple-element.430), channel_id=1, source_target_pairs={{0,1},{1,0},{2,3},{3,2},{4,5},{5,4},{6,7},{7,6},{8,9},{9,8},{10,11... | collective-permute-start | bytes 1572872 | tf_op jit(solution)/shard_map/ppermute | solution.py:1005
  272.9 31.0 %collective-permute-start.41 = (bf16[4,64,1024]{2,1,0:T(8,128)(2,1)}, bf16[4,64,1024]{2,1,0:T(8,128)(2,1)}, u32[]{:S(2)}, u32[]{:S(2)}) collective-permute-start(bf16[4,64,1024]{2,1,0:T(8,128)(2,1)} %get-tuple-element.432), channel_id=1, source_target_pairs={{0,4},{1,5},{2,6},{3,7},{4,0},{5,1},{6,2},{7,3},{8,12},{9,13},{10,... | collective-permute-start | bytes 1572872 | tf_op jit(solution)/shard_map/ppermute | solution.py:1005
  324.2 100.7 %reduce-scatter.4.cloned.1.call-start = ((), (), s32[]{:S(2)}) async-start(), calls=%async_computation.3 | async-start | bytes 1310720 | tf_op jit(solution)/shard_map/reduce_scatter | solution.py:1029
  331.1 22.1 %collective-permute-start.49 = (bf16[4,2,32,1280]{3,2,1,0:T(8,128)(2,1)S(1)}, bf16[4,2,32,1280]{3,2,1,0:T(8,128)(2,1)S(1)}, u32[]{:S(2)}, u32[]{:S(2)}) collective-permute-start(bf16[4,2,32,1280]{3,2,1,0:T(8,128)(2,1)S(1)} %get-tuple-element.422), channel_id=1, source_target_pairs={{0,4},{1,5},{2,6},{3,7},{4,0},{5,1},{6,2},{7,3},{8,12},{9,13},{10,... | collective-permute-start | bytes 1966088 | tf_op jit(solution)/shard_map/ppermute | solution.py:1005
  332.7 20.6 %collective-permute-start.48 = (bf16[4,2,32,1280]{3,2,1,0:T(8,128)(2,1)S(1)}, bf16[4,2,32,1280]{3,2,1,0:T(8,128)(2,1)S(1)}, u32[]{:S(2)}, u32[]{:S(2)}) collective-permute-start(bf16[4,2,32,1280]{3,2,1,0:T(8,128)(2,1)S(1)} %get-tuple-element.424), channel_id=1, source_target_pairs={{0,1},{1,0},{2,3},{3,2},{4,5},{5,4},{6,7},{7,6},{8,9},{9,8},{10,11... | collective-permute-start | bytes 1966088 | tf_op jit(solution)/shard_map/ppermute | solution.py:1005
  357.6 67.4 %reduce-scatter.8.cloned.1.call-start = ((), (), s32[]{:S(2)}) async-start(), calls=%async_computation.5 | async-start | bytes 819200 | tf_op jit(solution)/shard_map/reduce_scatter | solution.py:1029
  373.3 19.8 %collective-permute-start.54 = (bf16[4,2,32,768]{3,2,1,0:T(8,128)(2,1)S(1)}, bf16[4,2,32,768]{3,2,1,0:T(8,128)(2,1)S(1)}, u32[]{:S(2)}, u32[]{:S(2)}) collective-permute-start(bf16[4,2,32,768]{3,2,1,0:T(8,128)(2,1)S(1)} %get-tuple-element.434), channel_id=1, source_target_pairs={{0,4},{1,5},{2,6},{3,7},{4,0},{5,1},{6,2},{7,3},{8,12},{9,13},{10,... | collective-permute-start | bytes 1179656 | tf_op jit(solution)/shard_map/ppermute | solution.py:1005
  373.9 19.2 %collective-permute-start.53 = (bf16[4,2,32,768]{3,2,1,0:T(8,128)(2,1)S(1)}, bf16[4,2,32,768]{3,2,1,0:T(8,128)(2,1)S(1)}, u32[]{:S(2)}, u32[]{:S(2)}) collective-permute-start(bf16[4,2,32,768]{3,2,1,0:T(8,128)(2,1)S(1)} %get-tuple-element.436), channel_id=1, source_target_pairs={{0,1},{1,0},{2,3},{3,2},{4,5},{5,4},{6,7},{7,6},{8,9},{9,8},{10,11... | collective-permute-start | bytes 1179656 | tf_op jit(solution)/shard_map/ppermute | solution.py:1005
  394.0 22.4 %collective-permute-start.57 = (f32[12,1024]{1,0:T(8,128)S(1)}, f32[12,1024]{1,0:T(8,128)S(1)}, u32[]{:S(2)}, u32[]{:S(2)}) collective-permute-start(f32[12,1024]{1,0:T(8,128)S(1)} %pad_maximum_fusion.14), channel_id=1, source_target_pairs={{0,2},{1,3},{2,0},{3,1},{4,6},{5,7},{6,4},{7,5},{8,10},{9,11},{10,... | collective-permute-start | bytes 147464 | tf_op jit(solution)/shard_map/ppermute | solution.py:1005
  394.1 22.4 %collective-permute-start.58 = (f32[12,1024]{1,0:T(8,128)S(1)}, f32[12,1024]{1,0:T(8,128)S(1)}, u32[]{:S(2)}, u32[]{:S(2)}) collective-permute-start(f32[12,1024]{1,0:T(8,128)S(1)} %pad_maximum_fusion.14), channel_id=1, source_target_pairs={{0,1},{1,0},{2,3},{3,2},{4,5},{5,4},{6,7},{7,6},{8,9},{9,8},{10,11... | collective-permute-start | bytes 147464 | tf_op jit(solution)/shard_map/ppermute | solution.py:1005
  395.0 21.4 %collective-permute-start.59 = (f32[12,1024]{1,0:T(8,128)S(1)}, f32[12,1024]{1,0:T(8,128)S(1)}, u32[]{:S(2)}, u32[]{:S(2)}) collective-permute-start(f32[12,1024]{1,0:T(8,128)S(1)} %pad_maximum_fusion.14), channel_id=1, source_target_pairs={{0,3},{1,2},{2,1},{3,0},{4,7},{5,6},{6,5},{7,4},{8,11},{9,10},{10,... | collective-permute-start | bytes 147464 | tf_op jit(solution)/shard_map/ppermute | solution.py:1005
  396.1 20.4 %collective-permute-start.56 = (bf16[4,32,768]{2,1,0:T(8,128)(2,1)S(1)}, bf16[4,32,768]{2,1,0:T(8,128)(2,1)S(1)}, u32[]{:S(2)}, u32[]{:S(2)}) collective-permute-start(bf16[4,32,768]{2,1,0:T(8,128)(2,1)S(1)} %get-tuple-element.448), channel_id=1, source_target_pairs={{0,1},{1,0},{2,3},{3,2},{4,5},{5,4},{6,7},{7,6},{8,9},{9,8},{10,11... | collective-permute-start | bytes 589832 | tf_op jit(solution)/shard_map/ppermute | solution.py:1005
  397.2 19.3 %collective-permute-start.55 = (bf16[4,32,768]{2,1,0:T(8,128)(2,1)S(1)}, bf16[4,32,768]{2,1,0:T(8,128)(2,1)S(1)}, u32[]{:S(2)}, u32[]{:S(2)}) collective-permute-start(bf16[4,32,768]{2,1,0:T(8,128)(2,1)S(1)} %get-tuple-element.450), channel_id=1, source_target_pairs={{0,4},{1,5},{2,6},{3,7},{4,0},{5,1},{6,2},{7,3},{8,12},{9,13},{10,... | collective-permute-start | bytes 589832 | tf_op jit(solution)/shard_map/ppermute | solution.py:1005
  (129 other events, 859.7 us)
Sparse Core Ops, SparseCore 0:
  36.4 30.7 all-gather.4
  77.1 30.0 all-gather.6
  324.4 29.5 reduce-scatter.5
  357.7 28.6 reduce-scatter.3
  388.6 20.8 reduce-scatter.7

commit v5 on v4

--- a/solution.py
+++ b/solution.py
@@ -65,9 +65,8 @@
         o_ref[i*BQ:(i+1)*BQ,:]=jnp.where(first,outs[0],outs[1]).astype(bf16)
         lse_ref[i*BQ:(i+1)*BQ,:]=jnp.where(first,lses[0],lses[1])
 
-def attn_fwd(length,slopes,qkv,start):
+def attn_fwd(length,slopes,qkv):
     n=qkv.shape[0]; D=qkv.shape[1]//3; np_=D//128
-    length=jnp.stack([length,jnp.int32(start)])
     spec=lambda off: pl.BlockSpec((n,128),lambda p,*_: (0,p+off))
     return pl.pallas_call(attn_fwd_kernel,
         grid_spec=pltpu.PrefetchScalarGridSpec(num_scalar_prefetch=2,grid=(np_,),
@@ -136,7 +135,6 @@
 
 def attn_bwd(length,slopes3,qkv,o,lse,do,start):
     n=qkv.shape[0]; D=qkv.shape[1]//3; np_=D//128
-    length=jnp.stack([length,jnp.int32(start)])
     spec=lambda off: pl.BlockSpec((n,128),lambda p,*_: (0,p+off))
     return pl.pallas_call(attn_bwd_kernel,
         grid_spec=pltpu.PrefetchScalarGridSpec(num_scalar_prefetch=2,grid=(np_,),
@@ -665,6 +663,35 @@
     )(where, *u, g)
 
 
+def divide_kernel(place_ref, keep_ref, got_ref, ka_ref, ga_ref, kb_ref, gb_ref, sum_ref):
+    y, x = place_ref[1], place_ref[3]
+    total = keep_ref[...].astype(f32) + got_ref[...].astype(f32)
+    sum_ref[...] = total.astype(bf16).reshape(sum_ref.shape)
+    ka_ref[...] = sum_ref[:, pl.ds(x, 1), :64, :].reshape(ka_ref.shape)
+    ga_ref[...] = sum_ref[:, pl.ds(1 - x, 1), :64, :].reshape(ga_ref.shape)
+    kb_ref[...] = sum_ref[pl.ds(y, 1), :, 64:, :].reshape(kb_ref.shape)
+    gb_ref[...] = sum_ref[pl.ds(1 - y, 1), :, 64:, :].reshape(gb_ref.shape)
+
+
+def divide_call(place, keep, got):
+    d = keep.shape[2]
+    block = spec((2, 256, d), lambda i, *_: (i, 0, 0))
+    return pl.pallas_call(
+        divide_kernel,
+        grid_spec=pltpu.PrefetchScalarGridSpec(
+            num_scalar_prefetch=1,
+            grid=(4,),
+            in_specs=[block, block],
+            out_specs=[spec((1, 2, 64, d), lambda i, *_: (i, 0, 0, 0))] * 4,
+            scratch_shapes=[pltpu.VMEM((2, 2, 128, d), bf16)],
+        ),
+        out_shape=[jax.ShapeDtypeStruct((4, 2, 64, d), bf16)] * 4,
+        compiler_params=params(20),
+        cost_estimate=pl.CostEstimate(flops=2**21, bytes_accessed=12 * 2**20, transcendentals=0),
+        name="divide",
+    )(place, keep, got)
+
+
 def down_kernel(place_ref, *refs):
     pieces, (u0_ref, u1_ref, h_ref, b_ref, o_ref, acc_ref, w_ref, sems) = refs[:10], refs[10:]
     step = pl.program_id(0)
@@ -1122,6 +1149,10 @@
     bias0 = jnp.concatenate([qkv_bias[:512], no_bias, qkv_bias[1024:1536]])
     bias1 = jnp.concatenate([qkv_bias[512:1024], no_bias, qkv_bias[1536:]])
 
+    bias0, bias1 = bias0.reshape(1, 1536), bias1.reshape(1, 1536)
+    first_heads, other_heads = (jnp.stack([length, jnp.int32(s)]) for s in (0, 4))
+    split_slopes = jnp.asarray(slopes_split)
+
     one_z = gather_z(one)
     one_z, two, tokens, cotangent = tie(one_z, two, tokens, cotangent)
 
@@ -1131,6 +1162,9 @@
     also_za, also_zb = halves([p[:, 3:] for p in one_z])
     one_x, one_y, also_za, also_zb, tokens, cotangent = tie(
         one_x, one_y, also_za, also_zb, tokens, cotangent
+    )
+    place_vec, bias0, bias1, first_heads, other_heads, valid, one_x = tie(
+        place_vec, bias0, bias1, first_heads, other_heads, valid, one_x
     )
 
     one_a, one_b = jnp.stack([a, one_x]), jnp.stack([b, one_y])
@@ -1154,7 +1188,7 @@
     also_xy, also_yx = send(also_a, OVER_Y), send(also_b, OVER_X)
     also_ca, also_cb = send(also_a, OVER_C), send(also_b, OVER_C)
     three_z = gather_z_line(three)
-    context0, lse0 = attn_fwd(length, jnp.asarray(slopes_split), qkv0, 0)
+    context0, lse0 = attn_fwd(first_heads, split_slopes, qkv0)
     context0, also_xy, also_yx, also_ca, also_cb, a1 = tie(
         context0, also_xy, also_yx, also_ca, also_cb, a1
     )
@@ -1166,7 +1200,7 @@
     two_x, two_y = plain(send(two_z, OVER_X)), plain(send(two_z, OVER_Y))
     qkv1, w1 = qkv_call(place_vec, pieces, a1, bias1, True)
     qkv1, two_c, three_z = tie(qkv1, two_c, three_z)
-    context1, lse1 = attn_fwd(length, jnp.asarray(slopes_split), qkv1, 4)
+    context1, lse1 = attn_fwd(other_heads, split_slopes, qkv1)
     context0, context1, two_x, two_y, three_z = tie(context0, context1, two_x, two_y, three_z)
 
     two_xy, two_yx = send(two_x[:, 0], OVER_Y), send(two_y[:, 1], OVER_X)
@@ -1203,8 +1237,8 @@
     down_got = send(down_give, OVER_C)
     grad_before, up_bias_grad = gate_call(place_vec, pieces, grad_low, (slope0, slope1))
     grad_before, a2, down_got = tie(grad_before, a2, down_got)
-    down = add_low(down_keep, down_got).reshape(4, 2, 2, 2, 64, 1024)
-    down = fold_second(down[:, :, :, 0], down[:, :, :, 1], place)
+    keep_a, give_a, keep_b, give_b = divide_call(place_vec, down_keep, down_got)
+    down = (keep_a, send(give_a, OVER_X)), (keep_b, send(give_b, OVER_Y))
     up_keep, up_give = up_grad_call(place_vec, a2, grad_before)
     grad_before, up_keep, up_give = tie(grad_before, up_keep, up_give)
 
@@ -1224,11 +1258,11 @@
     ).reshape(8, 1024)
     grad_context = dense_back_call(grad_low_hidden, w1)
     q0, k0, v0 = attn_bwd(
-        length, jnp.asarray(slopes_split), qkv0, context0, lse0, grad_context, 0
+        first_heads, split_slopes, qkv0, context0, lse0, grad_context, 0
     )
     q0, k0, v0, down, up, a1, early = tie(q0, k0, v0, down, up, a1, early)
 
-    owner_down = scatter_z_line(both(down))
+    owner_down = scatter_z_line(plain(both(down)))
     up = fold_third(up, place)
     third_keep, third_give, sums0 = columns_call(
         place_vec,
@@ -1246,7 +1280,7 @@
     third = add_low(third_keep, third_got).reshape(4, 2, 2, 32, 2560)
     third = fold_second(third[..., :1280], third[..., 1280:], place)
     q1, k1, v1 = attn_bwd(
-        length, jnp.asarray(slopes_split), qkv1, context1, lse1, grad_context, 4
+        other_heads, split_slopes, qkv1, context1, lse1, grad_context, 4
     )
     q1, k1, v1, third = tie(q1, k1, v1, third)
 

time: 452 us -> 449 us (level)
  Pallas kernels: 237 us -> 244 us
  local copies, waits for them, and re-layouts: 46.8 us -> 40.6 us
    pallas_call x0 -> x1, Pallas kernels: none -> 6.61 us  [divide_call(): pl.pallas_call(divide_kernel, grid_spec=pltpu.PrefetchScalarGridSpec(num_...]
    unnamed x202 -> x194, local copies, waits for them, and re-layouts: 23.9 us -> 20.2 us
    squeeze x16 -> x14, local copies, waits for them, and re-layouts: 10.3 us -> 7.55 us  [take(): return lax.dynamic_index_in_dim(array, at, axis, keepdims=False)]
    convert_element_type x12 -> x11, other arithmetic: 16 us -> 14.3 us  [add_low(): return (a.astype(f32) + b.astype(f32)).astype(bf16)]
  transfers between devices with their start and end apart: 72 -> 72, of which waited for: 22 -> 20; matrix products, arithmetic and copies ran while one was open for 12% -> 11% of each run, Pallas kernels for 50% -> 52%
where the time goes in v5:
time: 449 us; the launch traced here: 443 us
  Pallas kernels  244 us (54%)
  starting transfers between devices  62.9 us (14%)
  other arithmetic  44.5 us (10%)
  local copies, waits for them, and re-layouts  40.6 us (9%)
  waiting for transfers between devices  35.3 us (8%)
  between operations  15.6 us (3%)
    ppermute x67, starting transfers between devices, send(): return lax.ppermute(array, ALL, pairs)  61.9 us
    pallas_call x2, Pallas kernels, attn_bwd(): pl.pallas_call(attn_bwd_kernel, grid_spec=pltpu.PrefetchScalarGridSpec(nu...  39.9 us
    ppermute x67, waiting for transfers between devices, send(): return lax.ppermute(array, ALL, pairs)  34.3 us
    pallas_call x2, Pallas kernels, attn_fwd(): pl.pallas_call(attn_fwd_kernel, grid_spec=pltpu.PrefetchScalarGridSpec(nu...  25.6 us
    pallas_call x1, Pallas kernels, up_call(): pl.pallas_call(up_kernel, grid_spec=pltpu.PrefetchScalarGridSpec(num_scal...  24.9 us
    pallas_call x1, Pallas kernels, norm_up_call(): pl.pallas_call(norm_up_kernel, grid_spec=pltpu.PrefetchScalarGridSpec(num...  23.6 us
    unnamed x194, local copies, waits for them, and re-layouts  20.2 us
    pallas_call x2, Pallas kernels, qkv_call(): pl.pallas_call(functools.partial(qkv_kernel, turned), grid_spec=pltpu.Pre...  18.9 us
  transfers between devices with their start and end apart: 72, of which 20 were waited for; matrix products, arithmetic and copies ran while one was open for 11% of the time, Pallas kernels for 52%

profile of v5, /device:TPU:0, one launch (start us, length us, event | category | flops | bytes accessed | tf_op | source)
XLA Modules:
  0.0 442.5 jit_solution(12567196373674524937)
XLA Ops:
  9.0 3.1 collective-permute-start
  12.0 2.6 collective-permute-start.1
  25.4 6.4 %collective-permute-done.1 = bf16[2,8,16,512]{3,2,1,0:T(8,128)(2,1)S(1)} collective-permute-done((bf16[2,8,16,512]{3,2,1,0:T(8,128)(2,1)S(1)}, bf16[2,8,16,512]{3,2,1,0:T(8,128)(2,1)S(1)}, u32[]{:S(2)}, u32[]{:S(2)}) %collective-permute-start.1) | collective-permute-done | bytes 262176 | tf_op jit(solution)/shard_map/ppermute | solution.py:1032
  36.5 3.1 collective-permute-done.4
  48.6 2.1 fusion.5.refs_8_.refs_2_.refs_0_
  52.4 4.3 collective-permute-done.5.refs_1_
  61.0 9.1 %qkv.2 = (bf16[1024,1536]{1,0:T(8,128)(2,1)}, bf16[3,1024,512]{2,1,0:T(8,128)(2,1)}) custom-call(s32[4]{0:T(128)} %pad_add_fusion.place_ref.where_ref, bf16[2,4,3,16,512]{4,3,2,1,0:T(8,128)(2,1)} %copy-done.51, bf16[2,4,3,16,512]{4,3,2,1,0:T(8,128)(2,1)} %copy-done.79, bf16[2,4,3,16,512]{4,3,2,1,0:T(8,128)(2,1)} %copy-done.80, ...), custom_call_target="tpu_custom_call" | custom-call | flops 3221225472 | bytes 13631488 | tf_op jit(solution)/shard_map/qkv/pallas_call | solution.py:486
  77.1 12.7 %attn_fwd.2 = (bf16[1024,512]{1,0:T(8,128)(2,1)}, f32[1024,512]{1,0:T(8,128)}) custom-call(s32[2]{0:T(128)} %get-tuple-element.229.len_ref, f32[48]{0:T(128)} %constant.173.clone.slope_ref, bf16[1024,1536]{1,0:T(8,128)(2,1)} %get-tuple-element.249.q_ref.k_ref.v_ref, bf16[1024,1536]{1,0:T(8,128)(2,1)} %get-tuple-element.249.q_ref.k_ref.v_ref, ...), custom_call_target="tpu_custom_call" | custom-call | flops 5368709120 | bytes 6291456 | tf_op jit(solution)/shard_map/attn_fwd/pallas_call | solution.py:71
  89.8 2.2 collective-permute-done.13.refs_1_
  96.1 9.8 %qkv.3 = (bf16[1024,1536]{1,0:T(8,128)(2,1)}, bf16[5,1024,512]{2,1,0:T(8,128)(2,1)}) custom-call(s32[4]{0:T(128)} %pad_add_fusion.place_ref.where_ref, bf16[2,4,5,16,512]{4,3,2,1,0:T(8,128)(2,1)} %copy-done.47, bf16[2,4,5,16,512]{4,3,2,1,0:T(8,128)(2,1)} %collective-permute-done.13.refs_1_, bf16[2,4,5,16,512]{4,3,2,1,0:T(8,128)(2,1)} %collective-permute-done.15.refs_2_, ...), custom_call_target="tpu_custom_call" | custom-call | flops 3221225472 | bytes 13631488 | tf_op jit(solution)/shard_map/qkv/pallas_call | solution.py:486
  106.7 12.9 %attn_fwd.3 = (bf16[1024,512]{1,0:T(8,128)(2,1)}, f32[1024,512]{1,0:T(8,128)}) custom-call(s32[2]{0:T(128)} %get-tuple-element.254.len_ref, f32[48]{0:T(128)} %constant.173.clone.slope_ref, bf16[1024,1536]{1,0:T(8,128)(2,1)} %get-tuple-element.357.q_ref.k_ref.v_ref, bf16[1024,1536]{1,0:T(8,128)(2,1)} %get-tuple-element.357.q_ref.k_ref.v_ref, ...), custom_call_target="tpu_custom_call" | custom-call | flops 5368709120 | bytes 6291456 | tf_op jit(solution)/shard_map/attn_fwd/pallas_call | solution.py:71
  127.9 5.6 %dense.1 = (f32[1024,1024]{1,0:T(8,128)S(1)}, bf16[1024,1024]{1,0:T(8,128)(2,1)S(1)}) custom-call(bf16[1024,512]{1,0:T(8,128)(2,1)S(1)} %copy-done.15, bf16[1024,512]{1,0:T(8,128)(2,1)S(1)} %copy-done.12, bf16[5,1024,512]{2,1,0:T(8,128)(2,1)} %get-tuple-element.271.w0_ref.w1_ref.refs_7_, bf16[5,1024,512]{2,1,0:T(8,128)(2,1)} %get-tuple-element.271.w0_ref.w1_ref.refs_7_, ...), custom_call_target="tpu_custom_call" | custom-call | flops 2147483648 | bytes 12582912 | tf_op jit(solution)/shard_map/dense/pallas_call | solution.py:528
  143.2 24.9 %up.1 = (bf16[1024,2048]{1,0:T(8,128)(2,1)}, bf16[1024,2048]{1,0:T(8,128)(2,1)}, bf16[1024,2048]{1,0:T(8,128)(2,1)}, bf16[1024,2048]{1,0:T(8,128)(2,1)}) custom-call(s32[4]{0:T(128)} %pad_add_fusion.place_ref.where_ref, bf16[4,2,2,32,1024]{4,3,2,1,0:T(8,128)(2,1)} %bitcast.22.refs_0_, bf16[4,2,2,32,1024]{4,3,2,1,0:T(8,128)(2,1)} %collective-permute-done.20.refs_1_, ...), custom_call_target="tpu_custom_call" | custom-call | flops 8589934592 | bytes 27262976 | tf_op jit(solution)/shard_map/up/pallas_call | solution.py:606
  171.1 14.0 %down_grad.1 = (bf16[8,256,1024]{2,1,0:T(8,128)(2,1)S(1)}, bf16[8,256,1024]{2,1,0:T(8,128)(2,1)}) custom-call(s32[4]{0:T(128)S(1)} %copy-done.21, bf16[1024,2048]{1,0:T(8,128)(2,1)} %get-tuple-element.387.u0_ref.refs_10_, bf16[1024,2048]{1,0:T(8,128)(2,1)} %get-tuple-element.293.u1_ref.refs_11_, bf16[1024,1024]{1,0:T(8,128)(2,1)S(1)} %copy-done.2), custom_call_target="tpu_custom_call" | custom-call | flops 8589934592 | bytes 18874368 | tf_op jit(solution)/shard_map/down_grad/pallas_call | solution.py:644
  188.7 17.5 %gate.1 = (bf16[1024,4096]{1,0:T(8,128)(2,1)}, f32[1,4096]{1,0:T(1,128)}) custom-call(s32[4]{0:T(128)} %pad_add_fusion.place_ref.where_ref, bf16[4,2,1,64,1024]{4,3,2,1,0:T(8,128)(2,1)} %bitcast.242, bf16[4,2,1,64,1024]{4,3,2,1,0:T(8,128)(2,1)} %copy-done.56, bf16[4,2,1,64,1024]{4,3,2,1,0:T(8,128)(2,1)} %copy-done.57, bf16[4,1,64,1024]{3,2,1,0:T(8,128)(2,1)} %copy-done.69, ...), custom_call_target="tpu_custom_call" | custom-call | flops 8589934592 | bytes 27262976 | tf_op jit(solution)/shard_map/gate/pallas_call | solution.py:774
  206.2 14.4 %up_grad.1 = (bf16[8,64,4096]{2,1,0:T(8,128)(2,1)S(1)}, bf16[8,64,4096]{2,1,0:T(8,128)(2,1)}) custom-call(s32[4]{0:T(128)S(1)} %copy-done.22, bf16[1024,1024]{1,0:T(8,128)(2,1)S(1)} %copy-done.28, bf16[1024,4096]{1,0:T(8,128)(2,1)} %get-tuple-element.316.g_ref.refs_10_), custom_call_target="tpu_custom_call" | custom-call | flops 8589934592 | bytes 18874368 | tf_op jit(solution)/shard_map/up_grad/pallas_call | solution.py:991
  220.8 6.6 %divide.1 = (bf16[4,2,64,1024]{3,2,1,0:T(8,128)(2,1)S(1)}, bf16[4,2,64,1024]{3,2,1,0:T(8,128)(2,1)}, bf16[4,2,64,1024]{3,2,1,0:T(8,128)(2,1)S(1)}, bf16[4,2,64,1024]{3,2,1,0:T(8,128)(2,1)}) custom-call(s32[4]{0:T(128)S(1)} %copy-done.22, bf16[8,256,1024]{2,1,0:T(8,128)(2,1)S(1)} %get-tuple-element.321.keep_ref, ...), custom_call_target="tpu_custom_call" | custom-call | flops 2097152 | bytes 12582912 | tf_op jit(solution)/shard_map/divide/pallas_call | solution.py:679
  229.5 23.6 %norm_up.1 = (bf16[1024,1024]{1,0:T(8,128)(2,1)}, f32[1024,1024]{1,0:T(8,128)}, f32[8,1024]{1,0:T(8,128)}) custom-call(s32[4]{0:T(128)} %pad_add_fusion.place_ref.where_ref, bf16[4,2,2,32,1024]{4,3,2,1,0:T(8,128)(2,1)} %bitcast.22.refs_0_, bf16[4,2,2,32,1024]{4,3,2,1,0:T(8,128)(2,1)} %collective-permute-done.20.refs_1_, ...), custom_call_target="tpu_custom_call" | custom-call | flops 8589934592 | bytes 33554432 | tf_op jit(solution)/shard_map/norm_up/pallas_call | solution.py:865
  254.2 3.7 add_convert_fusion
  270.0 3.0 dense_back.1.do_ref
  274.4 20.0 %attn_bwd.2 = (bf16[1024,512]{1,0:T(8,128)(2,1)S(1)}, bf16[1024,512]{1,0:T(8,128)(2,1)S(1)}, bf16[1024,512]{1,0:T(8,128)(2,1)S(1)}) custom-call(s32[2]{0:T(128)S(1)} %copy-done.25, f32[48]{0:T(128)S(1)} %copy-done.29, bf16[1024,1536]{1,0:T(8,128)(2,1)} %get-tuple-element.249.q_ref.k_ref.v_ref, bf16[1024,1536]{1,0:T(8,128)(2,1)} %get-tuple-element.249.q_ref.k_ref.v_ref, ...), custom_call_target="tpu_custom_call" | custom-call | flops 13421772800 | bytes 10485760 | tf_op jit(solution)/shard_map/attn_bwd/pallas_call | solution.py:139
  302.2 2.0 add_convert_fusion.4
  306.2 8.6 %dense_grad.1 = (bf16[8,64,2560]{2,1,0:T(8,128)(2,1)S(1)}, bf16[8,64,2560]{2,1,0:T(8,128)(2,1)}, f32[1,2560]{1,0:T(1,128)S(1)}) custom-call(s32[4]{0:T(128)S(1)} %copy-done.23, bf16[1024,512]{1,0:T(8,128)(2,1)S(1)} %copy-done.17, bf16[1024,512]{1,0:T(8,128)(2,1)S(1)} %copy-done.13, bf16[1024,1024]{1,0:T(8,128)(2,1)S(1)} %copy-done.8, ...), custom_call_target="tpu_custom_call" | custom-call | flops 5368709120 | bytes 14680064 | tf_op jit(solution)/shard_map/dense_grad/pallas_call | solution.py:958
  314.8 2.2 collective-permute-done.45
  324.7 2.4 add_convert_fusion.1
  329.7 19.9 %attn_bwd.3 = (bf16[1024,512]{1,0:T(8,128)(2,1)S(1)}, bf16[1024,512]{1,0:T(8,128)(2,1)S(1)}, bf16[1024,512]{1,0:T(8,128)(2,1)S(1)}) custom-call(s32[2]{0:T(128)S(1)} %copy-done.24, f32[48]{0:T(128)S(1)} %copy-done.29, bf16[1024,1536]{1,0:T(8,128)(2,1)} %get-tuple-element.357.q_ref.k_ref.v_ref, bf16[1024,1536]{1,0:T(8,128)(2,1)} %get-tuple-element.357.q_ref.k_ref.v_ref, ...), custom_call_target="tpu_custom_call" | custom-call | flops 13421772800 | bytes 10485760 | tf_op jit(solution)/shard_map/attn_bwd/pallas_call | solution.py:139
  357.3 5.6 %heads_grad.1 = (bf16[8,64,1536]{2,1,0:T(8,128)(2,1)S(1)}, bf16[8,64,1536]{2,1,0:T(8,128)(2,1)}, f32[1,1536]{1,0:T(1,128)S(1)}) custom-call(s32[4]{0:T(128)S(1)} %copy-done.23, bf16[1024,1024]{1,0:T(8,128)(2,1)S(1)} %copy-done.9, bf16[1024,512]{1,0:T(8,128)(2,1)S(1)} %copy-done.37, bf16[1024,512]{1,0:T(8,128)(2,1)S(1)} %copy-done.39, ...), custom_call_target="tpu_custom_call" | custom-call | flops 3221225472 | bytes 10485760 | tf_op jit(solution)/shard_map/heads_grad/pallas_call | solution.py:958
  371.8 17.9 %norm_qkv.1 = (bf16[1024,1024]{1,0:T(8,128)(2,1)}, f32[8,1024]{1,0:T(8,128)}) custom-call(bf16[1024,512]{1,0:T(8,128)(2,1)} %copy-done.30, bf16[1024,512]{1,0:T(8,128)(2,1)} %copy-done.32, bf16[1024,512]{1,0:T(8,128)(2,1)} %copy-done.34, bf16[1024,512]{1,0:T(8,128)(2,1)} %copy-done.36, bf16[1024,512]{1,0:T(8,128)(2,1)} %copy-done.38, ...), custom_call_target="tpu_custom_call" | custom-call | flops 6442450944 | bytes 23068672 | tf_op jit(solution)/shard_map/norm_qkv/pallas_call | solution.py:911
  394.6 17.6 %down.1 = bf16[1024,1024]{1,0:T(8,128)(2,1)} custom-call(s32[4]{0:T(128)} %pad_add_fusion.place_ref.where_ref, bf16[4,2,1,64,1024]{4,3,2,1,0:T(8,128)(2,1)} %bitcast.243, bf16[4,2,1,64,1024]{4,3,2,1,0:T(8,128)(2,1)} %copy-done.56, bf16[4,2,1,64,1024]{4,3,2,1,0:T(8,128)(2,1)} %copy-done.57, bf16[4,1,64,1024]{3,2,1,0:T(8,128)(2,1)} %copy-done.69, ...), custom_call_target="tpu_custom_call" | custom-call | flops 8589934592 | bytes 23068672 | tf_op jit(solution)/shard_map/down/pallas_call | solution.py:726
  413.9 5.4 %collective-permute-start.64 = (bf16[2,32,768]{2,1,0:T(8,128)(2,1)S(1)}, bf16[2,32,768]{2,1,0:T(8,128)(2,1)S(1)}, u32[]{:S(2)}, u32[]{:S(2)}) collective-permute-start(bf16[2,32,768]{2,1,0:T(8,128)(2,1)S(1)} %get-tuple-element.462), channel_id=1, source_target_pairs={{0,8},{1,9},{2,10},{3,11},{4,12},{5,13},{6,14},{7,15},{8,16},{9,17... | collective-permute-start | bytes 294920 | tf_op jit(solution)/shard_map/ppermute | solution.py:1032
  422.0 2.3 collective-permute-start.62
  429.5 3.6 collective-permute-done.62
  (433 shorter events, 137.9 us)
Async XLA Ops:
  7.2 63.0 %all-gather.5.cloned.1.call-start = ((), (), s32[]{:S(2)}) async-start(), calls=%async_computation.6 | async-start | bytes 1310720 | tf_op jit(solution)/shard_map/all_gather | solution.py:1052
  12.0 19.7 %collective-permute-start.1 = (bf16[2,8,16,512]{3,2,1,0:T(8,128)(2,1)S(1)}, bf16[2,8,16,512]{3,2,1,0:T(8,128)(2,1)S(1)}, u32[]{:S(2)}, u32[]{:S(2)}) collective-permute-start(bf16[2,8,16,512]{3,2,1,0:T(8,128)(2,1)S(1)} %bitcast.205), channel_id=1, source_target_pairs={{0,16},{1,17},{2,18},{3,19},{4,20},{5,21},{6,22},{7,23},{8,24},{9,... | collective-permute-start | bytes 786440 | tf_op jit(solution)/shard_map/ppermute | solution.py:1032
  36.3 70.4 %all-gather.7.cloned.1.call-start = ((), (), s32[]{:S(2)}) async-start(), calls=%async_computation.7 | async-start | bytes 1310720 | tf_op jit(solution)/shard_map/all_gather | solution.py:1052
  72.2 17.7 %collective-permute-start.14 = (bf16[2,4,5,16,512]{4,3,2,1,0:T(8,128)(2,1)}, bf16[2,4,5,16,512]{4,3,2,1,0:T(8,128)(2,1)}, u32[]{:S(2)}, u32[]{:S(2)}) collective-permute-start(bf16[2,4,5,16,512]{4,3,2,1,0:T(8,128)(2,1)} %pad_maximum_fusion.3.refs_4_), channel_id=1, source_target_pairs={{0,1},{1,0},{2,3},{3,2},{4,5},{5,4},{6,7},{7,6},{8,9},{9,8},{10,11... | collective-permute-start | bytes 1966088 | tf_op jit(solution)/shard_map/ppermute | solution.py:1032
  76.5 345.2 %reduce-scatter.6.cloned.1.call-start = ((), (), s32[]{:S(2)}) async-start(), calls=%async_computation.4 | async-start | bytes 1310720 | tf_op jit(solution)/shard_map/reduce_scatter | solution.py:1056
  76.7 30.0 %collective-permute-start.19 = (bf16[4,2,2,32,1024]{4,3,2,1,0:T(8,128)(2,1)}, bf16[4,2,2,32,1024]{4,3,2,1,0:T(8,128)(2,1)}, u32[]{:S(2)}, u32[]{:S(2)}) collective-permute-start(bf16[4,2,2,32,1024]{4,3,2,1,0:T(8,128)(2,1)} %bitcast.22.refs_0_), channel_id=1, source_target_pairs={{0,2},{1,3},{2,0},{3,1},{4,6},{5,7},{6,4},{7,5},{8,10},{9,11},{10,... | collective-permute-start | bytes 3145736 | tf_op jit(solution)/shard_map/ppermute | solution.py:1032
  92.5 27.1 %collective-permute-start.20 = (bf16[4,2,2,32,1024]{4,3,2,1,0:T(8,128)(2,1)}, bf16[4,2,2,32,1024]{4,3,2,1,0:T(8,128)(2,1)}, u32[]{:S(2)}, u32[]{:S(2)}) collective-permute-start(bf16[4,2,2,32,1024]{4,3,2,1,0:T(8,128)(2,1)} %bitcast.22.refs_0_), channel_id=1, source_target_pairs={{0,1},{1,0},{2,3},{3,2},{4,5},{5,4},{6,7},{7,6},{8,9},{9,8},{10,11... | collective-permute-start | bytes 3145736 | tf_op jit(solution)/shard_map/ppermute | solution.py:1032
  93.1 26.6 %collective-permute-start.21 = (bf16[4,2,2,32,1024]{4,3,2,1,0:T(8,128)(2,1)}, bf16[4,2,2,32,1024]{4,3,2,1,0:T(8,128)(2,1)}, u32[]{:S(2)}, u32[]{:S(2)}) collective-permute-start(bf16[4,2,2,32,1024]{4,3,2,1,0:T(8,128)(2,1)} %bitcast.22.refs_0_), channel_id=1, source_target_pairs={{0,4},{1,5},{2,6},{3,7},{4,0},{5,1},{6,2},{7,3},{8,12},{9,13},{10,... | collective-permute-start | bytes 3145736 | tf_op jit(solution)/shard_map/ppermute | solution.py:1032
  119.7 17.9 %collective-permute-start.24 = (bf16[4,2,2,32,1024]{4,3,2,1,0:T(8,128)(2,1)}, bf16[4,2,2,32,1024]{4,3,2,1,0:T(8,128)(2,1)S(1)}, u32[]{:S(2)}, u32[]{:S(2)}) collective-permute-start(bf16[4,2,2,32,1024]{4,3,2,1,0:T(8,128)(2,1)} %collective-permute-done.20.refs_1_), channel_id=1, source_target_pairs={{0,2},{1,3},{2,0},{3,1},{4,6},{5,7},{6,4},{7,5},{8,10},{9,11},{10,... | collective-permute-start | bytes 3145736 | tf_op jit(solution)/shard_map/ppermute | solution.py:1032
  119.7 17.8 %collective-permute-start.25 = (bf16[4,2,2,32,1024]{4,3,2,1,0:T(8,128)(2,1)}, bf16[4,2,2,32,1024]{4,3,2,1,0:T(8,128)(2,1)S(1)}, u32[]{:S(2)}, u32[]{:S(2)}) collective-permute-start(bf16[4,2,2,32,1024]{4,3,2,1,0:T(8,128)(2,1)} %collective-permute-done.21.refs_2_), channel_id=1, source_target_pairs={{0,2},{1,3},{2,0},{3,1},{4,6},{5,7},{6,4},{7,5},{8,10},{9,11},{10,... | collective-permute-start | bytes 3145736 | tf_op jit(solution)/shard_map/ppermute | solution.py:1032
  141.1 27.0 %collective-permute-start.28 = (bf16[4,2,1,64,1024]{4,3,2,1,0:T(8,128)(2,1)S(1)}, bf16[4,2,1,64,1024]{4,3,2,1,0:T(8,128)(2,1)S(1)}, u32[]{:S(2)}, u32[]{:S(2)}) collective-permute-start(bf16[4,2,1,64,1024]{4,3,2,1,0:T(8,128)(2,1)S(1)} %bitcast.244), channel_id=1, source_target_pairs={{0,1},{1,0},{2,3},{3,2},{4,5},{5,4},{6,7},{7,6},{8,9},{9,8},{10,11... | collective-permute-start | bytes 3145736 | tf_op jit(solution)/shard_map/ppermute | solution.py:1032
  142.6 25.5 %collective-permute-start.29 = (bf16[4,2,1,64,1024]{4,3,2,1,0:T(8,128)(2,1)S(1)}, bf16[4,2,1,64,1024]{4,3,2,1,0:T(8,128)(2,1)S(1)}, u32[]{:S(2)}, u32[]{:S(2)}) collective-permute-start(bf16[4,2,1,64,1024]{4,3,2,1,0:T(8,128)(2,1)S(1)} %bitcast.245), channel_id=1, source_target_pairs={{0,4},{1,5},{2,6},{3,7},{4,0},{5,1},{6,2},{7,3},{8,12},{9,13},{10,... | collective-permute-start | bytes 3145736 | tf_op jit(solution)/shard_map/ppermute | solution.py:1032
  143.2 25.0 %collective-permute-start.30 = (bf16[4,2,1,64,1024]{4,3,2,1,0:T(8,128)(2,1)S(1)}, bf16[4,2,1,64,1024]{4,3,2,1,0:T(8,128)(2,1)S(1)}, u32[]{:S(2)}, u32[]{:S(2)}) collective-permute-start(bf16[4,2,1,64,1024]{4,3,2,1,0:T(8,128)(2,1)S(1)} %bitcast.246), channel_id=1, source_target_pairs={{0,2},{1,3},{2,0},{3,1},{4,6},{5,7},{6,4},{7,5},{8,10},{9,11},{10,... | collective-permute-start | bytes 3145736 | tf_op jit(solution)/shard_map/ppermute | solution.py:1032
  187.9 18.3 %collective-permute-start.37 = (bf16[8,256,1024]{2,1,0:T(8,128)(2,1)}, bf16[8,256,1024]{2,1,0:T(8,128)(2,1)}, u32[]{:S(2)}, u32[]{:S(2)}) collective-permute-start(bf16[8,256,1024]{2,1,0:T(8,128)(2,1)} %get-tuple-element.311), channel_id=1, source_target_pairs={{0,2},{1,3},{2,0},{3,1},{4,6},{5,7},{6,4},{7,5},{8,10},{9,11},{10,... | collective-permute-start | bytes 12582920 | tf_op jit(solution)/shard_map/ppermute | solution.py:1032
  220.6 33.6 %collective-permute-start.40 = (bf16[8,64,4096]{2,1,0:T(8,128)(2,1)}, bf16[8,64,4096]{2,1,0:T(8,128)(2,1)}, u32[]{:S(2)}, u32[]{:S(2)}) collective-permute-start(bf16[8,64,4096]{2,1,0:T(8,128)(2,1)} %get-tuple-element.327), channel_id=1, source_target_pairs={{0,2},{1,3},{2,0},{3,1},{4,6},{5,7},{6,4},{7,5},{8,10},{9,11},{10,... | collective-permute-start | bytes 12582920 | tf_op jit(solution)/shard_map/ppermute | solution.py:1032
  227.5 25.6 %collective-permute-start.38 = (bf16[4,2,64,1024]{3,2,1,0:T(8,128)(2,1)}, bf16[4,2,64,1024]{3,2,1,0:T(8,128)(2,1)}, u32[]{:S(2)}, u32[]{:S(2)}) collective-permute-start(bf16[4,2,64,1024]{3,2,1,0:T(8,128)(2,1)} %get-tuple-element.324), channel_id=1, source_target_pairs={{0,1},{1,0},{2,3},{3,2},{4,5},{5,4},{6,7},{7,6},{8,9},{9,8},{10,11... | collective-permute-start | bytes 3145736 | tf_op jit(solution)/shard_map/ppermute | solution.py:1032
  228.9 25.2 %collective-permute-start.39 = (bf16[4,2,64,1024]{3,2,1,0:T(8,128)(2,1)}, bf16[4,2,64,1024]{3,2,1,0:T(8,128)(2,1)}, u32[]{:S(2)}, u32[]{:S(2)}) collective-permute-start(bf16[4,2,64,1024]{3,2,1,0:T(8,128)(2,1)} %get-tuple-element.326), channel_id=1, source_target_pairs={{0,4},{1,5},{2,6},{3,7},{4,0},{5,1},{6,2},{7,3},{8,12},{9,13},{10,... | collective-permute-start | bytes 3145736 | tf_op jit(solution)/shard_map/ppermute | solution.py:1032
  259.8 38.5 %collective-permute-start.44 = (bf16[4,2,32,2048]{3,2,1,0:T(8,128)(2,1)}, bf16[4,2,32,2048]{3,2,1,0:T(8,128)(2,1)}, u32[]{:S(2)}, u32[]{:S(2)}) collective-permute-start(bf16[4,2,32,2048]{3,2,1,0:T(8,128)(2,1)} %get-tuple-element.432), channel_id=1, source_target_pairs={{0,4},{1,5},{2,6},{3,7},{4,0},{5,1},{6,2},{7,3},{8,12},{9,13},{10,... | collective-permute-start | bytes 3145736 | tf_op jit(solution)/shard_map/ppermute | solution.py:1032
  262.1 36.3 %collective-permute-start.43 = (bf16[4,2,32,2048]{3,2,1,0:T(8,128)(2,1)}, bf16[4,2,32,2048]{3,2,1,0:T(8,128)(2,1)}, u32[]{:S(2)}, u32[]{:S(2)}) collective-permute-start(bf16[4,2,32,2048]{3,2,1,0:T(8,128)(2,1)} %get-tuple-element.434), channel_id=1, source_target_pairs={{0,1},{1,0},{2,3},{3,2},{4,5},{5,4},{6,7},{7,6},{8,9},{9,8},{10,11... | collective-permute-start | bytes 3145736 | tf_op jit(solution)/shard_map/ppermute | solution.py:1032
  265.3 33.0 %collective-permute-start.42 = (bf16[4,64,1024]{2,1,0:T(8,128)(2,1)S(1)}, bf16[4,64,1024]{2,1,0:T(8,128)(2,1)S(1)}, u32[]{:S(2)}, u32[]{:S(2)}) collective-permute-start(bf16[4,64,1024]{2,1,0:T(8,128)(2,1)S(1)} %get-tuple-element.446), channel_id=1, source_target_pairs={{0,1},{1,0},{2,3},{3,2},{4,5},{5,4},{6,7},{7,6},{8,9},{9,8},{10,11... | collective-permute-start | bytes 1572872 | tf_op jit(solution)/shard_map/ppermute | solution.py:1032
  268.7 29.7 %collective-permute-start.41 = (bf16[4,64,1024]{2,1,0:T(8,128)(2,1)}, bf16[4,64,1024]{2,1,0:T(8,128)(2,1)S(1)}, u32[]{:S(2)}, u32[]{:S(2)}) collective-permute-start(bf16[4,64,1024]{2,1,0:T(8,128)(2,1)} %get-tuple-element.448), channel_id=1, source_target_pairs={{0,4},{1,5},{2,6},{3,7},{4,0},{5,1},{6,2},{7,3},{8,12},{9,13},{10,... | collective-permute-start | bytes 1572872 | tf_op jit(solution)/shard_map/ppermute | solution.py:1032
  320.8 100.9 %reduce-scatter.4.cloned.1.call-start = ((), (), s32[]{:S(2)}) async-start(), calls=%async_computation.3 | async-start | bytes 1310720 | tf_op jit(solution)/shard_map/reduce_scatter | solution.py:1056
  327.5 22.1 %collective-permute-start.49 = (bf16[4,2,32,1280]{3,2,1,0:T(8,128)(2,1)S(1)}, bf16[4,2,32,1280]{3,2,1,0:T(8,128)(2,1)S(1)}, u32[]{:S(2)}, u32[]{:S(2)}) collective-permute-start(bf16[4,2,32,1280]{3,2,1,0:T(8,128)(2,1)S(1)} %get-tuple-element.438), channel_id=1, source_target_pairs={{0,4},{1,5},{2,6},{3,7},{4,0},{5,1},{6,2},{7,3},{8,12},{9,13},{10,... | collective-permute-start | bytes 1966088 | tf_op jit(solution)/shard_map/ppermute | solution.py:1032
  329.0 20.6 %collective-permute-start.48 = (bf16[4,2,32,1280]{3,2,1,0:T(8,128)(2,1)S(1)}, bf16[4,2,32,1280]{3,2,1,0:T(8,128)(2,1)S(1)}, u32[]{:S(2)}, u32[]{:S(2)}) collective-permute-start(bf16[4,2,32,1280]{3,2,1,0:T(8,128)(2,1)S(1)} %get-tuple-element.440), channel_id=1, source_target_pairs={{0,1},{1,0},{2,3},{3,2},{4,5},{5,4},{6,7},{7,6},{8,9},{9,8},{10,11... | collective-permute-start | bytes 1966088 | tf_op jit(solution)/shard_map/ppermute | solution.py:1032
  353.2 68.6 %reduce-scatter.8.cloned.1.call-start = ((), (), s32[]{:S(2)}) async-start(), calls=%async_computation.5 | async-start | bytes 819200 | tf_op jit(solution)/shard_map/reduce_scatter | solution.py:1056
  369.2 20.6 %collective-permute-start.54 = (bf16[4,2,32,768]{3,2,1,0:T(8,128)(2,1)S(1)}, bf16[4,2,32,768]{3,2,1,0:T(8,128)(2,1)S(1)}, u32[]{:S(2)}, u32[]{:S(2)}) collective-permute-start(bf16[4,2,32,768]{3,2,1,0:T(8,128)(2,1)S(1)} %get-tuple-element.450), channel_id=1, source_target_pairs={{0,4},{1,5},{2,6},{3,7},{4,0},{5,1},{6,2},{7,3},{8,12},{9,13},{10,... | collective-permute-start | bytes 1179656 | tf_op jit(solution)/shard_map/ppermute | solution.py:1032
  370.6 19.2 %collective-permute-start.53 = (bf16[4,2,32,768]{3,2,1,0:T(8,128)(2,1)S(1)}, bf16[4,2,32,768]{3,2,1,0:T(8,128)(2,1)S(1)}, u32[]{:S(2)}, u32[]{:S(2)}) collective-permute-start(bf16[4,2,32,768]{3,2,1,0:T(8,128)(2,1)S(1)} %get-tuple-element.452), channel_id=1, source_target_pairs={{0,1},{1,0},{2,3},{3,2},{4,5},{5,4},{6,7},{7,6},{8,9},{9,8},{10,11... | collective-permute-start | bytes 1179656 | tf_op jit(solution)/shard_map/ppermute | solution.py:1032
  390.7 21.6 %collective-permute-start.57 = (f32[12,1024]{1,0:T(8,128)S(1)}, f32[12,1024]{1,0:T(8,128)S(1)}, u32[]{:S(2)}, u32[]{:S(2)}) collective-permute-start(f32[12,1024]{1,0:T(8,128)S(1)} %pad_maximum_fusion.14), channel_id=1, source_target_pairs={{0,2},{1,3},{2,0},{3,1},{4,6},{5,7},{6,4},{7,5},{8,10},{9,11},{10,... | collective-permute-start | bytes 147464 | tf_op jit(solution)/shard_map/ppermute | solution.py:1032
  390.8 21.5 %collective-permute-start.58 = (f32[12,1024]{1,0:T(8,128)S(1)}, f32[12,1024]{1,0:T(8,128)S(1)}, u32[]{:S(2)}, u32[]{:S(2)}) collective-permute-start(f32[12,1024]{1,0:T(8,128)S(1)} %pad_maximum_fusion.14), channel_id=1, source_target_pairs={{0,1},{1,0},{2,3},{3,2},{4,5},{5,4},{6,7},{7,6},{8,9},{9,8},{10,11... | collective-permute-start | bytes 147464 | tf_op jit(solution)/shard_map/ppermute | solution.py:1032
  391.7 20.6 %collective-permute-start.59 = (f32[12,1024]{1,0:T(8,128)S(1)}, f32[12,1024]{1,0:T(8,128)S(1)}, u32[]{:S(2)}, u32[]{:S(2)}) collective-permute-start(f32[12,1024]{1,0:T(8,128)S(1)} %pad_maximum_fusion.14), channel_id=1, source_target_pairs={{0,3},{1,2},{2,1},{3,0},{4,7},{5,6},{6,5},{7,4},{8,11},{9,10},{10,... | collective-permute-start | bytes 147464 | tf_op jit(solution)/shard_map/ppermute | solution.py:1032
  392.8 19.6 %collective-permute-start.56 = (bf16[4,32,768]{2,1,0:T(8,128)(2,1)S(1)}, bf16[4,32,768]{2,1,0:T(8,128)(2,1)S(1)}, u32[]{:S(2)}, u32[]{:S(2)}) collective-permute-start(bf16[4,32,768]{2,1,0:T(8,128)(2,1)S(1)} %get-tuple-element.464), channel_id=1, source_target_pairs={{0,1},{1,0},{2,3},{3,2},{4,5},{5,4},{6,7},{7,6},{8,9},{9,8},{10,11... | collective-permute-start | bytes 589832 | tf_op jit(solution)/shard_map/ppermute | solution.py:1032
  393.9 18.5 %collective-permute-start.55 = (bf16[4,32,768]{2,1,0:T(8,128)(2,1)S(1)}, bf16[4,32,768]{2,1,0:T(8,128)(2,1)S(1)}, u32[]{:S(2)}, u32[]{:S(2)}) collective-permute-start(bf16[4,32,768]{2,1,0:T(8,128)(2,1)S(1)} %get-tuple-element.466), channel_id=1, source_target_pairs={{0,4},{1,5},{2,6},{3,7},{4,0},{5,1},{6,2},{7,3},{8,12},{9,13},{10,... | collective-permute-start | bytes 589832 | tf_op jit(solution)/shard_map/ppermute | solution.py:1032
  (125 other events, 863.7 us)
Sparse Core Ops, SparseCore 0:
  36.4 30.7 all-gather.4
  76.6 30.0 all-gather.6
  320.9 29.5 reduce-scatter.5
  353.3 29.3 reduce-scatter.3
  384.9 20.8 reduce-scatter.7
